TPU v7x, 32 devices: a whole 2x2x4 slice. The times are simulated.
32 devices in a mesh: dp: 8 (over y, x, core), tensor: 4 (over z).
Axes of the slice: x: 2, y: 2, z: 4, core: 2. Of those that a mesh axis runs over, the one named last changes fastest.
Arguments:
- teacher_in: bfloat16 [8192, 1600], P(('dp', 'tensor')), may hold values from -6 to 6
- student_in: bfloat16 [8192, 768], P(('dp', 'tensor')), may hold values from -6 to 6
- resp_mask: int32 [8192], P(('dp', 'tensor')), may hold values from 0 to 1, as said below
- replay: int32 [8], P('dp'), may hold values from 0 to 1
- t_gains: float32 [2, 1600], replicated, may hold values from 0.5 to 1.5
- t_shifts: float32 [2, 1600], replicated, may hold values from -1.75 to 1.75
- t_qkv: bfloat16 [1600, 3, 1792], P(None, None, 'tensor'), may hold values from -0.15625 to 0.15625
- t_out: bfloat16 [1792, 1600], P('tensor'), may hold values from -0.4375 to 0.4375
- t_fc: bfloat16 [1600, 6400], P(None, 'tensor'), may hold values from -0.15625 to 0.15625
- t_proj: bfloat16 [6400, 1600], P('tensor'), may hold values from -0.078125 to 0.078125
- s_norms: float32 [4, 768], replicated, may hold values from 0.1 to 1.9
- s_qkv: float32 [768, 3, 768], P(None, None, 'tensor'), may hold values from -0.21875 to 0.21875
- s_out: float32 [768, 768], P('tensor'), may hold values from -0.625 to 0.625
- s_fc: float32 [768, 3072], P(None, 'tensor'), may hold values from -0.21875 to 0.21875
- s_proj: float32 [3072, 768], P('tensor'), may hold values from -0.109375 to 0.109375
- s_map: float32 [768, 1600], replicated, may hold values from -0.21875 to 0.21875
- mom_qkv: float32 [768, 3, 768], P(None, None, 'tensor'), may hold values from -543.058 to 543.058
- mom_out: float32 [768, 768], P('tensor'), may hold values from -543.058 to 543.058
- mom_fc: float32 [768, 3072], P(None, 'tensor'), may hold values from -543.058 to 543.058
- mom_proj: float32 [3072, 768], P('tensor'), may hold values from -271.529 to 271.529
- mom_map: float32 [768, 1600], replicated, may hold values from -1024 to 1024
- adam_first: float32 [4, 768], replicated, may hold values from -112 to 112
- adam_second: float32 [4, 768], replicated, may hold values from 32.768 to 131.072
Outputs:
- teacher_out: bfloat16 [8192, 1600], P(('dp', 'tensor'))
- student_out: bfloat16 [8192, 768], P(('dp', 'tensor'))
- input_grad: float32 [8192, 768], P(('dp', 'tensor'))
- loss: float32 [], replicated
- grad_qkv: float32 [768, 3, 768], P(None, None, 'tensor')
- grad_out: float32 [768, 768], P('tensor')
- grad_fc: float32 [768, 3072], P(None, 'tensor')
- grad_proj: float32 [3072, 768], P('tensor')
- grad_map: float32 [768, 1600], replicated
- moment_qkv: float32 [768, 3, 768], P(None, None, 'tensor')
- moment_out: float32 [768, 768], P('tensor')
- moment_fc: float32 [768, 3072], P(None, 'tensor')
- moment_proj: float32 [3072, 768], P('tensor')
- moment_map: float32 [768, 1600], replicated
- weight_qkv: float32 [768, 3, 768], P(None, None, 'tensor')
- weight_out: float32 [768, 768], P('tensor')
- weight_fc: float32 [768, 3072], P(None, 'tensor')
- weight_proj: float32 [3072, 768], P('tensor')
- weight_map: float32 [768, 1600], replicated
- norm_first: float32 [4, 768], replicated
- norm_second: float32 [4, 768], replicated
- norm_values: float32 [4, 768], replicated
Inputs may be any that keep to these rules, and one draw needn't show every extreme that they name: `resp_mask`: the ones of each sequence form one run that ends at its last position and holds at least one token.
All inputs are finite; a program needn't handle non-finite values.
Results may differ from a plain program's by a relative error of at most 0.006.
The roundings to bfloat16 on the way count: a program that leaves them out, or rounds other values in their place, can miss the bound.
Values may be sent and summed in bfloat16 or wider, within the bound.
A program may use at most 256 MiB of HBM per device.

v0:
```python
import math

import jax
import jax.numpy as jnp
from jax import lax
from jax.sharding import PartitionSpec as P

DT = 1600
HT = 25
DS = 768
FS = 3072
HEAD = 64
LEN = 1024
STEP = 10
QBLK = 512


EPS = 1e-05
NS_A = 3.4445
NS_B = -4.775
NS_C = 2.0315
MOMENTUM = 0.95
MUON_RATE = 0.5
MUON_DECAY = 0.01
ADAM_RATE = 0.3
BETA_ONE = 0.9
BETA_TWO = 0.999
ADAM_EPS = 1e-08
ADAM_DECAY = 0.01
REPLAY_CUT = 0.5
NEG_FILL = -1e30
HIGH = lax.Precision.HIGHEST


def norm_parts(v, gain_vec, shift_vec):
    row_mean = jnp.mean(v, axis=-1, keepdims=True)
    centred = v - row_mean
    row_var = jnp.mean(centred * centred, axis=-1, keepdims=True)
    inv_scale = lax.rsqrt(row_var + EPS)
    unit_val = centred * inv_scale
    return (unit_val * gain_vec + shift_vec, unit_val, inv_scale)


def norm_back(grad_norm, unit_val, inv_scale, gain_vec):
    grad_unit = grad_norm * gain_vec
    first_mean = jnp.mean(grad_unit, axis=-1, keepdims=True)
    second_mean = jnp.mean(grad_unit * unit_val, axis=-1, keepdims=True)
    return inv_scale * (grad_unit - first_mean - unit_val * second_mean)


def smooth_gelu(v):
    return 0.5 * v * (1.0 + jnp.tanh(0.7978845608028654 * (v + 0.044715 * v * v * v)))


def masked_scores(query_block, keys, row_start):
    scores = jnp.einsum(
        "qhe,khe->hqk", query_block, keys, preferred_element_type=jnp.float32
    ) * HEAD ** (-0.5)
    row_pos = row_start + jnp.arange(query_block.shape[0], dtype=jnp.int32)
    key_pos = jnp.arange(keys.shape[0], dtype=jnp.int32)
    return jnp.where(key_pos[None, None, :] <= row_pos[None, :, None], scores, NEG_FILL)


def attend_forward(query, keys, values):
    head_count = query.shape[1]
    blocks = LEN // QBLK

    def one_block(block_args):
        query_block, row_start = block_args
        scores = masked_scores(query_block, keys, row_start)
        row_top = jnp.max(scores, axis=-1, keepdims=True)
        exp_vals = jnp.exp(scores - row_top)
        row_total = jnp.sum(exp_vals, axis=-1, keepdims=True)
        prob_vals = (exp_vals / row_total).astype(jnp.bfloat16)
        out_block = jnp.einsum(
            "hqk,khe->qhe", prob_vals, values, preferred_element_type=jnp.float32
        )
        return (out_block, (row_top + jnp.log(row_total))[..., 0])

    starts = jnp.arange(blocks, dtype=jnp.int32) * QBLK
    out_blocks, log_sums = lax.map(
        one_block, (query.reshape(blocks, QBLK, head_count, HEAD), starts)
    )
    return (out_blocks.reshape(LEN, head_count, HEAD), log_sums)


def attend_backward(query, keys, values, log_sums, grad_heads):
    head_count = query.shape[1]
    blocks = LEN // QBLK
    head_scale = HEAD ** (-0.5)

    def one_block(carry, block_args):
        grad_keys, grad_values = carry
        query_block, grad_block, log_block, row_start = block_args
        scores = masked_scores(query_block, keys, row_start)
        prob_vals = jnp.exp(scores - log_block[..., None])
        grad_probs = jnp.einsum(
            "qhe,khe->hqk", grad_block, values, preferred_element_type=jnp.float32
        )
        row_inner = jnp.sum(prob_vals * grad_probs, axis=-1, keepdims=True)
        grad_scores = (prob_vals * (grad_probs - row_inner)).astype(jnp.bfloat16)
        grad_query = (
            jnp.einsum("hqk,khe->qhe", grad_scores, keys, preferred_element_type=jnp.float32)
            * head_scale
        )
        grad_keys = (
            grad_keys
            + jnp.einsum(
                "hqk,qhe->khe", grad_scores, query_block, preferred_element_type=jnp.float32
            )
            * head_scale
        )
        grad_values = grad_values + jnp.einsum(
            "hqk,qhe->khe",
            prob_vals.astype(jnp.bfloat16),
            grad_block,
            preferred_element_type=jnp.float32,
        )
        return ((grad_keys, grad_values), grad_query)

    zero_acc = jnp.zeros((LEN, head_count, HEAD), jnp.float32)
    starts = jnp.arange(blocks, dtype=jnp.int32) * QBLK
    shaped = (
        query.reshape(blocks, QBLK, head_count, HEAD),
        grad_heads.reshape(blocks, QBLK, head_count, HEAD),
        log_sums,
        starts,
    )
    (grad_keys, grad_values), grad_query = lax.scan(one_block, (zero_acc, zero_acc), shaped)
    return (grad_query.reshape(LEN, head_count, HEAD), grad_keys, grad_values)


def gram_of(iterate, flipped):
    axis_num = 0 if flipped else 1
    return lax.dot_general(
        iterate,
        iterate,
        (((axis_num,), (axis_num,)), ((), ())),
        precision=HIGH,
        preferred_element_type=jnp.float32,
    )


def apply_poly(iterate, poly_mat, flipped):
    if flipped:
        return lax.dot_general(
            iterate,
            poly_mat,
            (((1,), (1,)), ((), ())),
            precision=HIGH,
            preferred_element_type=jnp.float32,
        )
    return jnp.dot(poly_mat, iterate, precision=HIGH, preferred_element_type=jnp.float32)


def poly_of(gram_sum):
    square = jnp.dot(gram_sum, gram_sum, precision=HIGH, preferred_element_type=jnp.float32)
    return NS_B * gram_sum + NS_C * square


def contract_rows(left, right):
    return lax.dot_general(
        left, right, (((0,), (0,)), ((), ())), preferred_element_type=jnp.float32
    )


def contract_cols(left, right):
    return lax.dot_general(
        left, right, (((1,), (1,)), ((), ())), preferred_element_type=jnp.float32
    )


def body(
    teacher_in,
    student_in,
    resp_mask,
    replay,
    t_gains,
    t_shifts,
    t_qkv,
    t_out,
    t_fc,
    t_proj,
    s_norms,
    s_qkv,
    s_out,
    s_fc,
    s_proj,
    s_map,
    mom_qkv,
    mom_out,
    mom_fc,
    mom_proj,
    mom_map,
    adam_first,
    adam_second,
):
    groups = lax.axis_size("tensor")
    tensor_rank = lax.axis_index("tensor")
    row_count = student_in.shape[0]
    seq_count = replay.shape[0]
    total_rows = row_count * groups
    count = lax.psum(jnp.sum(resp_mask), ("dp", "tensor"))
    count_val = count.astype(jnp.float32)
    tokens_all = lax.axis_size("dp") * seq_count * LEN
    factor = tokens_all / (2.0 * count_val)

    def teacher_gather(local_rows):
        return lax.all_gather(local_rows, "tensor", axis=0, tiled=True)

    def teacher_reduce(left, right):
        return lax.psum_scatter(
            jnp.dot(left, right, preferred_element_type=jnp.float32),
            "tensor",
            scatter_dimension=0,
            tiled=True,
        )

    def student_gather(local_rows):
        return lax.all_gather(local_rows, "tensor", axis=0, tiled=True)

    def student_reduce(left, right, right_dim):
        return lax.psum_scatter(
            lax.dot_general(
                left, right, (((1,), (right_dim,)), ((), ())), preferred_element_type=jnp.float32
            ),
            "tensor",
            scatter_dimension=0,
            tiled=True,
        )

    teacher_x = teacher_in.astype(jnp.float32)
    slot_width = t_qkv.shape[2]
    slot_count = slot_width // HEAD
    live_count = HT // groups + (tensor_rank < HT % groups).astype(jnp.int32)
    live_slots = (jnp.arange(slot_count, dtype=jnp.int32) < live_count).astype(jnp.float32)
    teacher_normed = norm_parts(teacher_x, t_gains[0], t_shifts[0])[0].astype(jnp.bfloat16)
    teacher_all = teacher_gather(teacher_normed)
    teacher_mixed = jnp.dot(
        teacher_all, t_qkv.reshape(DT, 3 * slot_width), preferred_element_type=jnp.float32
    ).astype(jnp.bfloat16)
    teacher_mixed = teacher_mixed.reshape(seq_count, LEN, 3, slot_count, HEAD)

    def teacher_heads(mixed_qkv):
        out_vals, log_sums = attend_forward(mixed_qkv[:, 0], mixed_qkv[:, 1], mixed_qkv[:, 2])
        return (out_vals * live_slots[None, :, None]).astype(jnp.bfloat16)

    teacher_head_out = lax.map(teacher_heads, teacher_mixed).reshape(total_rows, slot_width)
    teacher_resid = teacher_x + teacher_reduce(teacher_head_out, t_out)
    teacher_normed_two = norm_parts(teacher_resid, t_gains[1], t_shifts[1])[0].astype(jnp.bfloat16)
    teacher_hidden = smooth_gelu(
        jnp.dot(teacher_gather(teacher_normed_two), t_fc, preferred_element_type=jnp.float32)
    ).astype(jnp.bfloat16)
    teacher_out = (teacher_resid + teacher_reduce(teacher_hidden, t_proj)).astype(jnp.bfloat16)
    student_x = student_in.astype(jnp.float32)
    shard_width = s_qkv.shape[2]
    head_count = shard_width // HEAD
    w_qkv = s_qkv.astype(jnp.bfloat16).reshape(DS, 3 * shard_width)
    w_out = s_out.astype(jnp.bfloat16)
    w_fc = s_fc.astype(jnp.bfloat16)
    w_proj = s_proj.astype(jnp.bfloat16)
    w_map = s_map.astype(jnp.bfloat16)
    normed_one, unit_one, scale_one = norm_parts(student_x, s_norms[0], s_norms[1])
    low_one = normed_one.astype(jnp.bfloat16)
    rows_one = student_gather(low_one)
    mixed_qkv = jnp.dot(rows_one, w_qkv, preferred_element_type=jnp.float32).astype(jnp.bfloat16)
    mixed_qkv = mixed_qkv.reshape(seq_count, LEN, 3, head_count, HEAD)
    out_vals, log_sums = lax.map(
        lambda seq_qkv: attend_forward(seq_qkv[:, 0], seq_qkv[:, 1], seq_qkv[:, 2]), mixed_qkv
    )
    mixed_qkv, head_out, log_sums = (
        mixed_qkv,
        out_vals.astype(jnp.bfloat16).reshape(total_rows, shard_width),
        log_sums,
    )
    resid = student_x + student_reduce(head_out, w_out, 0)
    normed_two, unit_two, scale_two = norm_parts(resid, s_norms[2], s_norms[3])
    low_two = normed_two.astype(jnp.bfloat16)
    rows_two = student_gather(low_two)
    before = jnp.dot(rows_two, w_fc, preferred_element_type=jnp.float32)
    before, hidden = (before, smooth_gelu(before).astype(jnp.bfloat16))
    output = resid + student_reduce(hidden, w_proj, 0)
    student_out = output.astype(jnp.bfloat16)
    guess_vec = jnp.dot(student_out, w_map, preferred_element_type=jnp.float32)
    miss_vec = guess_vec - teacher_out.astype(jnp.float32)
    position = tensor_rank * row_count + jnp.arange(row_count, dtype=jnp.int32)
    seq_owner = position // LEN
    seq_pick = (seq_owner[:, None] == jnp.arange(seq_count, dtype=jnp.int32)[None, :]).astype(
        jnp.float32
    )
    flag_tok = jnp.sum(seq_pick * replay.astype(jnp.float32)[None, :], axis=1)
    weight = resp_mask.astype(jnp.float32) * (1.0 - REPLAY_CUT * flag_tok)
    loss_part = jnp.sum(weight[:, None] * miss_vec * miss_vec)
    grad_guess = (2.0 * factor * weight[:, None] * miss_vec).astype(jnp.bfloat16)
    grad_map = contract_rows(student_out, grad_guess)
    grad_output = contract_cols(grad_guess, w_map)
    rows_two_back, before_back, hidden_back = (rows_two, before, hidden)
    rows_one_back, mixed_back, heads_back, logs_back = (rows_one, mixed_qkv, head_out, log_sums)
    grad_mlp = student_gather(grad_output.astype(jnp.bfloat16))
    grad_proj = contract_rows(hidden_back, grad_mlp)
    grad_hidden = contract_cols(grad_mlp, w_proj)
    gelu_vals, gelu_pull = jax.vjp(smooth_gelu, before_back)
    grad_before = gelu_pull(grad_hidden)[0].astype(jnp.bfloat16)
    grad_fc = contract_rows(rows_two_back, grad_before)
    grad_normed_two = student_reduce(grad_before, w_fc, 1)
    grad_resid = grad_output + norm_back(grad_normed_two, unit_two, scale_two, s_norms[2])
    grad_attn = student_gather(grad_resid.astype(jnp.bfloat16))
    grad_out = contract_rows(heads_back, grad_attn)
    grad_heads = contract_cols(grad_attn, w_out).astype(jnp.bfloat16)

    def head_back(seq_args):
        seq_qkv, seq_logs, seq_grad = seq_args
        grad_query, grad_keys, grad_values = attend_backward(
            seq_qkv[:, 0], seq_qkv[:, 1], seq_qkv[:, 2], seq_logs, seq_grad
        )
        return jnp.stack([grad_query, grad_keys, grad_values], axis=1).astype(jnp.bfloat16)

    grad_mixed = lax.map(
        head_back, (mixed_back, logs_back, grad_heads.reshape(seq_count, LEN, head_count, HEAD))
    )
    grad_mixed = grad_mixed.reshape(total_rows, 3 * shard_width)
    grad_qkv = contract_rows(rows_one_back, grad_mixed).reshape(DS, 3, shard_width)
    grad_normed_one = student_reduce(grad_mixed, w_qkv, 1)
    input_grad = grad_resid + norm_back(grad_normed_one, unit_one, scale_one, s_norms[0])
    norm_grads = jnp.stack(
        [
            jnp.sum(grad_normed_one * unit_one, axis=0),
            jnp.sum(grad_normed_one, axis=0),
            jnp.sum(grad_normed_two * unit_two, axis=0),
            jnp.sum(grad_normed_two, axis=0),
        ]
    )
    grad_qkv, grad_out, grad_fc, grad_proj = lax.psum(
        (grad_qkv, grad_out, grad_fc, grad_proj), "dp"
    )
    grad_map, norm_grads, loss_sum = lax.psum((grad_map, norm_grads, loss_part), ("dp", "tensor"))
    loss = loss_sum / (count_val * DT)
    moments = [
        MOMENTUM * mom_qkv.reshape(DS, -1) + grad_qkv.reshape(DS, -1),
        MOMENTUM * mom_out + grad_out,
        MOMENTUM * mom_fc + grad_fc,
        MOMENTUM * mom_proj + grad_proj,
    ]
    moment_map = MOMENTUM * mom_map + grad_map
    flips = [False, True, False, True]
    squares = lax.psum(
        (
            jnp.sum(moments[0] * moments[0]),
            jnp.sum(moments[1] * moments[1]),
            jnp.sum(moments[2] * moments[2]),
            jnp.sum(moments[3] * moments[3]),
        ),
        "tensor",
    )
    iterates = [
        moment / (jnp.sqrt(square_sum) + 1e-07) for moment, square_sum in zip(moments, squares)
    ]
    map_iterate = moment_map / (jnp.sqrt(jnp.sum(moment_map * moment_map)) + 1e-07)
    for sweep_index in range(5):
        grams = (
            lax.psum(gram_of(iterates[0], False).astype(jnp.bfloat16), "tensor").astype(
                jnp.float32
            ),
            lax.psum(gram_of(iterates[1], True).astype(jnp.bfloat16), "tensor").astype(jnp.float32),
            lax.psum(gram_of(iterates[2], False).astype(jnp.bfloat16), "tensor").astype(
                jnp.float32
            ),
            lax.psum(gram_of(iterates[3], True).astype(jnp.bfloat16), "tensor").astype(jnp.float32),
        )
        renewed = []
        for iterate, gram_sum, flipped in zip(iterates, grams, flips):
            poly_mat = poly_of(gram_sum)
            renewed.append(NS_A * iterate + apply_poly(iterate, poly_mat, flipped))
        iterates = renewed
    for sweep_index in range(5):
        poly_mat = poly_of(gram_of(map_iterate, False))
        map_iterate = NS_A * map_iterate + apply_poly(map_iterate, poly_mat, False)
    keep_rate = 1.0 - MUON_RATE * MUON_DECAY
    weight_qkv = keep_rate * s_qkv - MUON_RATE * math.sqrt(3.0) * iterates[0].reshape(
        DS, 3, shard_width
    )
    weight_out = keep_rate * s_out - MUON_RATE * iterates[1]
    weight_fc = keep_rate * s_fc - MUON_RATE * math.sqrt(FS / DS) * iterates[2]
    weight_proj = keep_rate * s_proj - MUON_RATE * iterates[3]
    weight_map = keep_rate * s_map - MUON_RATE * math.sqrt(DT / DS) * map_iterate
    norm_first = BETA_ONE * adam_first + (1.0 - BETA_ONE) * norm_grads
    norm_second = BETA_TWO * adam_second + (1.0 - BETA_TWO) * norm_grads * norm_grads
    fix_one = 1.0 - BETA_ONE**STEP
    fix_two = 1.0 - BETA_TWO**STEP
    norm_values = s_norms - ADAM_RATE * (
        norm_first / fix_one / (jnp.sqrt(norm_second / fix_two) + ADAM_EPS) + ADAM_DECAY * s_norms
    )
    return (
        teacher_out,
        student_out,
        input_grad,
        loss,
        grad_qkv,
        grad_out,
        grad_fc,
        grad_proj,
        grad_map,
        moments[0].reshape(DS, 3, shard_width),
        moments[1],
        moments[2],
        moments[3],
        moment_map,
        weight_qkv,
        weight_out,
        weight_fc,
        weight_proj,
        weight_map,
        norm_first,
        norm_second,
        norm_values,
    )


def solution(mesh):
    return jax.shard_map(
        body,
        mesh=mesh,
        in_specs=(
            P(("dp", "tensor"), None),
            P(("dp", "tensor"), None),
            P(("dp", "tensor")),
            P("dp"),
            P(),
            P(),
            P(None, None, "tensor"),
            P("tensor", None),
            P(None, "tensor"),
            P("tensor", None),
            P(),
            P(None, None, "tensor"),
            P("tensor", None),
            P(None, "tensor"),
            P("tensor", None),
            P(),
            P(None, None, "tensor"),
            P("tensor", None),
            P(None, "tensor"),
            P("tensor", None),
            P(),
            P(),
            P(),
        ),
        out_specs=(
            P(("dp", "tensor"), None),
            P(("dp", "tensor"), None),
            P(("dp", "tensor"), None),
            P(),
            P(None, None, "tensor"),
            P("tensor", None),
            P(None, "tensor"),
            P("tensor", None),
            P(),
            P(None, None, "tensor"),
            P("tensor", None),
            P(None, "tensor"),
            P("tensor", None),
            P(),
            P(None, None, "tensor"),
            P("tensor", None),
            P(None, "tensor"),
            P("tensor", None),
            P(),
            P(),
            P(),
            P(),
        ),
        check_vma=False,
    )
```

profile of v0, /device:TPU:0, one launch (start us, length us, event | category | flops | bytes accessed | tf_op | source)
XLA Modules:
  0.0 2226.6 jit_solution(16885722425678028619)
XLA Ops:
  18.9 34.8 %all-gather.11.cloned.1.call-done = bf16[1024,768]{1,0:T(8,128)(2,1)} async-done(((bf16[256,768]{1,0:T(8,128)(2,1)}), bf16[1024,768]{1,0:T(8,128)(2,1)}) %all-gather.11.cloned.1.call-update) | async-done | bytes 1572880 | tf_op jit(solution)/shard_map/all_gather | solution.py:220
  58.2 19.1 while.63
  81.1 39.3 %all-gather.7.cloned.1.call-done = bf16[1024,1600]{0,1:T(8,128)(2,1)} async-done(((bf16[256,1600]{0,1:T(8,128)(2,1)}), bf16[1024,1600]{0,1:T(8,128)(2,1)}) %all-gather.7.cloned.1.call-update) | async-done | bytes 3276816 | tf_op jit(solution)/shard_map/all_gather | solution.py:209
  131.6 67.9 %while.62 = (s32[]{:T(128)}, f32[2,512,7,64]{1,0,3,2:T(2,128)}, s32[2]{0:T(128)S(1)}, bf16[2,512,7,64]{1,3,2,0:T(8,128)(2,1)}, bf16[1024,7,64]{0,2,1:T(8,128)(2,...) while((s32[]{:T(128)}, f32[2,512,7,64]{1,0,3,2:T(2,128)}, s32[2]{0:T(128)S(1)}, ...), condition=%wide.region_5.6_spmd, body=%wide.region_2.5_spmd.sunk | while | flops 1442846720 | bytes 9863289 | solution.py:81
  148.3 17.3 dynamic_update_slice.34
  182.0 17.3 dynamic_update_slice.34
  209.6 109.8 %reduce-scatter.7.cloned.1.call-done = f32[256,1600]{0,1:T(8,128)} async-done(((f32[1024,1600]{0,1:T(8,128)}), f32[256,1600]{0,1:T(8,128)}) %reduce-scatter.7.cloned.1.call-update) | async-done | bytes 1638416 | tf_op jit(solution)/shard_map/reduce_scatter | solution.py:212
  323.2 35.9 %all-gather.13.cloned.1.call-done = bf16[1024,768]{1,0:T(8,128)(2,1)} async-done(((bf16[256,768]{1,0:T(8,128)(2,1)}), bf16[1024,768]{1,0:T(8,128)(2,1)}) %all-gather.13.cloned.1.call-update) | async-done | bytes 1572880 | tf_op jit(solution)/shard_map/all_gather | solution.py:220
  368.4 57.1 %all-gather.9.cloned.1.call-done = bf16[1024,1600]{0,1:T(8,128)(2,1)} async-done(((bf16[256,1600]{0,1:T(8,128)(2,1)}), bf16[1024,1600]{0,1:T(8,128)(2,1)}) %all-gather.9.cloned.1.call-update) | async-done | bytes 3276816 | tf_op jit(solution)/shard_map/all_gather | solution.py:209
  425.5 20.7 fusion.83
  447.5 44.0 %psum.224 = s32[]{:T(128)} all-reduce(s32[]{:T(128)} %reduce_sum.246), channel_id=1, replica_groups=mesh['dp'=8,'tensor'=4] {'dp','tensor'}, use_global_device_ids=true, to_apply=%region_21.22 | all-reduce | flops 1 | bytes 8 | tf_op jit(solution)/shard_map/psum | solution.py:203
  494.9 110.3 %reduce-scatter.9.cloned.1.call-done = f32[256,1600]{0,1:T(8,128)} async-done(((f32[1024,1600]{0,1:T(8,128)}), f32[256,1600]{0,1:T(8,128)}) %reduce-scatter.9.cloned.1.call-update) | async-done | bytes 1638416 | tf_op jit(solution)/shard_map/reduce_scatter | solution.py:212
  613.1 37.7 %all-gather.15.cloned.1.call-done = bf16[1024,768]{1,0:T(8,128)(2,1)} async-done(((bf16[256,768]{1,0:T(8,128)(2,1)}), bf16[1024,768]{1,0:T(8,128)(2,1)}) %all-gather.15.cloned.1.call-update) | async-done | bytes 1572880 | tf_op jit(solution)/shard_map/all_gather | solution.py:220
  660.6 59.2 %reduce-scatter.15.cloned.1.call-done = f32[256,768]{1,0:T(8,128)} async-done(((f32[1024,768]{1,0:T(8,128)}), f32[256,768]{1,0:T(8,128)}) %reduce-scatter.15.cloned.1.call-update) | async-done | bytes 786448 | tf_op jit(solution)/shard_map/reduce_scatter | solution.py:223
  732.3 29.5 %all-gather.17.cloned.1.call-done = bf16[1024,768]{1,0:T(8,128)(2,1)} async-done(((bf16[256,768]{1,0:T(8,128)(2,1)}), bf16[1024,768]{1,0:T(8,128)(2,1)}) %all-gather.17.cloned.1.call-update) | async-done | bytes 1572880 | tf_op jit(solution)/shard_map/all_gather | solution.py:220
  764.9 53.5 %while.64 = (s32[]{:T(128)}, f32[1024,3,64]{0,2,1:T(8,128)}, f32[1024,3,64]{0,2,1:T(8,128)}, bf16[2,512,3,64]{1,0,3,2:T(2,128)(2,1)}, bf16[2,512,3,64]{1,3,2,0:T...) while((s32[]{:T(128)}, f32[1024,3,64]{0,2,1:T(8,128)}, ...), condition=%wide.region_27.28_spmd.clone, body=%wide.region_25.27_spmd.clone.sunk | while | flops 1031928832 | bytes 107854088 | solution.py:129
  825.3 112.4 %all-reduce.18.cloned.1.call-done = (f32[768,3,192]{0,2,1:T(8,128)}, f32[192,768]{1,0:T(8,128)}, f32[768,768]{1,0:T(8,128)}, f32[768,768]{1,0:T(8,128)}) async-done(((f32[768,3,192]{0,2,1:T(8,128)}, f32[192,768]{1,0:T(8,128)}, f32[768,768]{1,0:T(8,128)}, f32[768,768]{1,0:T(8,128)}), (f32[768,3,192]{0,2,1:T(8,128)}, f32[192,768]{1,0:T(8,128)}, f32[768,768]{1,0:T(8,128)}, ...) | async-done | bytes 7077904 | tf_op jit(solution)/shard_map/psum | solution.py:333
  989.2 170.2 %all-reduce.28.cloned.1.call-done = (bf16[768,768]{1,0:T(8,128)(2,1)}, bf16[768,768]{1,0:T(8,128)(2,1)}, bf16[768,768]{1,0:T(8,128)(2,1)}, bf16[768,768]{1,0:T(8,128)(2,1)}) async-done(((bf16[768,768]{1,0:T(8,128)(2,1)}, bf16[768,768]{1,0:T(8,128)(2,1)}, bf16[768,768]{1,0:T(8,128)(2,1)}, bf16[768,768]{1,0:T(8,128)(2,1)}), (bf16[768,768]{1,0:T(8,128)(2,1)}, bf16[768,768]{1,0:T(8,128)(2,1)}, ...) | async-done | bytes 4718608 | tf_op jit(solution)/shard_map/psum | solution.py:361
  1213.4 172.0 %all-reduce.26.cloned.1.call-done = (bf16[768,768]{1,0:T(8,128)(2,1)}, bf16[768,768]{1,0:T(8,128)(2,1)}, bf16[768,768]{1,0:T(8,128)(2,1)}, bf16[768,768]{1,0:T(8,128)(2,1)}) async-done(((bf16[768,768]{1,0:T(8,128)(2,1)}, bf16[768,768]{1,0:T(8,128)(2,1)}, bf16[768,768]{1,0:T(8,128)(2,1)}, bf16[768,768]{1,0:T(8,128)(2,1)}), (bf16[768,768]{1,0:T(8,128)(2,1)}, bf16[768,768]{1,0:T(8,128)(2,1)}, ...) | async-done | bytes 4718608 | tf_op jit(solution)/shard_map/psum | solution.py:361
  1445.3 166.3 %all-reduce.24.cloned.1.call-done = (bf16[768,768]{1,0:T(8,128)(2,1)}, bf16[768,768]{1,0:T(8,128)(2,1)}, bf16[768,768]{1,0:T(8,128)(2,1)}, bf16[768,768]{1,0:T(8,128)(2,1)}) async-done(((bf16[768,768]{1,0:T(8,128)(2,1)}, bf16[768,768]{1,0:T(8,128)(2,1)}, bf16[768,768]{1,0:T(8,128)(2,1)}, bf16[768,768]{1,0:T(8,128)(2,1)}), (bf16[768,768]{1,0:T(8,128)(2,1)}, bf16[768,768]{1,0:T(8,128)(2,1)}, ...) | async-done | bytes 4718608 | tf_op jit(solution)/shard_map/psum | solution.py:361
  1665.3 96.9 %all-reduce.16.cloned.1.call-done = f32[768,1600]{0,1:T(8,128)} async-done(((f32[768,1600]{0,1:T(8,128)}), f32[768,1600]{0,1:T(8,128)}) %all-reduce.16.cloned.1.call-update) | async-done | bytes 4915216 | tf_op jit(solution)/shard_map/psum | solution.py:336
  1770.9 17.7 fusion.210
  1808.3 15.1 fusion.447
  1834.3 16.8 multiply_add_fusion.3
  1851.1 15.3 fusion.449
  1886.7 50.8 %all-reduce.22.cloned.1.call-done = (bf16[768,768]{1,0:T(8,128)(2,1)}, bf16[768,768]{1,0:T(8,128)(2,1)}, bf16[768,768]{1,0:T(8,128)(2,1)}, bf16[768,768]{1,0:T(8,128)(2,1)}) async-done(((bf16[768,768]{1,0:T(8,128)(2,1)}, bf16[768,768]{1,0:T(8,128)(2,1)}, bf16[768,768]{1,0:T(8,128)(2,1)}, bf16[768,768]{1,0:T(8,128)(2,1)}), (bf16[768,768]{1,0:T(8,128)(2,1)}, bf16[768,768]{1,0:T(8,128)(2,1)}, ...) | async-done | bytes 4718608 | tf_op jit(solution)/shard_map/psum | solution.py:361
  1989.0 17.2 fusion.451
  2012.2 16.9 multiply_add_fusion.1
  2029.2 15.1 fusion.453
  2050.4 14.6 multiply_subtract_fusion
  2066.7 42.1 %all-reduce = (f32[]{:T(128)}, f32[4,768]{1,0:T(4,128)S(1)}) all-reduce(f32[]{:T(128)} %get-tuple-element.380, f32[4,768]{1,0:T(4,128)S(1)} %pad_maximum_fusion), channel_id=1, replica_groups=mesh['dp'=8,'tensor'=4] {'dp','tensor'}, use_global_device_ids=true, to_apply=%region_32.33 | all-reduce | flops 3073 | bytes 24584 | tf_op jit(solution)/shard_map/psum | solution.py:336
  2112.6 64.0 %all-reduce.20.cloned.1.call-done = (bf16[768,768]{1,0:T(8,128)(2,1)}, bf16[768,768]{1,0:T(8,128)(2,1)}, bf16[768,768]{1,0:T(8,128)(2,1)}, bf16[768,768]{1,0:T(8,128)(2,1)}) async-done(((bf16[768,768]{1,0:T(8,128)(2,1)}, bf16[768,768]{1,0:T(8,128)(2,1)}, bf16[768,768]{1,0:T(8,128)(2,1)}, bf16[768,768]{1,0:T(8,128)(2,1)}), (bf16[768,768]{1,0:T(8,128)(2,1)}, bf16[768,768]{1,0:T(8,128)(2,1)}, ...) | async-done | bytes 4718608 | tf_op jit(solution)/shard_map/psum | solution.py:361
  (503 shorter events, 586.9 us)
Async XLA Ops:
  7.2 194.1 %copy-start = (bf16[448,1600]{1,0:T(8,128)(2,1)S(1)}, bf16[448,1600]{1,0:T(8,128)(2,1)}, u32[]{:S(2)}) copy-start(bf16[448,1600]{1,0:T(8,128)(2,1)} %param.36) | copy-start | bytes 4300804
  7.2 46.5 %all-gather.11.cloned.1.call-start = ((), (), s32[]{:S(2)}) async-start(), calls=%async_computation.10 | async-start | bytes 1966080 | tf_op jit(solution)/shard_map/all_gather | solution.py:220
  13.8 106.6 %all-gather.7.cloned.1.call-start = ((), (), s32[]{:S(2)}) async-start(), calls=%async_computation.6 | async-start | bytes 4096000 | tf_op jit(solution)/shard_map/all_gather | solution.py:209
  17.3 188.9 %reduce-scatter.11.cloned.1.call-start = ((), (), s32[]{:S(2)}) async-start(), calls=%async_computation.11 | async-start | bytes 3932160 | tf_op jit(solution)/shard_map/reduce_scatter | solution.py:223
  18.9 37.4 %copy-start.83 = (bf16[768,3,192]{0,2,1:T(8,128)(2,1)}, bf16[768,3,192]{0,2,1:T(8,128)(2,1)S(1)}, u32[]{:S(2)}) copy-start(bf16[768,3,192]{0,2,1:T(8,128)(2,1)S(1)} %convert_element_type.261) | copy-start | bytes 2654212
  80.9 238.5 %reduce-scatter.7.cloned.1.call-start = ((), (), s32[]{:S(2)}) async-start(), calls=%async_computation.7 | async-start | bytes 8192000 | tf_op jit(solution)/shard_map/reduce_scatter | solution.py:212
  206.1 113.4 %copy-start.8 = (bf16[256,1600]{0,1:T(8,128)(2,1)S(1)}, bf16[256,1600]{0,1:T(8,128)(2,1)}, u32[]{:S(2)}) copy-start(bf16[256,1600]{0,1:T(8,128)(2,1)} %param.29) | copy-start | bytes 2457604
  206.1 153.0 %all-gather.13.cloned.1.call-start = ((), (), s32[]{:S(2)}) async-start(), calls=%async_computation.12 | async-start | bytes 1966080 | tf_op jit(solution)/shard_map/all_gather | solution.py:220
  209.5 112.2 %copy-start.91 = (f32[1600]{0:T(1024)S(1)}, f32[1600]{0:T(1024)}, u32[]{:S(2)}) copy-start(f32[1600]{0:T(1024)} %get-tuple-element.268) | copy-start | bytes 19204
  209.5 112.2 %copy-start.92 = (f32[1600]{0:T(1024)S(1)}, f32[1600]{0:T(1024)}, u32[]{:S(2)}) copy-start(f32[1600]{0:T(1024)} %get-tuple-element.382) | copy-start | bytes 19204
  209.6 215.9 %all-gather.9.cloned.1.call-start = ((), (), s32[]{:S(2)}) async-start(), calls=%async_computation.8 | async-start | bytes 4096000 | tf_op jit(solution)/shard_map/all_gather | solution.py:209
  323.1 169.8 %reduce-scatter.13.cloned.1.call-start = ((), (), s32[]{:S(2)}) async-start(), calls=%async_computation.13 | async-start | bytes 3932160 | tf_op jit(solution)/shard_map/reduce_scatter | solution.py:223
  368.1 237.1 %reduce-scatter.9.cloned.1.call-start = ((), (), s32[]{:S(2)}) async-start(), calls=%async_computation.9 | async-start | bytes 8192000 | tf_op jit(solution)/shard_map/reduce_scatter | solution.py:212
  446.2 204.6 %all-gather.15.cloned.1.call-start = ((), (), s32[]{:S(2)}) async-start(), calls=%async_computation.14 | async-start | bytes 1966080 | tf_op jit(solution)/shard_map/all_gather | solution.py:220
  492.9 118.4 %copy-start.95 = (f32[256]{0:T(256)}, f32[256]{0:T(256)S(1)}, u32[]{:S(2)}) copy-start(f32[256]{0:T(256)S(1)} %get-tuple-element.364) | copy-start | bytes 3076
  613.0 106.8 %reduce-scatter.15.cloned.1.call-start = ((), (), s32[]{:S(2)}) async-start(), calls=%async_computation.15 | async-start | bytes 3932160 | tf_op jit(solution)/shard_map/reduce_scatter | solution.py:223
  660.5 101.3 %all-gather.17.cloned.1.call-start = ((), (), s32[]{:S(2)}) async-start(), calls=%async_computation.16 | async-start | bytes 1966080 | tf_op jit(solution)/shard_map/all_gather | solution.py:220
  724.5 213.2 %all-reduce.18.cloned.1.call-start = ((), (), s32[]{:S(2)}) async-start(), calls=%async_computation.19 | async-start | bytes 14155776 | tf_op jit(solution)/shard_map/psum | solution.py:333
  729.0 32.8 %copy-start.44 = (f32[192,768]{1,0:T(8,128)S(1)}, f32[192,768]{1,0:T(8,128)}, u32[]{:S(2)}) copy-start(f32[192,768]{1,0:T(8,128)} %param.41) | copy-start | bytes 1769476
  732.3 32.6 %copy-start.6 = (bf16[1024,3,64]{0,2,1:T(8,128)(2,1)S(1)}, bf16[1024,3,64]{0,2,1:T(8,128)(2,1)}, u32[]{:S(2)}) copy-start(bf16[1024,3,64]{0,2,1:T(8,128)(2,1)} %copy-done.5) | copy-start | bytes 1179652
  825.2 112.5 %copy-start.63 = (f32[768,3,192]{0,2,1:T(8,128)S(1)}, f32[768,3,192]{0,2,1:T(8,128)}, u32[]{:S(2)}) copy-start(f32[768,3,192]{0,2,1:T(8,128)} %param.45) | copy-start | bytes 5308420
  825.3 334.1 %all-reduce.28.cloned.1.call-start = ((), (), s32[]{:S(2)}) async-start(), calls=%async_computation.24 | async-start | bytes 9437184 | tf_op jit(solution)/shard_map/psum | solution.py:361
  988.9 396.6 %all-reduce.26.cloned.1.call-start = ((), (), s32[]{:S(2)}) async-start(), calls=%async_computation.23 | async-start | bytes 9437184 | tf_op jit(solution)/shard_map/psum | solution.py:361
  1213.4 398.1 %all-reduce.24.cloned.1.call-start = ((), (), s32[]{:S(2)}) async-start(), calls=%async_computation.22 | async-start | bytes 9437184 | tf_op jit(solution)/shard_map/psum | solution.py:361
  1439.5 322.8 %all-reduce.16.cloned.1.call-start = ((), (), s32[]{:S(2)}) async-start(), calls=%async_computation.18 | async-start | bytes 9830400 | tf_op jit(solution)/shard_map/psum | solution.py:336
  1445.2 492.3 %all-reduce.22.cloned.1.call-start = ((), (), s32[]{:S(2)}) async-start(), calls=%async_computation.21 | async-start | bytes 9437184 | tf_op jit(solution)/shard_map/psum | solution.py:361
  1665.3 399.7 %reduce-scatter.17.cloned.1.call-start = ((), (), s32[]{:S(2)}) async-start(), calls=%async_computation.17 | async-start | bytes 3932160 | tf_op jit(solution)/shard_map/reduce_scatter | solution.py:223
  1834.3 342.3 %all-reduce.20.cloned.1.call-start = ((), (), s32[]{:S(2)}) async-start(), calls=%async_computation.20 | async-start | bytes 9437184 | tf_op jit(solution)/shard_map/psum | solution.py:361
  2012.2 38.1 %slice-start.2 = ((s8[4915200]{0:T(1024)(128)(4,1)}), s8[4194304]{0:T(1024)(128)(4,1)S(1)}, s32[]{:S(2)}) async-start(s8[4915200]{0:T(1024)(128)(4,1)} %bitcast.319), calls=%async_computation.27 | async-start | bytes 8388608
  2050.4 59.0 %copy-start.90 = (f32[4,768]{1,0:T(4,128)S(1)}, f32[4,768]{1,0:T(4,128)}, u32[]{:S(2)}) copy-start(f32[4,768]{1,0:T(4,128)} %param.39) | copy-start | bytes 36868
  2050.4 59.0 %copy-start.102 = (f32[4,768]{1,0:T(4,128)S(1)}, f32[4,768]{1,0:T(4,128)}, u32[]{:S(2)}) copy-start(f32[4,768]{1,0:T(4,128)} %param.51) | copy-start | bytes 36868
  2050.4 59.0 %copy-start.103 = (f32[4,768]{1,0:T(4,128)S(1)}, f32[4,768]{1,0:T(4,128)}, u32[]{:S(2)}) copy-start(f32[4,768]{1,0:T(4,128)} %param.50) | copy-start | bytes 36868
  (111 other events, 561.2 us)
Sparse Core Ops, SparseCore 0:
  13.9 39.7 all-gather.10
  55.9 64.4 all-gather.6
  123.2 58.4 reduce-scatter.10
  206.2 113.2 reduce-scatter.6
  321.4 37.5 all-gather.12
  361.0 64.4 all-gather.8
  428.4 59.4 reduce-scatter.12
  490.2 114.9 reduce-scatter.8
  613.2 37.5 all-gather.14
  660.6 59.0 reduce-scatter.14
  724.6 37.1 all-gather.16
  825.4 112.2 all-reduce.17
  989.0 170.2 all-reduce.27
  1213.5 171.9 all-reduce.25
  1439.6 171.9 all-reduce.23
  1617.7 144.4 all-reduce.15
  1765.2 172.1 all-reduce.21
  1940.2 59.1 reduce-scatter.16
  2003.2 173.4 all-reduce.19
where the time goes:
time: 2240 us; the launch traced here: 2230 us
  waiting for transfers between devices  1350 us (60%)
  matrix products  595 us (27%)
  blocking collectives  98.4 us (4%)
  local copies, waits for them, and re-layouts  97.7 us (4%)
  other arithmetic  64.4 us (3%)
    psum x5, waiting for transfers between devices, body(): lax.psum(gram_of(iterates[0], False).astype(jnp.bfloat16), 'tensor')  623 us
    reduce_scatter x2, waiting for transfers between devices, teacher_reduce(): lax.psum_scatter(jnp.dot(left, right, preferred_element_type=jnp.float32)...  220 us
    dot_general x25, matrix products, gram_of(): lax.dot_general(iterate, iterate, (((axis_num,), (axis_num,)), ((), ())),...  205 us
    all_gather x4, waiting for transfers between devices, student_gather(): return lax.all_gather(local_rows, 'tensor', axis=0, tiled=True)  138 us
    dot_general x15, matrix products, apply_poly(): jnp.dot(poly_mat, iterate, precision=HIGH, preferred_element_type=jnp.flo...  132 us
    psum x1, waiting for transfers between devices, body(): lax.psum((grad_qkv, grad_out, grad_fc, grad_proj), 'dp')  112 us
    psum x1, waiting for transfers between devices, body(): lax.psum((grad_map, norm_grads, loss_part), ('dp', 'tensor'))  96.9 us
    all_gather x2, waiting for transfers between devices, teacher_gather(): return lax.all_gather(local_rows, 'tensor', axis=0, tiled=True)  96.4 us
  transfers between devices with their start and end apart: 19, of which 16 were waited for; matrix products, arithmetic and copies ran while one was open for 21% of the time, Pallas kernels for 0%

commit v1 on v0

v1 whole, which is shorter than its diff:
```python
import functools
import math

import jax
import jax.numpy as jnp
from jax import lax
from jax.experimental import pallas as pl
from jax.experimental.pallas import tpu as pltpu
from jax.sharding import PartitionSpec as P

DT = 1600
HT = 25
DS = 768
FS = 3072
HEAD = 64
LEN = 1024
STEP = 10
ABLK = 256


EPS = 1e-05
NS_A = 3.4445
NS_B = -4.775
NS_C = 2.0315
MOMENTUM = 0.95
MUON_RATE = 0.5
MUON_DECAY = 0.01
ADAM_RATE = 0.3
BETA_ONE = 0.9
BETA_TWO = 0.999
ADAM_EPS = 1e-08
ADAM_DECAY = 0.01
REPLAY_CUT = 0.5
NEG_FILL = -1e30
HIGH = lax.Precision.HIGHEST


def norm_parts(v, gain_vec, shift_vec):
    row_mean = jnp.mean(v, axis=-1, keepdims=True)
    centred = v - row_mean
    row_var = jnp.mean(centred * centred, axis=-1, keepdims=True)
    inv_scale = lax.rsqrt(row_var + EPS)
    unit_val = centred * inv_scale
    return (unit_val * gain_vec + shift_vec, unit_val, inv_scale)


def norm_back(grad_norm, unit_val, inv_scale, gain_vec):
    grad_unit = grad_norm * gain_vec
    first_mean = jnp.mean(grad_unit, axis=-1, keepdims=True)
    second_mean = jnp.mean(grad_unit * unit_val, axis=-1, keepdims=True)
    return inv_scale * (grad_unit - first_mean - unit_val * second_mean)


def smooth_gelu(v):
    return 0.5 * v * (1.0 + jnp.tanh(0.7978845608028654 * (v + 0.044715 * v * v * v)))


def whole_vmem():
    return pl.BlockSpec(memory_space=pltpu.VMEM)


def nt_dot(left, right):
    return lax.dot_general(
        left, right, (((1,), (1,)), ((), ())), preferred_element_type=jnp.float32
    )


def tn_dot(left, right):
    return lax.dot_general(
        left, right, (((0,), (0,)), ((), ())), preferred_element_type=jnp.float32
    )


def plain_dot(left, right):
    return jnp.dot(left, right, preferred_element_type=jnp.float32)


def lower_mask():
    row_pos = lax.broadcasted_iota(jnp.int32, (ABLK, ABLK), 0)
    key_pos = lax.broadcasted_iota(jnp.int32, (ABLK, ABLK), 1)
    return key_pos <= row_pos


def attend_forward_kernel(head_count, qkv_ref, out_ref, log_ref):
    width = head_count * HEAD
    for head in range(head_count):
        cols = slice(head * HEAD, (head + 1) * HEAD)
        keys = qkv_ref[:, width + head * HEAD : width + (head + 1) * HEAD]
        values = qkv_ref[:, 2 * width + head * HEAD : 2 * width + (head + 1) * HEAD]
        for block in range(LEN // ABLK):
            low, high = block * ABLK, (block + 1) * ABLK
            query = qkv_ref[low:high, cols]
            near = nt_dot(query, keys[low:high]) * HEAD ** (-0.5)
            near = jnp.where(lower_mask(), near, NEG_FILL)
            row_top = jnp.max(near, axis=-1, keepdims=True)
            if block:
                far = nt_dot(query, keys[:low]) * HEAD ** (-0.5)
                row_top = jnp.maximum(row_top, jnp.max(far, axis=-1, keepdims=True))
            near = jnp.exp(near - row_top)
            row_total = jnp.sum(near, axis=-1, keepdims=True)
            if block:
                far = jnp.exp(far - row_top)
                row_total = row_total + jnp.sum(far, axis=-1, keepdims=True)
            inverse = 1.0 / row_total
            mixed = plain_dot((near * inverse).astype(jnp.bfloat16), values[low:high])
            if block:
                mixed = mixed + plain_dot((far * inverse).astype(jnp.bfloat16), values[:low])
            out_ref[low:high, cols] = mixed.astype(out_ref.dtype)
            log_ref[low:high, head : head + 1] = row_top + jnp.log(row_total)


def attend_forward(mixed_qkv, head_count):
    width = head_count * HEAD
    return pl.pallas_call(
        functools.partial(attend_forward_kernel, head_count),
        out_shape=(
            jax.ShapeDtypeStruct((LEN, width), jnp.bfloat16),
            jax.ShapeDtypeStruct((LEN, 128), jnp.float32),
        ),
        in_specs=[whole_vmem()],
        out_specs=(whole_vmem(), whole_vmem()),
        compiler_params=pltpu.CompilerParams(vmem_limit_bytes=40 * 2**20),
        cost_estimate=pl.CostEstimate(
            flops=4 * head_count * LEN * LEN * HEAD * 4,
            bytes_accessed=LEN * width * 8,
            transcendentals=head_count * LEN * LEN // 2,
        ),
    )(mixed_qkv)


def attend_backward_kernel(
    head_count, qkv_ref, log_ref, grad_ref, out_ref, key_acc, value_acc
):
    width = head_count * HEAD
    scale = HEAD ** (-0.5)
    for head in range(head_count):
        cols = slice(head * HEAD, (head + 1) * HEAD)
        key_cols = slice(width + head * HEAD, width + (head + 1) * HEAD)
        value_cols = slice(2 * width + head * HEAD, 2 * width + (head + 1) * HEAD)
        keys = qkv_ref[:, key_cols]
        values = qkv_ref[:, value_cols]
        for block in range(LEN // ABLK - 1, -1, -1):
            low, high = block * ABLK, (block + 1) * ABLK
            query = qkv_ref[low:high, cols]
            grad = grad_ref[low:high, cols]
            log_sum = log_ref[low:high, head : head + 1]
            near = nt_dot(query, keys[low:high]) * scale
            near = jnp.exp(jnp.where(lower_mask(), near, NEG_FILL) - log_sum)
            near_back = nt_dot(grad, values[low:high])
            inner = jnp.sum(near * near_back, axis=-1, keepdims=True)
            if block:
                far = jnp.exp(nt_dot(query, keys[:low]) * scale - log_sum)
                far_back = nt_dot(grad, values[:low])
                inner = inner + jnp.sum(far * far_back, axis=-1, keepdims=True)
            near_score = (near * (near_back - inner)).astype(jnp.bfloat16)
            grad_query = plain_dot(near_score, keys[low:high])
            near_key = tn_dot(near_score, query)
            near_value = tn_dot(near.astype(jnp.bfloat16), grad)
            if block == LEN // ABLK - 1:
                key_acc[low:high, :] = near_key
                value_acc[low:high, :] = near_value
            else:
                key_acc[low:high, :] += near_key
                value_acc[low:high, :] += near_value
            if block:
                far_score = (far * (far_back - inner)).astype(jnp.bfloat16)
                grad_query = grad_query + plain_dot(far_score, keys[:low])
                far_key = tn_dot(far_score, query)
                far_value = tn_dot(far.astype(jnp.bfloat16), grad)
                if block == LEN // ABLK - 1:
                    key_acc[:low, :] = far_key
                    value_acc[:low, :] = far_value
                else:
                    key_acc[:low, :] += far_key
                    value_acc[:low, :] += far_value
            out_ref[low:high, cols] = (grad_query * scale).astype(jnp.bfloat16)
        out_ref[:, key_cols] = (key_acc[...] * scale).astype(jnp.bfloat16)
        out_ref[:, value_cols] = value_acc[...].astype(jnp.bfloat16)


def attend_backward(mixed_qkv, log_sums, grad_heads, head_count):
    width = head_count * HEAD
    return pl.pallas_call(
        functools.partial(attend_backward_kernel, head_count),
        out_shape=jax.ShapeDtypeStruct((LEN, 3 * width), jnp.bfloat16),
        in_specs=[whole_vmem()] * 3,
        out_specs=whole_vmem(),
        scratch_shapes=[pltpu.VMEM((LEN, HEAD), jnp.float32)] * 2,
        compiler_params=pltpu.CompilerParams(vmem_limit_bytes=40 * 2**20),
        cost_estimate=pl.CostEstimate(
            flops=10 * head_count * LEN * LEN * HEAD * 4,
            bytes_accessed=LEN * width * 16,
            transcendentals=head_count * LEN * LEN // 2,
        ),
    )(mixed_qkv, log_sums, grad_heads)


MESH_ID = pl.DeviceIdType.MESH


def place_of():
    dp_count = lax.axis_size("dp")
    rank = lax.axis_index("dp")
    return dp_count // 2, rank // 2, rank % 2, lax.axis_index("tensor")


def greet(peers):
    barrier = pltpu.get_barrier_semaphore()
    for peer in peers:
        pl.semaphore_signal(barrier, inc=1, device_id=peer, device_id_type=MESH_ID)
    pl.semaphore_wait(barrier, len(peers))


def send_to(src, dst, send_sem, recv_sem, peer):
    return pltpu.make_async_remote_copy(
        src_ref=src,
        dst_ref=dst,
        send_sem=send_sem,
        recv_sem=recv_sem,
        device_id=peer,
        device_id_type=MESH_ID,
    )


def sum_small_kernel(
    x_ref, out_ref, pair, plane, line, pair_sems, plane_sems, line_sems
):
    chips, chip, core, depth = place_of()
    depths = lax.axis_size("tensor")
    sibling = (chip * 2 + 1 - core, depth)
    flat = [((lax.rem(chip + k, chips)) * 2 + core, depth) for k in range(1, chips)]
    deep = [(chip * 2 + core, lax.rem(depth + k, depths)) for k in range(1, depths)]
    greet([sibling] + flat + deep)
    copy = send_to(x_ref, pair, pair_sems.at[0], pair_sems.at[1], sibling)
    copy.start()
    copy.wait()
    plane[chip] = x_ref[...] + pair[...]
    copies = []
    for k in range(1, chips):
        copies.append(
            send_to(
                plane.at[chip], plane.at[chip], plane_sems.at[0, k], plane_sems.at[1, k], flat[k - 1]
            )
        )
    for copy in copies:
        copy.start()
    for copy in copies:
        copy.wait()
    total = plane[0]
    for k in range(1, chips):
        total = total + plane[k]
    line[depth] = total
    copies = []
    for k in range(1, depths):
        copies.append(
            send_to(
                line.at[depth], line.at[depth], line_sems.at[0, k], line_sems.at[1, k], deep[k - 1]
            )
        )
    for copy in copies:
        copy.start()
    for copy in copies:
        copy.wait()
    total = line[0]
    for k in range(1, depths):
        total = total + line[k]
    out_ref[...] = total


def sum_small(block, collective):
    chips, depths = lax.axis_size("dp") // 2, lax.axis_size("tensor")
    return pl.pallas_call(
        sum_small_kernel,
        out_shape=jax.ShapeDtypeStruct(block.shape, jnp.float32),
        in_specs=[whole_vmem()],
        out_specs=whole_vmem(),
        scratch_shapes=[
            pltpu.VMEM(block.shape, jnp.float32),
            pltpu.VMEM((chips,) + block.shape, jnp.float32),
            pltpu.VMEM((depths,) + block.shape, jnp.float32),
            pltpu.SemaphoreType.DMA((2,)),
            pltpu.SemaphoreType.DMA((2, chips)),
            pltpu.SemaphoreType.DMA((2, depths)),
        ],
        compiler_params=pltpu.CompilerParams(
            collective_id=collective, has_side_effects=True, vmem_limit_bytes=16 * 2**20
        ),
        cost_estimate=pl.CostEstimate(flops=10**10, bytes_accessed=10**6, transcendentals=0),
    )(block)


def sum_and_spread_kernel(
    x_ref,
    y_ref,
    x_out,
    y_out,
    pair_in,
    pair_sum,
    plane_in,
    total,
    pair_sems,
    plane_sems,
    spread_sems,
    share_sems,
):
    chips, chip, core, depth = place_of()
    rank = chip * 2 + core
    other = 1 - core
    sibling = (chip * 2 + other, depth)
    chip_at = [lax.rem(chip + k, chips) for k in range(chips)]
    flat = [(chip_at[k] * 2 + core, depth) for k in range(chips)]
    greet([sibling] + flat[1:])
    order = list(range(1, chips)) + [0]
    pair_copies, plane_copies = {}, {}
    for k in order:
        pair_copies[k] = send_to(
            x_ref.at[chip_at[k] * 2 + other],
            pair_in.at[k],
            pair_sems.at[0, k],
            pair_sems.at[1, k],
            sibling,
        )
        pair_copies[k].start()
    for k in order:
        pair_copies[k].wait_recv()
        pair_sum[k] = x_ref[chip_at[k] * 2 + core] + pair_in[k]
        if k:
            plane_copies[k] = send_to(
                pair_sum.at[k], plane_in.at[k], plane_sems.at[0, k], plane_sems.at[1, k], flat[k]
            )
            plane_copies[k].start()
    y_spread = start_spread(y_ref, y_out, spread_sems.at[0], flat, rank)
    y_out[rank] = y_ref[...]
    value = pair_sum[0]
    for k in range(1, chips):
        plane_copies[k].wait_recv()
        value = value + plane_in[k]
    total[...] = value
    x_spread = start_spread(total, x_out, spread_sems.at[1], flat, rank)
    x_out[rank] = value
    y_share = start_share(y_out, y_spread, share_sems.at[0], (chips, chip, core), sibling)
    x_share = start_share(x_out, x_spread, share_sems.at[1], (chips, chip, core), sibling)
    for k in range(chips):
        y_share[k].wait_recv()
        x_share[k].wait_recv()
    for copies in (pair_copies, plane_copies, y_spread, x_spread, y_share, x_share):
        for copy in copies.values():
            copy.wait_send()


def sum_and_spread(rows, slab_y, collective):
    dp_count = lax.axis_size("dp")
    chips = dp_count // 2
    count, width = rows.shape
    slab = (count // dp_count, width)
    out_x, out_y = pl.pallas_call(
        sum_and_spread_kernel,
        out_shape=(
            jax.ShapeDtypeStruct((dp_count,) + slab, jnp.float32),
            jax.ShapeDtypeStruct((dp_count,) + slab_y.shape, jnp.float32),
        ),
        in_specs=[whole_vmem()] * 2,
        out_specs=(whole_vmem(), whole_vmem()),
        scratch_shapes=[
            pltpu.VMEM((chips,) + slab, jnp.float32),
            pltpu.VMEM((chips,) + slab, jnp.float32),
            pltpu.VMEM((chips,) + slab, jnp.float32),
            pltpu.VMEM(slab, jnp.float32),
            pltpu.SemaphoreType.DMA((2, chips)),
            pltpu.SemaphoreType.DMA((2, chips)),
            pltpu.SemaphoreType.DMA((2, 2, chips)),
            pltpu.SemaphoreType.DMA((2, 2, chips)),
        ],
        compiler_params=pltpu.CompilerParams(
            collective_id=collective, has_side_effects=True, vmem_limit_bytes=32 * 2**20
        ),
        cost_estimate=pl.CostEstimate(
            flops=60 * 10**9, bytes_accessed=count * width * 16, transcendentals=0
        ),
    )(rows.reshape((dp_count,) + slab), slab_y)
    return out_x.reshape(count, width), out_y.reshape(-1, width)


def scatter_rows_kernel(
    x_ref, out_ref, pair_in, pair_sum, plane_in, pair_sems, plane_sems
):
    chips, chip, core, depth = place_of()
    other = 1 - core
    sibling = (chip * 2 + other, depth)
    chip_at = [lax.rem(chip + k, chips) for k in range(chips)]
    flat = [(chip_at[k] * 2 + core, depth) for k in range(chips)]
    greet([sibling] + flat[1:])
    order = list(range(1, chips)) + [0]
    pair_copies, plane_copies = {}, {}
    for k in order:
        pair_copies[k] = send_to(
            x_ref.at[chip_at[k] * 2 + other],
            pair_in.at[k],
            pair_sems.at[0, k],
            pair_sems.at[1, k],
            sibling,
        )
        pair_copies[k].start()
    for k in order:
        pair_copies[k].wait_recv()
        pair_sum[k] = x_ref[chip_at[k] * 2 + core] + pair_in[k]
        if k:
            plane_copies[k] = send_to(
                pair_sum.at[k], plane_in.at[k], plane_sems.at[0, k], plane_sems.at[1, k], flat[k]
            )
            plane_copies[k].start()
    value = pair_sum[0]
    for k in range(1, chips):
        plane_copies[k].wait_recv()
        value = value + plane_in[k]
    out_ref[...] = value
    for copies in (pair_copies, plane_copies):
        for copy in copies.values():
            copy.wait_send()


def pad_rows(rows, unit):
    have, width = rows.shape
    padded = -(-have // unit) * unit
    if padded == have:
        return rows
    return jnp.concatenate([rows, jnp.zeros((padded - have, width), rows.dtype)], axis=0)


def scatter_rows(rows, collective):
    dp_count = lax.axis_size("dp")
    chips = dp_count // 2
    slab = (rows.shape[0] // dp_count, rows.shape[1])
    return pl.pallas_call(
        scatter_rows_kernel,
        out_shape=jax.ShapeDtypeStruct(slab, jnp.float32),
        in_specs=[whole_vmem()],
        out_specs=whole_vmem(),
        scratch_shapes=[
            pltpu.VMEM((chips,) + slab, jnp.float32),
            pltpu.VMEM((chips,) + slab, jnp.float32),
            pltpu.VMEM((chips,) + slab, jnp.float32),
            pltpu.SemaphoreType.DMA((2, chips)),
            pltpu.SemaphoreType.DMA((2, chips)),
        ],
        compiler_params=pltpu.CompilerParams(
            collective_id=collective, has_side_effects=True, vmem_limit_bytes=32 * 2**20
        ),
        cost_estimate=pl.CostEstimate(
            flops=rows.shape[0] * 15 * 10**6,
            bytes_accessed=rows.shape[0] * rows.shape[1] * 4,
            transcendentals=0,
        ),
    )(rows.reshape((dp_count,) + slab))


def start_spread(src, out_ref, sems, flat, rank):
    copies = {}
    for k in range(1, len(flat)):
        copies[k] = send_to(src, out_ref.at[rank], sems.at[0, k], sems.at[1, k], flat[k])
        copies[k].start()
    return copies


def start_share(out_ref, spread_copies, sems, place, sibling):
    chips, chip, core = place
    copies = {}
    for k in range(chips):
        if k:
            spread_copies[k].wait_recv()
        held = lax.rem(chip + chips - k, chips) * 2 + core
        copies[k] = send_to(
            out_ref.at[held], out_ref.at[held], sems.at[0, k], sems.at[1, k], sibling
        )
        copies[k].start()
    return copies


def spread_and_line_kernel(
    x_ref, y_ref, x_out, y_out, line_in, line_sems, spread_sems, share_sems
):
    chips, chip, core, depth = place_of()
    depths = lax.axis_size("tensor")
    rank = chip * 2 + core
    sibling = (chip * 2 + 1 - core, depth)
    flat = [(lax.rem(chip + k, chips) * 2 + core, depth) for k in range(chips)]
    deep = [(rank, lax.rem(depth + k, depths)) for k in range(depths)]
    greet([sibling] + flat[1:] + deep[1:])
    part = y_ref.shape[0] // depths
    part_of = [
        pl.ds(pl.multiple_of(lax.rem(depth + k, depths) * part, 8), part) for k in range(depths)
    ]
    firsts, seconds = {}, {}
    for k in range(1, depths):
        firsts[k] = send_to(
            y_ref.at[part_of[k]], line_in.at[k], line_sems.at[0, k], line_sems.at[1, k], deep[k]
        )
        firsts[k].start()
    spread_copies = start_spread(x_ref, x_out, spread_sems, flat, rank)
    x_out[rank] = x_ref[...]
    value = y_ref[part_of[0]]
    for k in range(1, depths):
        firsts[k].wait_recv()
        value = value + line_in[k]
    y_out[part_of[0]] = value
    for k in range(1, depths):
        seconds[k] = send_to(
            y_out.at[part_of[0]],
            y_out.at[part_of[0]],
            line_sems.at[2, k],
            line_sems.at[3, k],
            deep[k],
        )
        seconds[k].start()
    share_copies = start_share(x_out, spread_copies, share_sems, (chips, chip, core), sibling)
    for k in range(1, depths):
        seconds[k].wait_recv()
    for k in range(chips):
        share_copies[k].wait_recv()
    for copies in (firsts, seconds, spread_copies, share_copies):
        for copy in copies.values():
            copy.wait_send()


def spread_and_line(slab, partial, collective):
    dp_count, depths = lax.axis_size("dp"), lax.axis_size("tensor")
    chips = dp_count // 2
    each, width = slab.shape
    full, total = pl.pallas_call(
        spread_and_line_kernel,
        out_shape=(
            jax.ShapeDtypeStruct((dp_count, each, width), jnp.float32),
            jax.ShapeDtypeStruct(partial.shape, jnp.float32),
        ),
        in_specs=[whole_vmem()] * 2,
        out_specs=(whole_vmem(), whole_vmem()),
        scratch_shapes=[
            pltpu.VMEM((depths, partial.shape[0] // depths, width), jnp.float32),
            pltpu.SemaphoreType.DMA((4, depths)),
            pltpu.SemaphoreType.DMA((2, chips)),
            pltpu.SemaphoreType.DMA((2, chips)),
        ],
        compiler_params=pltpu.CompilerParams(
            collective_id=collective, has_side_effects=True, vmem_limit_bytes=24 * 2**20
        ),
        cost_estimate=pl.CostEstimate(
            flops=35 * 10**9, bytes_accessed=dp_count * each * width * 4, transcendentals=0
        ),
    )(slab, partial)
    return full.reshape(dp_count * each, width), total


def line_gather_kernel(
    x_ref, out_ref, right_send, right_recv, left_send, left_recv
):
    rank = lax.axis_index("dp")
    depth = lax.axis_index("tensor")
    depths = lax.axis_size("tensor")
    last = depths - 1
    right, left = (rank, depth + 1), (rank, depth - 1)
    barrier = pltpu.get_barrier_semaphore()

    @pl.when(depth < last)
    def _():
        pl.semaphore_signal(barrier, inc=1, device_id=right, device_id_type=MESH_ID)

    @pl.when(depth > 0)
    def _():
        pl.semaphore_signal(barrier, inc=1, device_id=left, device_id_type=MESH_ID)

    @pl.when((depth > 0) & (depth < last))
    def _():
        pl.semaphore_wait(barrier, 2)

    @pl.when((depth == 0) | (depth == last))
    def _():
        pl.semaphore_wait(barrier, 1)

    def to_right(step):
        src = x_ref if step == 0 else out_ref.at[depth - step]
        return send_to(
            src, out_ref.at[depth - step], right_send.at[step], right_recv.at[step], right
        )

    def to_left(step):
        src = x_ref if step == 0 else out_ref.at[depth + step]
        return send_to(src, out_ref.at[depth + step], left_send.at[step], left_recv.at[step], left)

    for step in range(last):

        @pl.when((depth < last) & (depth >= step))
        def _():
            to_right(step).start()

        @pl.when((depth > 0) & (depth + step <= last))
        def _():
            to_left(step).start()

        if step == 0:
            out_ref[depth] = x_ref[...]

        @pl.when(depth - 1 >= step)
        def _():
            send_to(
                x_ref,
                out_ref.at[depth - 1 - step],
                right_send.at[step],
                right_recv.at[step],
                left,
            ).wait_recv()

        @pl.when(depth + 1 + step <= last)
        def _():
            send_to(
                x_ref, out_ref.at[depth + 1 + step], left_send.at[step], left_recv.at[step], right
            ).wait_recv()

    for step in range(last):

        @pl.when((depth < last) & (depth >= step))
        def _():
            to_right(step).wait_send()

        @pl.when((depth > 0) & (depth + step <= last))
        def _():
            to_left(step).wait_send()


def line_gather(block, collective):
    depths = lax.axis_size("tensor")
    rows, width = block.shape
    out = pl.pallas_call(
        line_gather_kernel,
        out_shape=jax.ShapeDtypeStruct((depths, rows, width), block.dtype),
        in_specs=[whole_vmem()],
        out_specs=whole_vmem(),
        scratch_shapes=[pltpu.SemaphoreType.DMA((depths,))] * 4,
        compiler_params=pltpu.CompilerParams(
            collective_id=collective, has_side_effects=True, vmem_limit_bytes=16 * 2**20
        ),
        cost_estimate=pl.CostEstimate(
            flops=25 * 10**9, bytes_accessed=depths * rows * width * 4, transcendentals=0
        ),
    )(block)
    return out.reshape(depths * rows, width)


NBLK = 256


def split_store(value, high_ref, low_ref, rows, cols):
    high = value.astype(jnp.bfloat16)
    high_ref[rows, cols] = high
    low_ref[rows, cols] = (value - high.astype(jnp.float32)).astype(jnp.bfloat16)


def polynomial_kernel(gram_ref, out_ref, full_g, full_h, full_m, *pairs):
    gram_pair, half_pair, poly_pair, prod_pair = (
        pairs[0:2], pairs[2:4], pairs[4:6], pairs[6:8]
    )
    size = gram_ref.shape[0]
    blocks = size // NBLK
    spans = [slice(i * NBLK, (i + 1) * NBLK) for i in range(blocks)]
    upper = [(i, j) for i in range(blocks) for j in range(i, blocks)]

    def eye(i, j):
        if i != j:
            return 0.0
        row = lax.broadcasted_iota(jnp.int32, (NBLK, NBLK), 0)
        col = lax.broadcasted_iota(jnp.int32, (NBLK, NBLK), 1)
        return jnp.where(row == col, 1.0, 0.0)

    def place(i, j, value, full, pair):
        if full is not None:
            full[spans[i], spans[j]] = value
        if pair is not None:
            split_store(value, *pair, spans[i], spans[j])
        if i != j:
            flip = value.T
            if full is not None:
                full[spans[j], spans[i]] = flip
            if pair is not None:
                split_store(flip, *pair, spans[j], spans[i])

    def product(left, right, i, j):
        return plain_dot(left[0][spans[i], :], right[0][:, spans[j]]) + (
            plain_dot(left[0][spans[i], :], right[1][:, spans[j]])
            + plain_dot(left[1][spans[i], :], right[0][:, spans[j]])
        )

    trace = 0.0
    for i in range(blocks):
        trace = trace + jnp.sum(gram_ref[spans[i], spans[i]] * eye(i, i))
    root = jnp.sqrt(jnp.full((1, 1), trace, jnp.float32)) + 1e-07
    inverse = 1.0 / root
    for i, j in upper:
        place(i, j, gram_ref[spans[i], spans[j]] * (inverse * inverse), full_g, gram_pair)

    def make_poly():
        for i, j in upper:
            value = NS_B * full_g[spans[i], spans[j]] + NS_C * product(gram_pair, gram_pair, i, j)
            place(i, j, value, None, poly_pair)

    def advance():
        for i, j in upper:
            value = NS_A * full_g[spans[i], spans[j]] + product(poly_pair, gram_pair, i, j)
            place(i, j, value, full_h, half_pair)
        for i, j in upper:
            value = NS_A * full_h[spans[i], spans[j]] + product(poly_pair, half_pair, i, j)
            place(i, j, value, full_g, gram_pair)

    make_poly()
    for i, j in upper:
        value = (
            poly_pair[0][spans[i], spans[j]].astype(jnp.float32)
            + poly_pair[1][spans[i], spans[j]].astype(jnp.float32)
            + NS_A * eye(i, j)
        )
        place(i, j, value, full_m, prod_pair)
    advance()

    def sweep(index, carry):
        make_poly()
        for i, j in upper:
            value = NS_A * full_m[spans[i], spans[j]] + product(poly_pair, prod_pair, i, j)
            place(i, j, value, full_h, None)
        for i in range(blocks):
            full_m[spans[i], :] = full_h[spans[i], :]
            split_store(full_h[spans[i], :], *prod_pair, spans[i], slice(None))
        advance()
        return carry

    lax.fori_loop(0, 3, sweep, 0)
    make_poly()
    for i, j in upper:
        value = NS_A * full_m[spans[i], spans[j]] + product(poly_pair, prod_pair, i, j)
        place(i, j, value * inverse, out_ref, None)


def orthogonal_factor(gram_mat):
    size = gram_mat.shape[0]
    return pl.pallas_call(
        polynomial_kernel,
        out_shape=jax.ShapeDtypeStruct((size, size), jnp.float32),
        in_specs=[whole_vmem()],
        out_specs=whole_vmem(),
        scratch_shapes=[pltpu.VMEM((size, size), jnp.float32)] * 3
        + [pltpu.VMEM((size, size), jnp.bfloat16)] * 8,
        compiler_params=pltpu.CompilerParams(vmem_limit_bytes=48 * 2**20),
        cost_estimate=pl.CostEstimate(
            flops=17 * 2 * 2 * size**3, bytes_accessed=8 * size * size, transcendentals=0
        ),
    )(gram_mat)


def contract_rows(left, right):
    return lax.dot_general(
        left, right, (((0,), (0,)), ((), ())), preferred_element_type=jnp.float32
    )


def contract_cols(left, right):
    return lax.dot_general(
        left, right, (((1,), (1,)), ((), ())), preferred_element_type=jnp.float32
    )


def body(
    teacher_in,
    student_in,
    resp_mask,
    replay,
    t_gains,
    t_shifts,
    t_qkv,
    t_out,
    t_fc,
    t_proj,
    s_norms,
    s_qkv,
    s_out,
    s_fc,
    s_proj,
    s_map,
    mom_qkv,
    mom_out,
    mom_fc,
    mom_proj,
    mom_map,
    adam_first,
    adam_second,
):
    groups = lax.axis_size("tensor")
    tensor_rank = lax.axis_index("tensor")
    row_count = student_in.shape[0]
    seq_count = replay.shape[0]
    total_rows = row_count * groups
    count_block = jnp.full((8, 128), jnp.sum(resp_mask), jnp.int32).astype(jnp.float32)
    count_val = sum_small(count_block, 0)[0, 0]
    tokens_all = lax.axis_size("dp") * seq_count * LEN
    factor = tokens_all / (2.0 * count_val)

    def teacher_gather(local_rows):
        return lax.all_gather(local_rows, "tensor", axis=0, tiled=True)

    def teacher_reduce(left, right):
        return lax.psum_scatter(
            jnp.dot(left, right, preferred_element_type=jnp.float32).astype(jnp.bfloat16),
            "tensor",
            scatter_dimension=0,
            tiled=True,
        ).astype(jnp.float32)

    def student_gather(local_rows):
        return lax.all_gather(local_rows, "tensor", axis=0, tiled=True)

    def student_reduce(left, right, right_dim):
        return lax.psum_scatter(
            lax.dot_general(
                left, right, (((1,), (right_dim,)), ((), ())), preferred_element_type=jnp.float32
            ).astype(jnp.bfloat16),
            "tensor",
            scatter_dimension=0,
            tiled=True,
        ).astype(jnp.float32)

    teacher_x = teacher_in.astype(jnp.float32)
    slot_width = t_qkv.shape[2]
    slot_count = slot_width // HEAD
    live_count = HT // groups + (tensor_rank < HT % groups).astype(jnp.int32)
    live_slots = (jnp.arange(slot_count, dtype=jnp.int32) < live_count).astype(jnp.float32)
    teacher_normed = norm_parts(teacher_x, t_gains[0], t_shifts[0])[0].astype(jnp.bfloat16)
    teacher_all = teacher_gather(teacher_normed)
    teacher_mixed = jnp.dot(
        teacher_all, t_qkv.reshape(DT, 3 * slot_width), preferred_element_type=jnp.float32
    ).astype(jnp.bfloat16)
    teacher_head_out = attend_forward(teacher_mixed, slot_count)[0]
    slot_mask = jnp.repeat(live_slots, HEAD)[None, :] > 0.0
    teacher_head_out = jnp.where(slot_mask, teacher_head_out, jnp.zeros_like(teacher_head_out))
    student_x = student_in.astype(jnp.float32)
    shard_width = s_qkv.shape[2]
    shard_hidden = s_fc.shape[1]
    head_count = shard_width // HEAD
    w_qkv = s_qkv.astype(jnp.bfloat16).reshape(DS, 3 * shard_width)
    w_out = s_out.astype(jnp.bfloat16)
    w_fc = s_fc.astype(jnp.bfloat16)
    w_proj = s_proj.astype(jnp.bfloat16)
    w_map = s_map.astype(jnp.bfloat16)
    normed_one, unit_one, scale_one = norm_parts(student_x, s_norms[0], s_norms[1])
    low_one = normed_one.astype(jnp.bfloat16)
    rows_one = line_gather(low_one, 5)
    mixed_qkv = jnp.dot(rows_one, w_qkv, preferred_element_type=jnp.float32).astype(jnp.bfloat16)
    head_out, log_sums = attend_forward(mixed_qkv, head_count)
    resid = student_x + student_reduce(head_out, w_out, 0)
    normed_two, unit_two, scale_two = norm_parts(resid, s_norms[2], s_norms[3])
    low_two = normed_two.astype(jnp.bfloat16)
    rows_two = line_gather(low_two, 6)
    attn_part = teacher_reduce(teacher_head_out, t_out)
    attn_part, rows_two = lax.optimization_barrier((attn_part, rows_two))
    teacher_resid = teacher_x + attn_part
    teacher_normed_two = norm_parts(teacher_resid, t_gains[1], t_shifts[1])[0].astype(jnp.bfloat16)
    teacher_hidden = smooth_gelu(
        jnp.dot(teacher_gather(teacher_normed_two), t_fc, preferred_element_type=jnp.float32)
    ).astype(jnp.bfloat16)
    teacher_out = (teacher_resid + teacher_reduce(teacher_hidden, t_proj)).astype(jnp.bfloat16)
    before = jnp.dot(rows_two, w_fc, preferred_element_type=jnp.float32)
    before, hidden = (before, smooth_gelu(before).astype(jnp.bfloat16))
    output = resid + student_reduce(hidden, w_proj, 0)
    student_out = output.astype(jnp.bfloat16)
    guess_vec = jnp.dot(student_out, w_map, preferred_element_type=jnp.float32)
    miss_vec = guess_vec - teacher_out.astype(jnp.float32)
    position = tensor_rank * row_count + jnp.arange(row_count, dtype=jnp.int32)
    seq_owner = position // LEN
    seq_pick = (seq_owner[:, None] == jnp.arange(seq_count, dtype=jnp.int32)[None, :]).astype(
        jnp.float32
    )
    flag_tok = jnp.sum(seq_pick * replay.astype(jnp.float32)[None, :], axis=1)
    weight = resp_mask.astype(jnp.float32) * (1.0 - REPLAY_CUT * flag_tok)
    loss_part = jnp.sum(weight[:, None] * miss_vec * miss_vec)
    grad_guess = (2.0 * factor * weight[:, None] * miss_vec).astype(jnp.bfloat16)
    row_unit = 8 * lax.axis_size("dp") * groups
    map_slab = scatter_rows(pad_rows(contract_rows(grad_guess, student_out), row_unit), 1)
    grad_output = contract_cols(grad_guess, w_map)
    rows_two_back, before_back, hidden_back = (rows_two, before, hidden)
    rows_one_back, mixed_back, heads_back, logs_back = (rows_one, mixed_qkv, head_out, log_sums)
    grad_mlp = student_gather(grad_output.astype(jnp.bfloat16))
    grad_mlp, map_slab = lax.optimization_barrier((grad_mlp, map_slab))
    grad_proj = contract_rows(hidden_back, grad_mlp)
    grad_hidden = contract_cols(grad_mlp, w_proj)
    gelu_vals, gelu_pull = jax.vjp(smooth_gelu, before_back)
    grad_before = gelu_pull(grad_hidden)[0].astype(jnp.bfloat16)
    grad_fc = contract_rows(rows_two_back, grad_before).reshape(-1, DS)
    mlp_slab = scatter_rows(jnp.concatenate([grad_proj, grad_fc], axis=0), 2)
    grad_normed_two = student_reduce(grad_before, w_fc, 1)
    grad_normed_two, mlp_slab = lax.optimization_barrier((grad_normed_two, mlp_slab))
    grad_resid = grad_output + norm_back(grad_normed_two, unit_two, scale_two, s_norms[2])
    grad_attn = student_gather(grad_resid.astype(jnp.bfloat16))
    grad_mlp_rows, map_slab = spread_and_line(mlp_slab, map_slab, 7)
    grad_attn, grad_mlp_rows, map_slab = lax.optimization_barrier(
        (grad_attn, grad_mlp_rows, map_slab)
    )
    grad_proj, grad_fc = grad_mlp_rows[:shard_hidden], grad_mlp_rows[shard_hidden:]
    grad_out = contract_rows(heads_back, grad_attn)
    grad_heads = contract_cols(grad_attn, w_out).astype(jnp.bfloat16)

    grad_mixed = attend_backward(mixed_back, logs_back, grad_heads, head_count)
    grad_qkv = contract_rows(grad_mixed, rows_one_back)
    grad_attn_rows, grad_map = sum_and_spread(
        jnp.concatenate([grad_out, grad_qkv], axis=0), map_slab, 3
    )
    grad_map = grad_map[:DT]
    grad_out, grad_qkv = grad_attn_rows[:shard_width], grad_attn_rows[shard_width:]
    grad_fc = grad_fc.reshape(DS, shard_hidden)
    grad_normed_one = student_reduce(grad_mixed, w_qkv, 1)
    grad_normed_one, grad_out, grad_qkv, grad_map = lax.optimization_barrier(
        (grad_normed_one, grad_out, grad_qkv, grad_map)
    )
    input_grad = grad_resid + norm_back(grad_normed_one, unit_one, scale_one, s_norms[0])
    norm_grads = jnp.stack(
        [
            jnp.sum(grad_normed_one * unit_one, axis=0),
            jnp.sum(grad_normed_one, axis=0),
            jnp.sum(grad_normed_two * unit_two, axis=0),
            jnp.sum(grad_normed_two, axis=0),
        ]
    )
    small = jnp.concatenate(
        [norm_grads, jnp.full((4, DS), loss_part, jnp.float32)], axis=0
    )
    small = sum_small(small, 4)
    norm_grads = small[:4]
    loss = small[4, 0] / (count_val * DT)

    def to_tall(mat):
        return mat.transpose(1, 2, 0).reshape(-1, DS)

    def from_tall(mat):
        return mat.reshape(3, shard_width, DS).transpose(2, 0, 1)

    moments = [
        MOMENTUM * to_tall(mom_qkv) + grad_qkv,
        MOMENTUM * mom_out + grad_out,
        MOMENTUM * mom_fc + grad_fc,
        MOMENTUM * mom_proj + grad_proj,
    ]
    moment_map = MOMENTUM * mom_map.T + grad_map
    dp_count = lax.axis_size("dp")
    dp_rank = lax.axis_index("dp")
    slice_rows = DS // dp_count
    first_row = dp_rank * slice_rows
    talls = [moments[0], moments[1], moments[2], moments[3], moment_map]
    sums = [0, 0, 1, 0, 0]

    def gram_rows(tall, axis):
        return lax.dot_general(
            lax.dynamic_slice_in_dim(tall, first_row, slice_rows, 1 - axis),
            tall,
            (((axis,), (axis,)), ((), ())),
            precision=HIGH,
            preferred_element_type=jnp.float32,
        )

    parts = jnp.concatenate([gram_rows(talls[i], sums[i]) for i in range(4)], axis=0)
    own_rows = lax.psum_scatter(parts, "tensor", scatter_dimension=0, tiled=True)
    both_rows = jnp.concatenate([own_rows[None], gram_rows(talls[4], sums[4])[None]], axis=0)
    both_rows = lax.all_gather(both_rows, "dp", axis=1, tiled=True)
    mine = dp_rank % 2
    factor_mat = orthogonal_factor(jnp.where(mine == 0, both_rows[0], both_rows[1]))
    pair_rows = lax.dynamic_slice_in_dim(factor_mat, (dp_rank // 2) * 2 * slice_rows, 2 * slice_rows, 0)
    other_rows = lax.ppermute(
        pair_rows, "dp", [(i, i ^ 1) for i in range(dp_count)]
    )
    even_rows = jnp.where(mine == 0, pair_rows, other_rows)
    odd_rows = jnp.where(mine == 0, other_rows, pair_rows)
    even_rows = lax.dynamic_slice_in_dim(even_rows, mine * slice_rows, slice_rows, 0)
    odd_rows = lax.dynamic_slice_in_dim(odd_rows, mine * slice_rows, slice_rows, 0)
    factor_rows = lax.all_gather(even_rows, "tensor", axis=0)
    pieces = [
        lax.dot_general(
            factor_rows[i] if i < 4 else odd_rows,
            talls[i],
            (((1,), (1 - sums[i],)), ((), ())),
            precision=lax.Precision.HIGH,
            preferred_element_type=jnp.float32,
        ).astype(jnp.bfloat16)
        for i in range(5)
    ]
    widths = [piece.shape[1] for piece in pieces]
    iterate_all = lax.all_gather(jnp.concatenate(pieces, axis=1), "dp", axis=0, tiled=True)
    iterates = []
    offset = 0
    for index, width in enumerate(widths):
        piece = iterate_all[:, offset : offset + width]
        iterates.append(piece if index == 2 else piece.T)
        offset += width
    iterates = [
        piece.astype(jnp.float32) for piece in lax.optimization_barrier(tuple(iterates))
    ]
    keep_rate = 1.0 - MUON_RATE * MUON_DECAY
    weight_qkv = keep_rate * to_tall(s_qkv) - MUON_RATE * math.sqrt(3.0) * iterates[0]
    weight_out = keep_rate * s_out - MUON_RATE * iterates[1]
    weight_fc = keep_rate * s_fc - MUON_RATE * math.sqrt(FS / DS) * iterates[2]
    weight_proj = keep_rate * s_proj - MUON_RATE * iterates[3]
    weight_map = keep_rate * s_map.T - MUON_RATE * math.sqrt(DT / DS) * iterates[4]
    norm_first = BETA_ONE * adam_first + (1.0 - BETA_ONE) * norm_grads
    norm_second = BETA_TWO * adam_second + (1.0 - BETA_TWO) * norm_grads * norm_grads
    fix_one = 1.0 - BETA_ONE**STEP
    fix_two = 1.0 - BETA_TWO**STEP
    norm_values = s_norms - ADAM_RATE * (
        norm_first / fix_one / (jnp.sqrt(norm_second / fix_two) + ADAM_EPS) + ADAM_DECAY * s_norms
    )
    return (
        teacher_out,
        student_out,
        input_grad,
        loss,
        from_tall(grad_qkv),
        grad_out,
        grad_fc,
        grad_proj,
        grad_map.T,
        from_tall(moments[0]),
        moments[1],
        moments[2],
        moments[3],
        moment_map.T,
        from_tall(weight_qkv),
        weight_out,
        weight_fc,
        weight_proj,
        weight_map.T,
        norm_first,
        norm_second,
        norm_values,
    )


def solution(mesh):
    return jax.shard_map(
        body,
        mesh=mesh,
        in_specs=(
            P(("dp", "tensor"), None),
            P(("dp", "tensor"), None),
            P(("dp", "tensor")),
            P("dp"),
            P(),
            P(),
            P(None, None, "tensor"),
            P("tensor", None),
            P(None, "tensor"),
            P("tensor", None),
            P(),
            P(None, None, "tensor"),
            P("tensor", None),
            P(None, "tensor"),
            P("tensor", None),
            P(),
            P(None, None, "tensor"),
            P("tensor", None),
            P(None, "tensor"),
            P("tensor", None),
            P(),
            P(),
            P(),
        ),
        out_specs=(
            P(("dp", "tensor"), None),
            P(("dp", "tensor"), None),
            P(("dp", "tensor"), None),
            P(),
            P(None, None, "tensor"),
            P("tensor", None),
            P(None, "tensor"),
            P("tensor", None),
            P(),
            P(None, None, "tensor"),
            P("tensor", None),
            P(None, "tensor"),
            P("tensor", None),
            P(),
            P(None, None, "tensor"),
            P("tensor", None),
            P(None, "tensor"),
            P("tensor", None),
            P(),
            P(),
            P(),
            P(),
        ),
        check_vma=False,
    )
```

time: 2240 us -> 916 us (0.41)
  waiting for transfers between devices: 1350 us -> 233 us
  matrix products: 595 us -> 99.2 us
  Pallas kernels: 0 us -> 434 us
  blocking collectives: 98.4 us -> 0 us
  local copies, waits for them, and re-layouts: 97.7 us -> 56.3 us
    psum x7 -> x0, waiting for transfers between devices: 833 us -> none  [the longest x5 623 us: body(): lax.psum(gram_of(iterates[0], False).astype(jnp.bfloat16), 'tensor')]
    dot_general x91 -> x10, matrix products: 500 us -> 27.1 us  [the longest x5 14.4 us: body(): lax.dot_general(factor_rows[i] if i < 4 else odd_rows, talls[i], (((1,),...]
    pallas_call x0 -> x12, Pallas kernels: none -> 434 us  [the longest x2 161 us: line_gather(): pl.pallas_call(line_gather_kernel, out_shape=jax.ShapeDtypeStruct((depths...]
    reduce_scatter x2, waiting for transfers between devices: 220 us -> 66.2 us  [teacher_reduce(): lax.psum_scatter(jnp.dot(left, right, preferred_element_type=jnp.float32)...]
    all_gather x4 -> x2, waiting for transfers between devices: 138 us -> 0.02 us  [student_gather(): return lax.all_gather(local_rows, 'tensor', axis=0, tiled=True)]
    psum x3 -> x0, blocking collectives: 98.4 us -> none  [the longest x1 44 us: body(): count = lax.psum(jnp.sum(resp_mask), ('dp', 'tensor'))]
    all_gather x0 -> x3, waiting for transfers between devices: none -> 84.3 us  [the longest x1 37.7 us: body(): both_rows = lax.all_gather(both_rows, 'dp', axis=1, tiled=True)]
    reduce_scatter x4, waiting for transfers between devices: 59.3 us -> 6.43 us  [student_reduce(): lax.psum_scatter(lax.dot_general(left, right, (((1,), (right_dim,)), ((),...]
  transfers between devices with their start and end apart: 19 -> 15, of which waited for: 16 -> 9; matrix products, arithmetic and copies ran while one was open for 21% -> 11% of each run, Pallas kernels for 0% -> 43%
where the time goes in v1:
time: 916 us; the launch traced here: 908 us
  Pallas kernels  434 us (47%)
  waiting for transfers between devices  233 us (25%)
  matrix products  99.2 us (11%)
  other arithmetic  63.8 us (7%)
  local copies, waits for them, and re-layouts  56.3 us (6%)
  between operations  19.7 us (2%)
    pallas_call x2, Pallas kernels, line_gather(): pl.pallas_call(line_gather_kernel, out_shape=jax.ShapeDtypeStruct((depths...  161 us
    pallas_call x2, Pallas kernels, scatter_rows(): pl.pallas_call(scatter_rows_kernel, out_shape=jax.ShapeDtypeStruct(slab,...  67.2 us
    reduce_scatter x2, waiting for transfers between devices, teacher_reduce(): lax.psum_scatter(jnp.dot(left, right, preferred_element_type=jnp.float32)...  66.2 us
    pallas_call x1, Pallas kernels, sum_and_spread(): pl.pallas_call(sum_and_spread_kernel, out_shape=(jax.ShapeDtypeStruct((dp...  61.1 us
    pallas_call x1, Pallas kernels, spread_and_line(): pl.pallas_call(spread_and_line_kernel, out_shape=(jax.ShapeDtypeStruct((d...  57.8 us
    all_gather x2, waiting for transfers between devices, teacher_gather(): return lax.all_gather(local_rows, 'tensor', axis=0, tiled=True)  56.5 us
    all_gather x1, waiting for transfers between devices, body(): both_rows = lax.all_gather(both_rows, 'dp', axis=1, tiled=True)  37.7 us
    unnamed x160, local copies, waits for them, and re-layouts  36.3 us
  transfers between devices with their start and end apart: 15, of which 9 were waited for; matrix products, arithmetic and copies ran while one was open for 11% of the time, Pallas kernels for 43%

profile of v1, /device:TPU:0, one launch (start us, length us, event | category | flops | bytes accessed | tf_op | source)
XLA Modules:
  0.0 908.2 jit_solution(12957234165140413317)
XLA Ops:
  14.5 3.5 broadcast_multiply_fusion
  17.9 83.1 %shard_map.391 = bf16[4,256,768]{2,1,0:T(8,128)(2,1)S(1)} custom-call(bf16[256,768]{1,0:T(8,128)(2,1)S(1)} %fusion.38.x_ref), custom_call_target="tpu_custom_call" | custom-call | flops 24999999488 | bytes 3145728 | tf_op jit(solution)/shard_map/pallas_call | solution.py:632
  103.7 6.4 shard_map.392
  113.1 8.9 convolution_convert_fusion.1.qkv_ref
  122.0 15.9 %shard_map.390 = (bf16[1024,448]{1,0:T(8,128)(2,1)S(1)}, f32[1024,128]{1,0:T(8,128)}) custom-call(bf16[1024,1344]{1,0:T(8,128)(2,1)S(1)} %convolution_convert_fusion.1.qkv_ref), custom_call_target="tpu_custom_call" | custom-call | flops 7516192768 | bytes 3670016 | tf_op jit(solution)/shard_map/pallas_call | solution.py:114
  137.9 3.6 convolution_convert_fusion.2
  141.6 6.4 reduce-scatter.10.cloned.1.call-done
  151.7 77.6 %shard_map.393 = bf16[4,256,768]{2,1,0:T(8,128)(2,1)S(1)} custom-call(bf16[256,768]{1,0:T(8,128)(2,1)S(1)} %add_convert_fusion.3.x_ref), custom_call_target="tpu_custom_call" | custom-call | flops 24999999488 | bytes 3145728 | tf_op jit(solution)/shard_map/pallas_call | solution.py:632
  229.3 4.0 reduce-scatter.8.cloned.1.call-done
  237.3 3.2 fusion.52
  245.4 56.5 %all-gather.11.cloned.1.call-done = bf16[1024,1600]{0,1:T(8,128)(2,1)} async-done(((bf16[256,1600]{0,1:T(8,128)(2,1)}), bf16[1024,1600]{0,1:T(8,128)(2,1)}) %all-gather.11.cloned.1.call-update) | async-done | bytes 3276816 | tf_op jit(solution)/shard_map/all_gather | solution.py:804
  302.0 19.1 %convolution_convert_fusion = bf16[1024,1600]{0,1:T(8,128)(2,1)} fusion(bf16[1600,1600]{1,0:T(8,128)(2,1)} %param.32, bf16[1024,1600]{0,1:T(8,128)(2,1)} %all-gather.11.cloned.1.call-done, bf16[1600,1600]{1,0:T(8,128)(2,1)} %param.31), kind=kOutput, calls=%fused_computation.14 | convolution fusion | flops 10502144000 | bytes 16793600 | tf_op jit(solution)/shard_map/dot_general | solution.py:808
  323.0 10.7 %shard_map.394 = f32[8,128]{1,0:T(8,128)S(1)} custom-call(f32[8,128]{1,0:T(8,128)S(1)} %broadcast_in_dim.23.x_ref), custom_call_target="tpu_custom_call" | custom-call | flops 10000000000 | bytes 1000000 | tf_op jit(solution)/shard_map/pallas_call | solution.py:272
  340.4 62.1 %reduce-scatter.12.cloned.1.call-done = bf16[256,1600]{0,1:T(8,128)(2,1)} async-done(((bf16[1024,1600]{0,1:T(8,128)(2,1)}), bf16[256,1600]{0,1:T(8,128)(2,1)}) %reduce-scatter.12.cloned.1.call-update) | async-done | bytes 819216 | tf_op jit(solution)/shard_map/reduce_scatter | solution.py:807
  404.9 4.2 fusion.24
  417.1 35.8 %shard_map.395.y_ref = f32[224,768]{1,0:T(8,128)S(1)} custom-call(f32[8,224,768]{2,1,0:T(8,128)S(1)} %bitcast.94), custom_call_target="tpu_custom_call" | custom-call | flops 26880000000 | bytes 5505024 | tf_op jit(solution)/shard_map/pallas_call | solution.py:434
  452.9 6.6 fusion.14
  468.6 31.4 %shard_map.396.x_ref = f32[192,768]{1,0:T(8,128)S(1)} custom-call(f32[8,192,768]{2,1,0:T(8,128)S(1)} %bitcast.95), custom_call_target="tpu_custom_call" | custom-call | flops 23040000000 | bytes 4718592 | tf_op jit(solution)/shard_map/pallas_call | solution.py:434
  504.1 57.8 %shard_map.397 = (f32[8,192,768]{2,1,0:T(8,128)S(1)}, f32[224,768]{1,0:T(8,128)S(1)}) custom-call(f32[192,768]{1,0:T(8,128)S(1)} %shard_map.396.x_ref, f32[224,768]{1,0:T(8,128)S(1)} %shard_map.395.y_ref), custom_call_target="tpu_custom_call" | custom-call | flops 35000000512 | bytes 4718592 | tf_op jit(solution)/shard_map/pallas_call | solution.py:529
  568.0 8.9 shard_map.398
  583.8 61.1 %shard_map.399 = (f32[8,96,768]{2,1,0:T(8,128)S(1)}, f32[8,224,768]{2,1,0:T(8,128)S(1)}) custom-call(f32[8,96,768]{2,1,0:T(8,128)S(1)} %bitcast.100, f32[224,768]{1,0:T(8,128)S(1)} %copy-done.10), custom_call_target="tpu_custom_call" | custom-call | flops 60000002048 | bytes 9437184 | tf_op jit(solution)/shard_map/pallas_call | solution.py:356
  651.9 3.2 multiply_add_fusion.3
  668.4 6.8 bitcast_add_fusion
  675.2 6.1 convolution_bitcast_fusion
  681.3 17.6 %reduce-scatter.20.cloned.1.call-done = f32[96,768]{1,0:T(8,128)} async-done(((f32[384,768]{1,0:T(8,128)}), f32[96,768]{1,0:T(8,128)}) %reduce-scatter.20.cloned.1.call-update) | async-done | bytes 294928 | tf_op jit(solution)/shard_map/reduce_scatter | solution.py:964
  701.2 37.7 %all-gather.17.cloned.1.call-done = f32[2,768,768]{2,1,0:T(8,128)} async-done(((f32[2,96,768]{2,1,0:T(8,128)}), f32[2,768,768]{2,1,0:T(8,128)}) %all-gather.17.cloned.1.call-update) | async-done | bytes 4718608 | tf_op jit(solution)/shard_map/all_gather | solution.py:966
  741.5 33.1 %shard_map.401 = f32[768,768]{1,0:T(8,128)S(1)} custom-call(f32[768,768]{1,0:T(8,128)S(1)} %fusion.17.gram_ref), custom_call_target="tpu_custom_call" | custom-call | flops 30802968576 | bytes 4718592 | tf_op jit(solution)/shard_map/pallas_call | solution.py:742
  779.9 4.7 convolution_convert_fusion.3
  784.6 25.6 %all-gather.21.cloned.1.call-done = f32[384,768]{1,0:T(8,128)} async-done(((f32[96,768]{1,0:T(8,128)}), f32[384,768]{1,0:T(8,128)}) %all-gather.21.cloned.1.call-update) | async-done | bytes 1179664 | tf_op jit(solution)/shard_map/all_gather | solution.py:977
  830.3 11.7 %shard_map.400 = f32[8,768]{1,0:T(8,128)S(1)} custom-call(f32[8,768]{1,0:T(8,128)S(1)} %concatenate.24.x_ref), custom_call_target="tpu_custom_call" | custom-call | flops 10000000000 | bytes 1000000 | tf_op jit(solution)/shard_map/pallas_call | solution.py:272
  845.0 21.0 %all-gather.19.cloned.1.call-done = bf16[768,3904]{1,0:T(8,128)(2,1)} async-done(((bf16[96,3904]{1,0:T(8,128)(2,1)}), bf16[768,3904]{1,0:T(8,128)(2,1)}) %all-gather.19.cloned.1.call-update) | async-done | bytes 5996560 | tf_op jit(solution)/shard_map/all_gather | solution.py:989
  892.6 6.3 fusion.5
  (295 shorter events, 147.8 us)
Async XLA Ops:
  7.2 130.7 %copy-start = (bf16[448,1600]{1,0:T(8,128)(2,1)S(1)}, bf16[448,1600]{1,0:T(8,128)(2,1)}, u32[]{:S(2)}) copy-start(bf16[448,1600]{1,0:T(8,128)(2,1)} %param.30) | copy-start | bytes 4300804
  7.2 105.9 %all-gather.9.cloned.1.call-start = ((), (), s32[]{:S(2)}) async-start(), calls=%async_computation.7 | async-start | bytes 4096000 | tf_op jit(solution)/shard_map/all_gather | solution.py:804
  13.6 134.3 %reduce-scatter.10.cloned.1.call-start = ((), (), s32[]{:S(2)}) async-start(), calls=%async_computation.9 | async-start | bytes 1966080 | tf_op jit(solution)/shard_map/reduce_scatter | solution.py:818
  13.8 136.7 %copy-start.51 = (f32[768]{0:T(1024)}, f32[768]{0:T(1024)S(1)}, u32[]{:S(2)}) copy-start(f32[768]{0:T(1024)S(1)} %get-tuple-element.151) | copy-start | bytes 9220
  17.9 83.2 %copy-start.45 = (bf16[768,3,192]{0,2,1:T(8,128)(2,1)}, bf16[768,3,192]{0,2,1:T(8,128)(2,1)S(1)}, u32[]{:S(2)}) copy-start(bf16[768,3,192]{0,2,1:T(8,128)(2,1)S(1)} %get-tuple-element.170) | copy-start | bytes 2654212
  112.6 120.7 %reduce-scatter.8.cloned.1.call-start = ((), (), s32[]{:S(2)}) async-start(), calls=%async_computation.8 | async-start | bytes 4096000 | tf_op jit(solution)/shard_map/reduce_scatter | solution.py:807
  141.5 160.4 %all-gather.11.cloned.1.call-start = ((), (), s32[]{:S(2)}) async-start(), calls=%async_computation.10 | async-start | bytes 4096000 | tf_op jit(solution)/shard_map/all_gather | solution.py:804
  149.2 80.1 %copy-start.57 = (f32[256]{0:T(256)}, f32[256]{0:T(256)S(1)}, u32[]{:S(2)}) copy-start(f32[256]{0:T(256)S(1)} %broadcast_multiply_fusion.7) | copy-start | bytes 3076
  150.4 78.9 %copy-start.61 = (f32[256]{0:T(256)}, f32[256]{0:T(256)S(1)}, u32[]{:S(2)}) copy-start(f32[256]{0:T(256)S(1)} %add_rsqrt_fusion.1) | copy-start | bytes 3076
  237.3 101.2 %reduce-scatter.14.cloned.1.call-start = ((), (), s32[]{:S(2)}) async-start(), calls=%async_computation.12 | async-start | bytes 1966080 | tf_op jit(solution)/shard_map/reduce_scatter | solution.py:818
  245.4 157.1 %reduce-scatter.12.cloned.1.call-start = ((), (), s32[]{:S(2)}) async-start(), calls=%async_computation.11 | async-start | bytes 4096000 | tf_op jit(solution)/shard_map/reduce_scatter | solution.py:807
  321.1 131.9 %all-gather.13.cloned.1.call-start = ((), (), s32[]{:S(2)}) async-start(), calls=%async_computation.13 | async-start | bytes 1966080 | tf_op jit(solution)/shard_map/all_gather | solution.py:815
  340.4 64.4 %copy-start.34 = (bf16[256,768]{1,0:T(8,128)(2,1)S(1)}, bf16[256,768]{1,0:T(8,128)(2,1)}, u32[]{:S(2)}) copy-start(bf16[256,768]{1,0:T(8,128)(2,1)} %add_convert_fusion.2) | copy-start | bytes 1179652
  414.1 86.0 %reduce-scatter.16.cloned.1.call-start = ((), (), s32[]{:S(2)}) async-start(), calls=%async_computation.14 | async-start | bytes 1966080 | tf_op jit(solution)/shard_map/reduce_scatter | solution.py:818
  463.2 100.9 %all-gather.15.cloned.1.call-start = ((), (), s32[]{:S(2)}) async-start(), calls=%async_computation.15 | async-start | bytes 1966080 | tf_op jit(solution)/shard_map/all_gather | solution.py:815
  468.5 32.7 %copy-start.21 = (bf16[256,768]{1,0:T(8,128)(2,1)S(1)}, bf16[256,768]{1,0:T(8,128)(2,1)}, u32[]{:S(2)}) copy-start(bf16[256,768]{1,0:T(8,128)(2,1)} %reduce-scatter.10.cloned.1.call-done) | copy-start | bytes 1179652
  468.5 32.7 %copy-start.52 = (f32[768]{0:T(1024)S(1)}, f32[768]{0:T(1024)}, u32[]{:S(2)}) copy-start(f32[768]{0:T(1024)} %copy-done.51) | copy-start | bytes 9220
  468.6 32.7 %copy-start.58 = (f32[256]{0:T(256)S(1)}, f32[256]{0:T(256)}, u32[]{:S(2)}) copy-start(f32[256]{0:T(256)} %copy-done.57) | copy-start | bytes 3076
  468.6 32.7 %copy-start.62 = (f32[256]{0:T(256)S(1)}, f32[256]{0:T(256)}, u32[]{:S(2)}) copy-start(f32[256]{0:T(256)} %copy-done.61) | copy-start | bytes 3076
  503.6 60.5 %copy-start.30 = (f32[192,768]{1,0:T(8,128)S(1)}, f32[192,768]{1,0:T(8,128)}, u32[]{:S(2)}) copy-start(f32[192,768]{1,0:T(8,128)} %param.35) | copy-start | bytes 1769476
  503.6 157.6 %reduce-scatter.18.cloned.1.call-start = ((), (), s32[]{:S(2)}) async-start(), calls=%async_computation.16 | async-start | bytes 1966080 | tf_op jit(solution)/shard_map/reduce_scatter | solution.py:818
  582.5 116.4 %reduce-scatter.20.cloned.1.call-start = ((), (), s32[]{:S(2)}) async-start(), calls=%async_computation.17 | async-start | bytes 1474560 | tf_op jit(solution)/shard_map/reduce_scatter | solution.py:964
  645.8 18.5 %copy-start.25 = (f32[6,96,768]{2,1,0:T(8,128)}, f32[6,96,768]{2,1,0:T(8,128)S(1)}, u32[]{:S(2)}) copy-start(f32[6,96,768]{2,1,0:T(8,128)S(1)} %slice.100) | copy-start | bytes 5308420
  668.4 70.5 %all-gather.17.cloned.1.call-start = ((), (), s32[]{:S(2)}) async-start(), calls=%async_computation.18 | async-start | bytes 5308416 | tf_op jit(solution)/shard_map/all_gather | solution.py:966
  700.7 109.5 %all-gather.21.cloned.1.call-start = ((), (), s32[]{:S(2)}) async-start(), calls=%async_computation.20 | async-start | bytes 1474560 | tf_op jit(solution)/shard_map/all_gather | solution.py:977
  775.6 2.3 collective-permute-start
  779.6 86.4 %all-gather.19.cloned.1.call-start = ((), (), s32[]{:S(2)}) async-start(), calls=%async_computation.19 | async-start | bytes 6856704 | tf_op jit(solution)/shard_map/all_gather | solution.py:989
  784.6 30.6 %copy-start.18 = (f32[768,768]{1,0:T(8,128)S(1)}, f32[768,768]{1,0:T(8,128)}, u32[]{:S(2)}) copy-start(f32[768,768]{1,0:T(8,128)} %copy-done.17) | copy-start | bytes 7077892
  830.2 12.9 %copy-start.54 = (f32[4,768]{1,0:T(4,128)S(1)}, f32[4,768]{1,0:T(4,128)}, u32[]{:S(2)}) copy-start(f32[4,768]{1,0:T(4,128)} %param.33) | copy-start | bytes 36868
  830.3 12.9 %copy-start.65 = (f32[4,768]{1,0:T(4,128)S(1)}, f32[4,768]{1,0:T(4,128)}, u32[]{:S(2)}) copy-start(f32[4,768]{1,0:T(4,128)} %param.45) | copy-start | bytes 36868
  830.3 12.9 %copy-start.66 = (f32[4,768]{1,0:T(4,128)S(1)}, f32[4,768]{1,0:T(4,128)}, u32[]{:S(2)}) copy-start(f32[4,768]{1,0:T(4,128)} %param.44) | copy-start | bytes 36868
  830.3 13.6 %copy-start.38 = (f32[256,768]{1,0:T(8,128)S(1)}, f32[256,768]{1,0:T(8,128)}, u32[]{:S(2)}) copy-start(f32[256,768]{1,0:T(8,128)} %get-tuple-element.162) | copy-start | bytes 2359300
  (61 other events, 221.6 us)
Sparse Core Ops, SparseCore 0:
  13.8 86.9 all-gather.8
  112.8 35.1 reduce-scatter.9
  150.9 82.4 reduce-scatter.7
  237.4 64.5 all-gather.10
  304.7 33.7 reduce-scatter.13
  341.2 61.2 reduce-scatter.11
  414.2 37.2 all-gather.12
  463.4 35.0 reduce-scatter.15
  503.8 58.7 all-gather.14
  582.6 36.0 reduce-scatter.17
  668.5 30.3 reduce-scatter.19
  701.2 37.6 all-gather.16
  779.8 30.4 all-gather.20
  821.1 44.8 all-gather.18

commit v2 on v1

--- a/solution.py
+++ b/solution.py
@@ -298,18 +298,33 @@
     pair_sum,
     plane_in,
     total,
+    line_in,
+    line_out,
     pair_sems,
     plane_sems,
+    line_sems,
     spread_sems,
     share_sems,
 ):
     chips, chip, core, depth = place_of()
+    depths = lax.axis_size("tensor")
     rank = chip * 2 + core
     other = 1 - core
     sibling = (chip * 2 + other, depth)
     chip_at = [lax.rem(chip + k, chips) for k in range(chips)]
     flat = [(chip_at[k] * 2 + core, depth) for k in range(chips)]
-    greet([sibling] + flat[1:])
+    deep = [(rank, lax.rem(depth + k, depths)) for k in range(depths)]
+    greet([sibling] + flat[1:] + deep[1:])
+    part = y_ref.shape[0] // depths
+    part_of = [
+        pl.ds(pl.multiple_of(lax.rem(depth + k, depths) * part, 8), part) for k in range(depths)
+    ]
+    firsts, seconds = {}, {}
+    for k in range(1, depths):
+        firsts[k] = send_to(
+            y_ref.at[part_of[k]], line_in.at[k], line_sems.at[0, k], line_sems.at[1, k], deep[k]
+        )
+        firsts[k].start()
     order = list(range(1, chips)) + [0]
     pair_copies, plane_copies = {}, {}
     for k in order:
@@ -329,8 +344,20 @@
                 pair_sum.at[k], plane_in.at[k], plane_sems.at[0, k], plane_sems.at[1, k], flat[k]
             )
             plane_copies[k].start()
-    y_spread = start_spread(y_ref, y_out, spread_sems.at[0], flat, rank)
-    y_out[rank] = y_ref[...]
+    value = y_ref[part_of[0]]
+    for k in range(1, depths):
+        firsts[k].wait_recv()
+        value = value + line_in[k]
+    line_out[part_of[0]] = value
+    for k in range(1, depths):
+        seconds[k] = send_to(
+            line_out.at[part_of[0]],
+            line_out.at[part_of[0]],
+            line_sems.at[2, k],
+            line_sems.at[3, k],
+            deep[k],
+        )
+        seconds[k].start()
     value = pair_sum[0]
     for k in range(1, chips):
         plane_copies[k].wait_recv()
@@ -338,18 +365,31 @@
     total[...] = value
     x_spread = start_spread(total, x_out, spread_sems.at[1], flat, rank)
     x_out[rank] = value
+    for k in range(1, depths):
+        seconds[k].wait_recv()
+    y_spread = start_spread(line_out, y_out, spread_sems.at[0], flat, rank)
+    y_out[rank] = line_out[...]
+    x_share = start_share(x_out, x_spread, share_sems.at[1], (chips, chip, core), sibling)
     y_share = start_share(y_out, y_spread, share_sems.at[0], (chips, chip, core), sibling)
-    x_share = start_share(x_out, x_spread, share_sems.at[1], (chips, chip, core), sibling)
     for k in range(chips):
         y_share[k].wait_recv()
         x_share[k].wait_recv()
-    for copies in (pair_copies, plane_copies, y_spread, x_spread, y_share, x_share):
+    for copies in (
+        pair_copies,
+        plane_copies,
+        firsts,
+        seconds,
+        y_spread,
+        x_spread,
+        y_share,
+        x_share,
+    ):
         for copy in copies.values():
             copy.wait_send()
 
 
 def sum_and_spread(rows, slab_y, collective):
-    dp_count = lax.axis_size("dp")
+    dp_count, depths = lax.axis_size("dp"), lax.axis_size("tensor")
     chips = dp_count // 2
     count, width = rows.shape
     slab = (count // dp_count, width)
@@ -366,8 +406,11 @@
             pltpu.VMEM((chips,) + slab, jnp.float32),
             pltpu.VMEM((chips,) + slab, jnp.float32),
             pltpu.VMEM(slab, jnp.float32),
+            pltpu.VMEM((depths, slab_y.shape[0] // depths, width), jnp.float32),
+            pltpu.VMEM(slab_y.shape, jnp.float32),
             pltpu.SemaphoreType.DMA((2, chips)),
             pltpu.SemaphoreType.DMA((2, chips)),
+            pltpu.SemaphoreType.DMA((4, depths)),
             pltpu.SemaphoreType.DMA((2, 2, chips)),
             pltpu.SemaphoreType.DMA((2, 2, chips)),
         ],
@@ -476,78 +519,43 @@
     return copies
 
 
-def spread_and_line_kernel(
-    x_ref, y_ref, x_out, y_out, line_in, line_sems, spread_sems, share_sems
-):
+def spread_kernel(x_ref, out_ref, spread_sems, share_sems):
     chips, chip, core, depth = place_of()
-    depths = lax.axis_size("tensor")
     rank = chip * 2 + core
     sibling = (chip * 2 + 1 - core, depth)
     flat = [(lax.rem(chip + k, chips) * 2 + core, depth) for k in range(chips)]
-    deep = [(rank, lax.rem(depth + k, depths)) for k in range(depths)]
-    greet([sibling] + flat[1:] + deep[1:])
-    part = y_ref.shape[0] // depths
-    part_of = [
-        pl.ds(pl.multiple_of(lax.rem(depth + k, depths) * part, 8), part) for k in range(depths)
-    ]
-    firsts, seconds = {}, {}
-    for k in range(1, depths):
-        firsts[k] = send_to(
-            y_ref.at[part_of[k]], line_in.at[k], line_sems.at[0, k], line_sems.at[1, k], deep[k]
-        )
-        firsts[k].start()
-    spread_copies = start_spread(x_ref, x_out, spread_sems, flat, rank)
-    x_out[rank] = x_ref[...]
-    value = y_ref[part_of[0]]
-    for k in range(1, depths):
-        firsts[k].wait_recv()
-        value = value + line_in[k]
-    y_out[part_of[0]] = value
-    for k in range(1, depths):
-        seconds[k] = send_to(
-            y_out.at[part_of[0]],
-            y_out.at[part_of[0]],
-            line_sems.at[2, k],
-            line_sems.at[3, k],
-            deep[k],
-        )
-        seconds[k].start()
-    share_copies = start_share(x_out, spread_copies, share_sems, (chips, chip, core), sibling)
-    for k in range(1, depths):
-        seconds[k].wait_recv()
+    greet([sibling] + flat[1:])
+    spread_copies = start_spread(x_ref, out_ref, spread_sems, flat, rank)
+    out_ref[rank] = x_ref[...]
+    share_copies = start_share(out_ref, spread_copies, share_sems, (chips, chip, core), sibling)
     for k in range(chips):
         share_copies[k].wait_recv()
-    for copies in (firsts, seconds, spread_copies, share_copies):
+    for copies in (spread_copies, share_copies):
         for copy in copies.values():
             copy.wait_send()
 
 
-def spread_and_line(slab, partial, collective):
-    dp_count, depths = lax.axis_size("dp"), lax.axis_size("tensor")
+def spread(slab, collective):
+    dp_count = lax.axis_size("dp")
     chips = dp_count // 2
     each, width = slab.shape
-    full, total = pl.pallas_call(
-        spread_and_line_kernel,
-        out_shape=(
-            jax.ShapeDtypeStruct((dp_count, each, width), jnp.float32),
-            jax.ShapeDtypeStruct(partial.shape, jnp.float32),
-        ),
-        in_specs=[whole_vmem()] * 2,
-        out_specs=(whole_vmem(), whole_vmem()),
+    full = pl.pallas_call(
+        spread_kernel,
+        out_shape=jax.ShapeDtypeStruct((dp_count, each, width), slab.dtype),
+        in_specs=[whole_vmem()],
+        out_specs=whole_vmem(),
         scratch_shapes=[
-            pltpu.VMEM((depths, partial.shape[0] // depths, width), jnp.float32),
-            pltpu.SemaphoreType.DMA((4, depths)),
             pltpu.SemaphoreType.DMA((2, chips)),
             pltpu.SemaphoreType.DMA((2, chips)),
         ],
         compiler_params=pltpu.CompilerParams(
-            collective_id=collective, has_side_effects=True, vmem_limit_bytes=24 * 2**20
+            collective_id=collective, has_side_effects=True, vmem_limit_bytes=16 * 2**20
         ),
         cost_estimate=pl.CostEstimate(
             flops=35 * 10**9, bytes_accessed=dp_count * each * width * 4, transcendentals=0
         ),
-    )(slab, partial)
-    return full.reshape(dp_count * each, width), total
+    )(slab)
+    return full.reshape(dp_count * each, width)
 
 
 def line_gather_kernel(
@@ -643,6 +651,250 @@
         ),
     )(block)
     return out.reshape(depths * rows, width)
+
+
+def renew_kernel(widths, flips, gains, iterate_ref, *refs):
+    olds, news = refs[: len(widths)], refs[len(widths) :]
+    keep_rate = 1.0 - MUON_RATE * MUON_DECAY
+    offset = 0
+    for width, flip, gain, old, new in zip(widths, flips, gains, olds, news):
+        if flip:
+            for first in range(0, width, 128):
+                size = min(128, width - first)
+                piece = iterate_ref[:, offset + first : offset + first + size]
+                rows = slice(first, first + size)
+                new[rows, :] = keep_rate * old[rows, :] - MUON_RATE * gain * (
+                    piece.astype(jnp.float32).T
+                )
+        else:
+            for first in range(0, old.shape[0], 128):
+                rows = slice(first, first + 128)
+                piece = iterate_ref[rows, offset : offset + width]
+                new[rows, :] = keep_rate * old[rows, :] - MUON_RATE * gain * (
+                    piece.astype(jnp.float32)
+                )
+        offset += width
+
+
+def renew(iterate, olds, widths, flips, gains):
+    return pl.pallas_call(
+        functools.partial(renew_kernel, widths, flips, gains),
+        out_shape=tuple(jax.ShapeDtypeStruct(old.shape, jnp.float32) for old in olds),
+        in_specs=[whole_vmem()] * (1 + len(olds)),
+        out_specs=tuple(whole_vmem() for _ in olds),
+        compiler_params=pltpu.CompilerParams(vmem_limit_bytes=48 * 2**20),
+        cost_estimate=pl.CostEstimate(
+            flops=10**9, bytes_accessed=iterate.size * 10, transcendentals=0
+        ),
+    )(iterate, *olds)
+
+
+HALF = 128
+
+
+def greet_line(depth, last, rank):
+    barrier = pltpu.get_barrier_semaphore()
+
+    @pl.when(depth < last)
+    def _():
+        pl.semaphore_signal(
+            barrier, inc=1, device_id=(rank, depth + 1), device_id_type=MESH_ID
+        )
+
+    @pl.when(depth > 0)
+    def _():
+        pl.semaphore_signal(
+            barrier, inc=1, device_id=(rank, depth - 1), device_id_type=MESH_ID
+        )
+
+    @pl.when((depth > 0) & (depth < last))
+    def _():
+        pl.semaphore_wait(barrier, 2)
+
+    @pl.when((depth == 0) | (depth == last))
+    def _():
+        pl.semaphore_wait(barrier, 1)
+
+
+def line_mlp_kernel(
+    x_ref,
+    first_ref,
+    second_ref,
+    out_ref,
+    rows,
+    parts,
+    from_left,
+    from_right,
+    stage,
+    right_sems,
+    left_sems,
+    row_sems,
+    sum_sems,
+    from_left_sems,
+    from_right_sems,
+):
+    rank = lax.axis_index("dp")
+    depth = lax.axis_index("tensor")
+    last = lax.axis_size("tensor") - 1
+    right, left = (rank, depth + 1), (rank, depth - 1)
+    greet_line(depth, last, rank)
+
+    def rows_right(j, h):
+        return send_to(rows.at[j, h], rows.at[j, h], right_sems.at[j, h], row_sems.at[j, h], right)
+
+    def rows_left(j, h):
+        return send_to(rows.at[j, h], rows.at[j, h], left_sems.at[j, h], row_sems.at[j, h], left)
+
+    def sum_right(j, h):
+        return send_to(
+            stage.at[j, h], from_left.at[j, h], sum_sems.at[j, h], from_left_sems.at[j, h], right
+        )
+
+    def sum_left(j, h):
+        return send_to(
+            stage.at[j, h], from_right.at[j, h], sum_sems.at[j, h], from_right_sems.at[j, h], left
+        )
+
+    for h in range(2):
+        rows[depth, h] = x_ref[h * HALF : (h + 1) * HALF, :]
+
+        @pl.when(depth < last)
+        def _():
+            rows_right(depth, h).start()
+
+        @pl.when(depth > 0)
+        def _():
+            rows_left(depth, h).start()
+
+    inner = depth * (last - depth) // 2
+    side = depth // 2
+    for step, shift in enumerate((1, 1, -2, 0)):
+        base = step + inner * shift
+        j = base + side * (last - 2 * base)
+
+        def half_step(h, carry):
+            if step:
+
+                @pl.when(j < depth)
+                def _():
+                    rows_right(j, h).wait_recv()
+
+                @pl.when(j > depth)
+                def _():
+                    rows_left(j, h).wait_recv()
+
+                @pl.when((j < depth) & (depth < last))
+                def _():
+                    rows_right(j, h).start()
+
+                @pl.when((j > depth) & (depth > 0))
+                def _():
+                    rows_left(j, h).start()
+
+            hidden = smooth_gelu(plain_dot(rows[j, h], first_ref[...])).astype(jnp.bfloat16)
+            part = plain_dot(hidden, second_ref[...])
+            parts[j, h] = part
+            if step:
+
+                @pl.when((depth == 0) | (depth == last))
+                def _():
+                    stage[j, h] = part.astype(jnp.bfloat16)
+
+                @pl.when(depth == 0)
+                def _():
+                    sum_right(j, h).start()
+
+                @pl.when(depth == last)
+                def _():
+                    sum_left(j, h).start()
+
+            return carry
+
+        lax.fori_loop(0, 2, half_step, 0)
+
+    def relay_right(j):
+        for h in range(2):
+            sum_right(j, h).wait_recv()
+            stage[j, h] = (parts[j, h] + from_left[j, h].astype(jnp.float32)).astype(jnp.bfloat16)
+            sum_right(j, h).start()
+
+    def relay_left(j):
+        for h in range(2):
+            sum_left(j, h).wait_recv()
+            stage[j, h] = (parts[j, h] + from_right[j, h].astype(jnp.float32)).astype(jnp.bfloat16)
+            sum_left(j, h).start()
+
+    @pl.when(depth == 1)
+    def _():
+        relay_right(2)
+        relay_right(3)
+        relay_left(0)
+
+    @pl.when(depth == 2)
+    def _():
+        relay_left(1)
+        relay_left(0)
+        relay_right(3)
+
+    for h in range(2):
+        span = slice(h * HALF, (h + 1) * HALF)
+        out_ref[span, :] = parts[depth, h]
+
+        @pl.when(depth > 0)
+        def _():
+            sum_right(depth, h).wait_recv()
+            out_ref[span, :] += from_left[depth, h].astype(jnp.float32)
+
+        @pl.when(depth < last)
+        def _():
+            sum_left(depth, h).wait_recv()
+            out_ref[span, :] += from_right[depth, h].astype(jnp.float32)
+
+    for j in range(4):
+        for h in range(2):
+
+            @pl.when((depth >= j) & (depth < last))
+            def _():
+                rows_right(j, h).wait_send()
+
+            @pl.when((depth <= j) & (depth > 0))
+            def _():
+                rows_left(j, h).wait_send()
+
+            @pl.when(depth < j)
+            def _():
+                sum_right(j, h).wait_send()
+
+            @pl.when(depth > j)
+            def _():
+                sum_left(j, h).wait_send()
+
+
+def line_mlp(block, first, second, collective):
+    count, width = block.shape
+    slots = (4, 2, HALF, width)
+    return pl.pallas_call(
+        line_mlp_kernel,
+        out_shape=jax.ShapeDtypeStruct((count, width), jnp.float32),
+        in_specs=[whole_vmem()] * 3,
+        out_specs=whole_vmem(),
+        scratch_shapes=[
+            pltpu.VMEM(slots, jnp.bfloat16),
+            pltpu.VMEM(slots, jnp.float32),
+            pltpu.VMEM(slots, jnp.bfloat16),
+            pltpu.VMEM(slots, jnp.bfloat16),
+            pltpu.VMEM(slots, jnp.bfloat16),
+        ]
+        + [pltpu.SemaphoreType.DMA((4, 2))] * 6,
+        compiler_params=pltpu.CompilerParams(
+            collective_id=collective, has_side_effects=True, vmem_limit_bytes=48 * 2**20
+        ),
+        cost_estimate=pl.CostEstimate(
+            flops=16 * count * width * first.shape[1] * 4,
+            bytes_accessed=16 * count * width,
+            transcendentals=4 * count * first.shape[1],
+        ),
+    )(block, first, second)
 
 
 NBLK = 256
@@ -859,10 +1111,8 @@
     attn_part, rows_two = lax.optimization_barrier((attn_part, rows_two))
     teacher_resid = teacher_x + attn_part
     teacher_normed_two = norm_parts(teacher_resid, t_gains[1], t_shifts[1])[0].astype(jnp.bfloat16)
-    teacher_hidden = smooth_gelu(
-        jnp.dot(teacher_gather(teacher_normed_two), t_fc, preferred_element_type=jnp.float32)
-    ).astype(jnp.bfloat16)
-    teacher_out = (teacher_resid + teacher_reduce(teacher_hidden, t_proj)).astype(jnp.bfloat16)
+    mlp_part = line_mlp(teacher_normed_two, t_fc, t_proj, 8)
+    teacher_out = (teacher_resid + mlp_part).astype(jnp.bfloat16)
     before = jnp.dot(rows_two, w_fc, preferred_element_type=jnp.float32)
     before, hidden = (before, smooth_gelu(before).astype(jnp.bfloat16))
     output = resid + student_reduce(hidden, w_proj, 0)
@@ -895,10 +1145,8 @@
     grad_normed_two, mlp_slab = lax.optimization_barrier((grad_normed_two, mlp_slab))
     grad_resid = grad_output + norm_back(grad_normed_two, unit_two, scale_two, s_norms[2])
     grad_attn = student_gather(grad_resid.astype(jnp.bfloat16))
-    grad_mlp_rows, map_slab = spread_and_line(mlp_slab, map_slab, 7)
-    grad_attn, grad_mlp_rows, map_slab = lax.optimization_barrier(
-        (grad_attn, grad_mlp_rows, map_slab)
-    )
+    grad_mlp_rows = spread(mlp_slab, 7)
+    grad_attn, grad_mlp_rows = lax.optimization_barrier((grad_attn, grad_mlp_rows))
     grad_proj, grad_fc = grad_mlp_rows[:shard_hidden], grad_mlp_rows[shard_hidden:]
     grad_out = contract_rows(heads_back, grad_attn)
     grad_heads = contract_cols(grad_attn, w_out).astype(jnp.bfloat16)
@@ -911,26 +1159,6 @@
     grad_map = grad_map[:DT]
     grad_out, grad_qkv = grad_attn_rows[:shard_width], grad_attn_rows[shard_width:]
     grad_fc = grad_fc.reshape(DS, shard_hidden)
-    grad_normed_one = student_reduce(grad_mixed, w_qkv, 1)
-    grad_normed_one, grad_out, grad_qkv, grad_map = lax.optimization_barrier(
-        (grad_normed_one, grad_out, grad_qkv, grad_map)
-    )
-    input_grad = grad_resid + norm_back(grad_normed_one, unit_one, scale_one, s_norms[0])
-    norm_grads = jnp.stack(
-        [
-            jnp.sum(grad_normed_one * unit_one, axis=0),
-            jnp.sum(grad_normed_one, axis=0),
-            jnp.sum(grad_normed_two * unit_two, axis=0),
-            jnp.sum(grad_normed_two, axis=0),
-        ]
-    )
-    small = jnp.concatenate(
-        [norm_grads, jnp.full((4, DS), loss_part, jnp.float32)], axis=0
-    )
-    small = sum_small(small, 4)
-    norm_grads = small[:4]
-    loss = small[4, 0] / (count_val * DT)
-
     def to_tall(mat):
         return mat.transpose(1, 2, 0).reshape(-1, DS)
 
@@ -964,6 +1192,8 @@
     own_rows = lax.psum_scatter(parts, "tensor", scatter_dimension=0, tiled=True)
     both_rows = jnp.concatenate([own_rows[None], gram_rows(talls[4], sums[4])[None]], axis=0)
     both_rows = lax.all_gather(both_rows, "dp", axis=1, tiled=True)
+    both_rows, grad_mixed = lax.optimization_barrier((both_rows, grad_mixed))
+    grad_normed_one = student_reduce(grad_mixed, w_qkv, 1)
     mine = dp_rank % 2
     factor_mat = orthogonal_factor(jnp.where(mine == 0, both_rows[0], both_rows[1]))
     pair_rows = lax.dynamic_slice_in_dim(factor_mat, (dp_rank // 2) * 2 * slice_rows, 2 * slice_rows, 0)
@@ -974,7 +1204,24 @@
     odd_rows = jnp.where(mine == 0, other_rows, pair_rows)
     even_rows = lax.dynamic_slice_in_dim(even_rows, mine * slice_rows, slice_rows, 0)
     odd_rows = lax.dynamic_slice_in_dim(odd_rows, mine * slice_rows, slice_rows, 0)
+    even_rows, grad_normed_one = lax.optimization_barrier((even_rows, grad_normed_one))
     factor_rows = lax.all_gather(even_rows, "tensor", axis=0)
+    input_grad = grad_resid + norm_back(grad_normed_one, unit_one, scale_one, s_norms[0])
+    norm_grads = jnp.stack(
+        [
+            jnp.sum(grad_normed_one * unit_one, axis=0),
+            jnp.sum(grad_normed_one, axis=0),
+            jnp.sum(grad_normed_two * unit_two, axis=0),
+            jnp.sum(grad_normed_two, axis=0),
+        ]
+    )
+    small = jnp.concatenate(
+        [norm_grads, jnp.full((4, DS), loss_part, jnp.float32)], axis=0
+    )
+    small = sum_small(small, 4)
+    norm_grads = small[:4]
+    loss = small[4, 0] / (count_val * DT)
+
     pieces = [
         lax.dot_general(
             factor_rows[i] if i < 4 else odd_rows,
@@ -983,25 +1230,16 @@
             precision=lax.Precision.HIGH,
             preferred_element_type=jnp.float32,
         ).astype(jnp.bfloat16)
-        for i in range(5)
+        for i in (2, 3, 1, 0, 4)
     ]
-    widths = [piece.shape[1] for piece in pieces]
     iterate_all = lax.all_gather(jnp.concatenate(pieces, axis=1), "dp", axis=0, tiled=True)
-    iterates = []
-    offset = 0
-    for index, width in enumerate(widths):
-        piece = iterate_all[:, offset : offset + width]
-        iterates.append(piece if index == 2 else piece.T)
-        offset += width
-    iterates = [
-        piece.astype(jnp.float32) for piece in lax.optimization_barrier(tuple(iterates))
-    ]
-    keep_rate = 1.0 - MUON_RATE * MUON_DECAY
-    weight_qkv = keep_rate * to_tall(s_qkv) - MUON_RATE * math.sqrt(3.0) * iterates[0]
-    weight_out = keep_rate * s_out - MUON_RATE * iterates[1]
-    weight_fc = keep_rate * s_fc - MUON_RATE * math.sqrt(FS / DS) * iterates[2]
-    weight_proj = keep_rate * s_proj - MUON_RATE * iterates[3]
-    weight_map = keep_rate * s_map.T - MUON_RATE * math.sqrt(DT / DS) * iterates[4]
+    weight_fc, weight_proj, weight_out, weight_qkv, weight_map = renew(
+        iterate_all,
+        (s_fc, s_proj, s_out, to_tall(s_qkv), s_map.T),
+        [piece.shape[1] for piece in pieces],
+        [False, True, True, True, True],
+        [math.sqrt(FS / DS), 1.0, 1.0, math.sqrt(3.0), math.sqrt(DT / DS)],
+    )
     norm_first = BETA_ONE * adam_first + (1.0 - BETA_ONE) * norm_grads
     norm_second = BETA_TWO * adam_second + (1.0 - BETA_TWO) * norm_grads * norm_grads
     fix_one = 1.0 - BETA_ONE**STEP

time: 916 us -> 852 us (0.930)
  waiting for transfers between devices: 233 us -> 108 us
  Pallas kernels: 434 us -> 543 us
  matrix products: 99.2 us -> 73 us
  local copies, waits for them, and re-layouts: 56.3 us -> 43.9 us
  other arithmetic: 63.8 us -> 51.9 us
    pallas_call x1 -> x3, Pallas kernels: 57.8 us -> 167 us  [the longest x1 125 us: line_mlp(): pl.pallas_call(line_mlp_kernel, out_shape=jax.ShapeDtypeStruct((count, wi...]
    reduce_scatter x2 -> x1, waiting for transfers between devices: 66.2 us -> 0.01 us  [teacher_reduce(): lax.psum_scatter(jnp.dot(left, right, preferred_element_type=jnp.float32)...]
    all_gather x2 -> x1, waiting for transfers between devices: 56.5 us -> 0.01 us  [teacher_gather(): return lax.all_gather(local_rows, 'tensor', axis=0, tiled=True)]
    dot_general x2 -> x1, matrix products: 22.7 us -> 3.63 us  [teacher_reduce(): jnp.dot(left, right, preferred_element_type=jnp.float32)]
    unnamed x160 -> x180, local copies, waits for them, and re-layouts: 36.3 us -> 31.6 us
  transfers between devices with their start and end apart: 15 -> 13, of which waited for: 9 -> 6; matrix products, arithmetic and copies ran while one was open for 11% -> 8% of each run, Pallas kernels for 43% -> 54%
where the time goes in v2:
time: 852 us; the launch traced here: 842 us
  Pallas kernels  543 us (64%)
  waiting for transfers between devices  108 us (13%)
  matrix products  73 us (9%)
  other arithmetic  51.9 us (6%)
  local copies, waits for them, and re-layouts  43.9 us (5%)
  between operations  20.1 us (2%)
    pallas_call x2, Pallas kernels, line_gather(): pl.pallas_call(line_gather_kernel, out_shape=jax.ShapeDtypeStruct((depths...  154 us
    pallas_call x1, Pallas kernels, line_mlp(): pl.pallas_call(line_mlp_kernel, out_shape=jax.ShapeDtypeStruct((count, wi...  125 us
    pallas_call x2, Pallas kernels, scatter_rows(): pl.pallas_call(scatter_rows_kernel, out_shape=jax.ShapeDtypeStruct(slab,...  68.9 us
    pallas_call x1, Pallas kernels, sum_and_spread(): pl.pallas_call(sum_and_spread_kernel, out_shape=(jax.ShapeDtypeStruct((dp...  65.6 us
    all_gather x1, waiting for transfers between devices, body(): both_rows = lax.all_gather(both_rows, 'dp', axis=1, tiled=True)  38.2 us
    pallas_call x1, Pallas kernels, orthogonal_factor(): pl.pallas_call(polynomial_kernel, out_shape=jax.ShapeDtypeStruct((size, s...  33.1 us
    unnamed x180, local copies, waits for them, and re-layouts  31.6 us
    pallas_call x1, Pallas kernels, spread(): pl.pallas_call(spread_kernel, out_shape=jax.ShapeDtypeStruct((dp_count, e...  31.4 us
  transfers between devices with their start and end apart: 13, of which 6 were waited for; matrix products, arithmetic and copies ran while one was open for 8% of the time, Pallas kernels for 54%

profile of v2, /device:TPU:0, one launch (start us, length us, event | category | flops | bytes accessed | tf_op | source)
XLA Modules:
  0.0 841.8 jit_solution(3290534575510660087)
XLA Ops:
  16.9 85.2 %shard_map.391 = bf16[4,256,768]{2,1,0:T(8,128)(2,1)S(1)} custom-call(bf16[256,768]{1,0:T(8,128)(2,1)S(1)} %fusion.27.x_ref), custom_call_target="tpu_custom_call" | custom-call | flops 24999999488 | bytes 3145728 | tf_op jit(solution)/shard_map/pallas_call | solution.py:640
  104.8 6.4 shard_map.392
  114.8 9.0 %convolution_convert_fusion.qkv_ref = bf16[1024,1344]{1,0:T(8,128)(2,1)S(1)} fusion(bf16[1024,1600]{1,0:T(8,128)(2,1)} %all-gather.8.cloned.1.call-done, bf16[1600,1344]{0,1:T(8,128)(2,1)} %bitcast.107), kind=kOutput, calls=%fused_computation.7 | convolution fusion | flops 4405395456 | bytes 10330112 | tf_op jit(solution)/shard_map/dot_general | solution.py:1086
  123.8 15.9 %shard_map.390 = (bf16[1024,448]{1,0:T(8,128)(2,1)S(1)}, f32[1024,128]{1,0:T(8,128)}) custom-call(bf16[1024,1344]{1,0:T(8,128)(2,1)S(1)} %convolution_convert_fusion.qkv_ref), custom_call_target="tpu_custom_call" | custom-call | flops 7516192768 | bytes 3670016 | tf_op jit(solution)/shard_map/pallas_call | solution.py:114
  139.7 3.6 convolution_convert_fusion.1
  143.3 5.4 copy.52
  150.7 10.6 %shard_map.395 = f32[8,128]{1,0:T(8,128)S(1)} custom-call(f32[8,128]{1,0:T(8,128)S(1)} %broadcast_in_dim.23.x_ref), custom_call_target="tpu_custom_call" | custom-call | flops 10000000000 | bytes 1000000 | tf_op jit(solution)/shard_map/pallas_call | solution.py:272
  169.7 69.1 %shard_map.393 = bf16[4,256,768]{2,1,0:T(8,128)(2,1)S(1)} custom-call(bf16[256,768]{1,0:T(8,128)(2,1)S(1)} %add_convert_fusion.3.x_ref), custom_call_target="tpu_custom_call" | custom-call | flops 24999999488 | bytes 3145728 | tf_op jit(solution)/shard_map/pallas_call | solution.py:640
  247.2 3.1 convolution_convert_fusion.5
  252.5 124.9 %shard_map.394 = f32[256,1600]{1,0:T(8,128)S(1)} custom-call(bf16[256,1600]{1,0:T(8,128)(2,1)S(1)} %add_convert_fusion.1.x_ref, bf16[1600,1600]{1,0:T(8,128)(2,1)} %first_ref.1, bf16[1600,1600]{1,0:T(8,128)(2,1)} %second_ref.1), custom_call_target="tpu_custom_call" | custom-call | flops 41943040000 | bytes 6553600 | tf_op jit(solution)/shard_map/pallas_call | solution.py:876
  379.8 4.3 fusion.13
  384.1 3.2 fusion.75
  392.3 37.4 %shard_map.396.y_ref = f32[224,768]{1,0:T(8,128)S(1)} custom-call(f32[8,224,768]{2,1,0:T(8,128)S(1)} %bitcast.83), custom_call_target="tpu_custom_call" | custom-call | flops 26880000000 | bytes 5505024 | tf_op jit(solution)/shard_map/pallas_call | solution.py:477
  429.8 6.7 fusion.3
  440.3 3.5 fusion.81
  446.0 31.5 %shard_map.397.x_ref = f32[192,768]{1,0:T(8,128)S(1)} custom-call(f32[8,192,768]{2,1,0:T(8,128)S(1)} %bitcast.84), custom_call_target="tpu_custom_call" | custom-call | flops 23040000000 | bytes 4718592 | tf_op jit(solution)/shard_map/pallas_call | solution.py:477
  482.7 31.4 %shard_map.398 = f32[8,192,768]{2,1,0:T(8,128)S(1)} custom-call(f32[192,768]{1,0:T(8,128)S(1)} %shard_map.397.x_ref), custom_call_target="tpu_custom_call" | custom-call | flops 35000000512 | bytes 4718592 | tf_op jit(solution)/shard_map/pallas_call | solution.py:542
  524.7 8.9 %shard_map.399 = bf16[1024,576]{1,0:T(8,128)(2,1)S(1)} custom-call(bf16[1024,576]{1,0:T(8,128)(2,1)S(1)} %copy-done.22, f32[1024,128]{1,0:T(8,128)S(1)} %copy-done.24, bf16[1024,192]{1,0:T(8,128)(2,1)S(1)} %copy-done.14), custom_call_target="tpu_custom_call" | custom-call | flops 8053063680 | bytes 3145728 | tf_op jit(solution)/shard_map/pallas_call | solution.py:183
  536.9 65.6 %shard_map.400 = (f32[8,96,768]{2,1,0:T(8,128)S(1)}, f32[8,224,768]{2,1,0:T(8,128)S(1)}) custom-call(f32[8,96,768]{2,1,0:T(8,128)S(1)} %bitcast.89, f32[224,768]{1,0:T(8,128)S(1)} %copy-done.26), custom_call_target="tpu_custom_call" | custom-call | flops 60000002048 | bytes 9437184 | tf_op jit(solution)/shard_map/pallas_call | solution.py:396
  610.2 3.2 multiply_add_fusion.3
  618.7 6.8 slice_bitcast_fusion
  627.7 3.2 convolution_bitcast_fusion
  630.9 18.4 %reduce-scatter.15.cloned.1.call-done = f32[96,768]{1,0:T(8,128)} async-done(((f32[384,768]{1,0:T(8,128)}), f32[96,768]{1,0:T(8,128)}) %reduce-scatter.15.cloned.1.call-update) | async-done | bytes 294928 | tf_op jit(solution)/shard_map/reduce_scatter | solution.py:1192
  651.2 38.2 %all-gather.14.cloned.1.call-done = f32[2,768,768]{2,1,0:T(8,128)} async-done(((f32[2,96,768]{2,1,0:T(8,128)}), f32[2,768,768]{2,1,0:T(8,128)}) %all-gather.14.cloned.1.call-update) | async-done | bytes 4718608 | tf_op jit(solution)/shard_map/all_gather | solution.py:1194
  689.5 3.7 convolution_convert_fusion.3
  696.3 33.1 %shard_map.401 = f32[768,768]{1,0:T(8,128)S(1)} custom-call(f32[768,768]{1,0:T(8,128)S(1)} %select_bitcast_fusion.gram_ref), custom_call_target="tpu_custom_call" | custom-call | flops 30802968576 | bytes 4718592 | tf_op jit(solution)/shard_map/pallas_call | solution.py:994
  737.1 4.8 convolution_convert_fusion.2
  741.9 25.5 %all-gather.18.cloned.1.call-done = f32[384,768]{1,0:T(8,128)} async-done(((f32[96,768]{1,0:T(8,128)}), f32[384,768]{1,0:T(8,128)}) %all-gather.18.cloned.1.call-update) | async-done | bytes 1179664 | tf_op jit(solution)/shard_map/all_gather | solution.py:1208
  777.0 3.5 fusion.8
  781.7 11.5 %shard_map.402 = f32[8,768]{1,0:T(8,128)S(1)} custom-call(f32[8,768]{1,0:T(8,128)S(1)} %concatenate.26.x_ref), custom_call_target="tpu_custom_call" | custom-call | flops 10000000000 | bytes 1000000 | tf_op jit(solution)/shard_map/pallas_call | solution.py:272
  796.3 23.7 %all-gather.16.cloned.1.call-done.iterate_ref = bf16[768,3904]{1,0:T(8,128)(2,1)} async-done(((bf16[96,3904]{1,0:T(8,128)(2,1)}), bf16[768,3904]{1,0:T(8,128)(2,1)}) %all-gather.16.cloned.1.call-update) | async-done | bytes 5996560 | tf_op jit(solution)/shard_map/all_gather | solution.py:1235
  822.8 10.8 %shard_map.403 = (f32[768,768]{1,0:T(8,128)}, f32[768,768]{1,0:T(8,128)}, f32[192,768]{1,0:T(8,128)}, f32[576,768]{1,0:T(8,128)}, f32[1600,768]{1,0:T(8,128)}) custom-call(bf16[768,3904]{1,0:T(8,128)(2,1)} %all-gather.16.cloned.1.call-done.iterate_ref, f32[768,768]{1,0:T(8,128)S(1)} %copy-done.10, f32[768,768]{1,0:T(8,128)} %refs_1_.1, ...), custom_call_target="tpu_custom_call" | custom-call | flops 1000000000 | bytes 29982720 | tf_op jit(solution)/shard_map/pallas_call | solution.py:680
  (299 shorter events, 109.2 us)
Async XLA Ops:
  7.2 132.5 %copy-start = (bf16[448,1600]{1,0:T(8,128)(2,1)S(1)}, bf16[448,1600]{1,0:T(8,128)(2,1)}, u32[]{:S(2)}) copy-start(bf16[448,1600]{1,0:T(8,128)(2,1)} %param.30) | copy-start | bytes 4300804
  7.2 107.6 %all-gather.8.cloned.1.call-start = ((), (), s32[]{:S(2)}) async-start(), calls=%async_computation.6 | async-start | bytes 4259840 | tf_op jit(solution)/shard_map/all_gather | solution.py:1056
  15.2 150.9 %reduce-scatter.9.cloned.1.call-start = ((), (), s32[]{:S(2)}) async-start(), calls=%async_computation.8 | async-start | bytes 1966080 | tf_op jit(solution)/shard_map/reduce_scatter | solution.py:1070
  15.4 86.9 %copy-start.57 = (bf16[768,3,192]{0,2,1:T(8,128)(2,1)}, bf16[768,3,192]{0,2,1:T(8,128)(2,1)S(1)}, u32[]{:S(2)}) copy-start(bf16[768,3,192]{0,2,1:T(8,128)(2,1)S(1)} %convert_element_type.136) | copy-start | bytes 2654212
  16.2 85.9 %copy-start.60 = (f32[768]{0:T(1024)}, f32[768]{0:T(1024)S(1)}, u32[]{:S(2)}) copy-start(f32[768]{0:T(1024)S(1)} %get-tuple-element.122) | copy-start | bytes 9220
  16.2 152.3 %copy-start.62 = (f32[768]{0:T(1024)}, f32[768]{0:T(1024)S(1)}, u32[]{:S(2)}) copy-start(f32[768]{0:T(1024)S(1)} %get-tuple-element.123) | copy-start | bytes 9220
  16.4 85.8 %copy-start.66 = (f32[256]{0:T(256)}, f32[256]{0:T(256)S(1)}, u32[]{:S(2)}) copy-start(f32[256]{0:T(256)S(1)} %broadcast_multiply_fusion.7) | copy-start | bytes 3076
  16.6 85.5 %copy-start.70 = (f32[256]{0:T(256)}, f32[256]{0:T(256)S(1)}, u32[]{:S(2)}) copy-start(f32[256]{0:T(256)S(1)} %add_rsqrt_fusion.2) | copy-start | bytes 3076
  114.5 125.5 %reduce-scatter.7.cloned.1.call-start = ((), (), s32[]{:S(2)}) async-start(), calls=%async_computation.7 | async-start | bytes 4259840 | tf_op jit(solution)/shard_map/reduce_scatter | solution.py:1059
  148.7 229.9 %reduce-scatter.11.cloned.1.call-start = ((), (), s32[]{:S(2)}) async-start(), calls=%async_computation.9 | async-start | bytes 1966080 | tf_op jit(solution)/shard_map/reduce_scatter | solution.py:1070
  167.2 71.6 %copy-start.68 = (f32[256]{0:T(256)}, f32[256]{0:T(256)S(1)}, u32[]{:S(2)}) copy-start(f32[256]{0:T(256)S(1)} %broadcast_multiply_fusion.6) | copy-start | bytes 3076
  168.5 70.4 %copy-start.72 = (f32[256]{0:T(256)}, f32[256]{0:T(256)S(1)}, u32[]{:S(2)}) copy-start(f32[256]{0:T(256)S(1)} %add_rsqrt_fusion.1) | copy-start | bytes 3076
  250.4 179.4 %all-gather.10.cloned.1.call-start = ((), (), s32[]{:S(2)}) async-start(), calls=%async_computation.10 | async-start | bytes 1966080 | tf_op jit(solution)/shard_map/all_gather | solution.py:1067
  252.5 124.9 %copy-start.28 = (bf16[256,1600]{1,0:T(8,128)(2,1)S(1)}, bf16[256,1600]{1,0:T(8,128)(2,1)}, u32[]{:S(2)}) copy-start(bf16[256,1600]{1,0:T(8,128)(2,1)} %copy.51) | copy-start | bytes 2457604
  252.5 124.9 %copy-start.34 = (f32[256,1600]{1,0:T(8,128)S(1)}, f32[256,1600]{1,0:T(8,128)}, u32[]{:S(2)}) copy-start(f32[256,1600]{1,0:T(8,128)} %copy-done.33) | copy-start | bytes 4915204
  389.3 88.3 %reduce-scatter.13.cloned.1.call-start = ((), (), s32[]{:S(2)}) async-start(), calls=%async_computation.11 | async-start | bytes 1966080 | tf_op jit(solution)/shard_map/reduce_scatter | solution.py:1070
  440.2 76.5 %all-gather.12.cloned.1.call-start = ((), (), s32[]{:S(2)}) async-start(), calls=%async_computation.12 | async-start | bytes 1966080 | tf_op jit(solution)/shard_map/all_gather | solution.py:1067
  446.0 32.7 %copy-start.63 = (f32[768]{0:T(1024)S(1)}, f32[768]{0:T(1024)}, u32[]{:S(2)}) copy-start(f32[768]{0:T(1024)} %copy-done.62) | copy-start | bytes 9220
  446.0 32.7 %copy-start.69 = (f32[256]{0:T(256)S(1)}, f32[256]{0:T(256)}, u32[]{:S(2)}) copy-start(f32[256]{0:T(256)} %copy-done.68) | copy-start | bytes 3076
  446.0 32.7 %copy-start.73 = (f32[256]{0:T(256)S(1)}, f32[256]{0:T(256)}, u32[]{:S(2)}) copy-start(f32[256]{0:T(256)} %copy-done.72) | copy-start | bytes 3076
  482.2 34.5 %copy-start.12 = (bf16[1024,192]{1,0:T(8,128)(2,1)S(1)}, bf16[1024,192]{1,0:T(8,128)(2,1)}, u32[]{:S(2)}) copy-start(bf16[1024,192]{1,0:T(8,128)(2,1)} %copy-done.11) | copy-start | bytes 1179652
  482.3 167.1 %reduce-scatter.15.cloned.1.call-start = ((), (), s32[]{:S(2)}) async-start(), calls=%async_computation.13 | async-start | bytes 1474560 | tf_op jit(solution)/shard_map/reduce_scatter | solution.py:1192
  536.9 65.7 %copy-start.38 = (f32[768,3,192]{0,2,1:T(8,128)S(1)}, f32[768,3,192]{0,2,1:T(8,128)}, u32[]{:S(2)}) copy-start(f32[768,3,192]{0,2,1:T(8,128)} %broadcast_multiply_fusion) | copy-start | bytes 5308420
  618.7 70.8 %all-gather.14.cloned.1.call-start = ((), (), s32[]{:S(2)}) async-start(), calls=%async_computation.14 | async-start | bytes 5308416 | tf_op jit(solution)/shard_map/all_gather | solution.py:1194
  627.7 61.7 %copy-start.20 = (bf16[1024,576]{1,0:T(8,128)(2,1)S(1)}, bf16[1024,576]{1,0:T(8,128)(2,1)}, u32[]{:S(2)}) copy-start(bf16[1024,576]{1,0:T(8,128)(2,1)} %copy-done.19) | copy-start | bytes 3538948
  651.1 83.7 %reduce-scatter.17.cloned.1.call-start = ((), (), s32[]{:S(2)}) async-start(), calls=%async_computation.15 | async-start | bytes 1966080 | tf_op jit(solution)/shard_map/reduce_scatter | solution.py:1070
  693.2 74.3 %all-gather.18.cloned.1.call-start = ((), (), s32[]{:S(2)}) async-start(), calls=%async_computation.17 | async-start | bytes 1474560 | tf_op jit(solution)/shard_map/all_gather | solution.py:1208
  730.9 2.1 collective-permute-start
  736.8 30.6 %copy-start.47 = (f32[192,768]{1,0:T(8,128)S(1)}, f32[192,768]{1,0:T(8,128)}, u32[]{:S(2)}) copy-start(f32[192,768]{1,0:T(8,128)} %copy-done.46) | copy-start | bytes 1769476
  736.8 83.2 %all-gather.16.cloned.1.call-start = ((), (), s32[]{:S(2)}) async-start(), calls=%async_computation.16 | async-start | bytes 6856704 | tf_op jit(solution)/shard_map/all_gather | solution.py:1235
  781.7 12.8 %copy-start.65 = (f32[4,768]{1,0:T(4,128)S(1)}, f32[4,768]{1,0:T(4,128)}, u32[]{:S(2)}) copy-start(f32[4,768]{1,0:T(4,128)} %param.33) | copy-start | bytes 36868
  781.7 13.4 %copy-start.50 = (f32[256,768]{1,0:T(8,128)S(1)}, f32[256,768]{1,0:T(8,128)}, u32[]{:S(2)}) copy-start(f32[256,768]{1,0:T(8,128)} %get-tuple-element.134) | copy-start | bytes 2359300
  (70 other events, 254.4 us)
Sparse Core Ops, SparseCore 0:
  15.3 87.0 all-gather.7
  114.7 33.8 reduce-scatter.8
  151.4 81.5 reduce-scatter.6
  250.5 59.1 reduce-scatter.10
  389.4 37.0 all-gather.9
  440.4 32.8 reduce-scatter.12
  482.4 34.3 all-gather.11
  618.8 30.4 reduce-scatter.14
  651.8 37.6 all-gather.13
  693.3 35.2 reduce-scatter.16
  737.0 30.4 all-gather.17
  775.2 44.8 all-gather.15

commit v3 on v2

--- a/solution.py
+++ b/solution.py
@@ -222,7 +222,15 @@
     )
 
 
-def sum_small_kernel(
+def small_peers():
+    chips, chip, core, depth = place_of()
+    depths = lax.axis_size("tensor")
+    flat = [((lax.rem(chip + k, chips)) * 2 + core, depth) for k in range(1, chips)]
+    deep = [(chip * 2 + core, lax.rem(depth + k, depths)) for k in range(1, depths)]
+    return [(chip * 2 + 1 - core, depth)] + flat + deep
+
+
+def exchange_small(
     x_ref, out_ref, pair, plane, line, pair_sems, plane_sems, line_sems
 ):
     chips, chip, core, depth = place_of()
@@ -230,7 +238,6 @@
     sibling = (chip * 2 + 1 - core, depth)
     flat = [((lax.rem(chip + k, chips)) * 2 + core, depth) for k in range(1, chips)]
     deep = [(chip * 2 + core, lax.rem(depth + k, depths)) for k in range(1, depths)]
-    greet([sibling] + flat + deep)
     copy = send_to(x_ref, pair, pair_sems.at[0], pair_sems.at[1], sibling)
     copy.start()
     copy.wait()
@@ -267,6 +274,22 @@
     out_ref[...] = total
 
 
+def sum_small_kernel(*refs):
+    greet(small_peers())
+    exchange_small(*refs)
+
+
+def small_scratch(shape, chips, depths):
+    return [
+        pltpu.VMEM(shape, jnp.float32),
+        pltpu.VMEM((chips,) + shape, jnp.float32),
+        pltpu.VMEM((depths,) + shape, jnp.float32),
+        pltpu.SemaphoreType.DMA((2,)),
+        pltpu.SemaphoreType.DMA((2, chips)),
+        pltpu.SemaphoreType.DMA((2, depths)),
+    ]
+
+
 def sum_small(block, collective):
     chips, depths = lax.axis_size("dp") // 2, lax.axis_size("tensor")
     return pl.pallas_call(
@@ -274,14 +297,7 @@
         out_shape=jax.ShapeDtypeStruct(block.shape, jnp.float32),
         in_specs=[whole_vmem()],
         out_specs=whole_vmem(),
-        scratch_shapes=[
-            pltpu.VMEM(block.shape, jnp.float32),
-            pltpu.VMEM((chips,) + block.shape, jnp.float32),
-            pltpu.VMEM((depths,) + block.shape, jnp.float32),
-            pltpu.SemaphoreType.DMA((2,)),
-            pltpu.SemaphoreType.DMA((2, chips)),
-            pltpu.SemaphoreType.DMA((2, depths)),
-        ],
+        scratch_shapes=small_scratch(block.shape, chips, depths),
         compiler_params=pltpu.CompilerParams(
             collective_id=collective, has_side_effects=True, vmem_limit_bytes=16 * 2**20
         ),
@@ -319,12 +335,18 @@
     part_of = [
         pl.ds(pl.multiple_of(lax.rem(depth + k, depths) * part, 8), part) for k in range(depths)
     ]
+    halves = [slice(0, y_ref.shape[1] // 2), slice(y_ref.shape[1] // 2, y_ref.shape[1])]
     firsts, seconds = {}, {}
-    for k in range(1, depths):
-        firsts[k] = send_to(
-            y_ref.at[part_of[k]], line_in.at[k], line_sems.at[0, k], line_sems.at[1, k], deep[k]
-        )
-        firsts[k].start()
+    for c in range(2):
+        for k in range(1, depths):
+            firsts[c, k] = send_to(
+                y_ref.at[part_of[k], halves[c]],
+                line_in.at[k, :, halves[c]],
+                line_sems.at[c, 0, k],
+                line_sems.at[c, 1, k],
+                deep[k],
+            )
+            firsts[c, k].start()
     order = list(range(1, chips)) + [0]
     pair_copies, plane_copies = {}, {}
     for k in order:
@@ -344,44 +366,56 @@
                 pair_sum.at[k], plane_in.at[k], plane_sems.at[0, k], plane_sems.at[1, k], flat[k]
             )
             plane_copies[k].start()
-    value = y_ref[part_of[0]]
-    for k in range(1, depths):
-        firsts[k].wait_recv()
-        value = value + line_in[k]
-    line_out[part_of[0]] = value
-    for k in range(1, depths):
-        seconds[k] = send_to(
-            line_out.at[part_of[0]],
-            line_out.at[part_of[0]],
-            line_sems.at[2, k],
-            line_sems.at[3, k],
-            deep[k],
-        )
-        seconds[k].start()
+    for c in range(2):
+        value = y_ref[part_of[0], halves[c]]
+        for k in range(1, depths):
+            firsts[c, k].wait_recv()
+            value = value + line_in[k, :, halves[c]]
+        line_out[part_of[0], halves[c]] = value
+        for k in range(1, depths):
+            seconds[c, k] = send_to(
+                line_out.at[part_of[0], halves[c]],
+                line_out.at[part_of[0], halves[c]],
+                line_sems.at[c, 2, k],
+                line_sems.at[c, 3, k],
+                deep[k],
+            )
+            seconds[c, k].start()
     value = pair_sum[0]
     for k in range(1, chips):
         plane_copies[k].wait_recv()
         value = value + plane_in[k]
     total[...] = value
-    x_spread = start_spread(total, x_out, spread_sems.at[1], flat, rank)
+    x_spread = start_spread(total, x_out, spread_sems.at[2], flat, rank)
     x_out[rank] = value
-    for k in range(1, depths):
-        seconds[k].wait_recv()
-    y_spread = start_spread(line_out, y_out, spread_sems.at[0], flat, rank)
-    y_out[rank] = line_out[...]
-    x_share = start_share(x_out, x_spread, share_sems.at[1], (chips, chip, core), sibling)
-    y_share = start_share(y_out, y_spread, share_sems.at[0], (chips, chip, core), sibling)
+    y_spread, y_share = {}, {}
+    for c in range(2):
+        for k in range(1, depths):
+            seconds[c, k].wait_recv()
+        y_spread[c] = start_spread(
+            line_out, y_out, spread_sems.at[c], flat, rank, halves[c]
+        )
+        y_out[rank, :, halves[c]] = line_out[:, halves[c]]
+    place = (chips, chip, core)
+    x_share = start_share(x_out, x_spread, share_sems.at[2], place, sibling)
+    for c in range(2):
+        y_share[c] = start_share(
+            y_out, y_spread[c], share_sems.at[c], place, sibling, halves[c]
+        )
     for k in range(chips):
-        y_share[k].wait_recv()
         x_share[k].wait_recv()
+        y_share[0][k].wait_recv()
+        y_share[1][k].wait_recv()
     for copies in (
         pair_copies,
         plane_copies,
         firsts,
         seconds,
-        y_spread,
+        y_spread[0],
+        y_spread[1],
         x_spread,
-        y_share,
+        y_share[0],
+        y_share[1],
         x_share,
     ):
         for copy in copies.values():
@@ -410,9 +444,9 @@
             pltpu.VMEM(slab_y.shape, jnp.float32),
             pltpu.SemaphoreType.DMA((2, chips)),
             pltpu.SemaphoreType.DMA((2, chips)),
-            pltpu.SemaphoreType.DMA((4, depths)),
-            pltpu.SemaphoreType.DMA((2, 2, chips)),
-            pltpu.SemaphoreType.DMA((2, 2, chips)),
+            pltpu.SemaphoreType.DMA((2, 4, depths)),
+            pltpu.SemaphoreType.DMA((3, 2, chips)),
+            pltpu.SemaphoreType.DMA((3, 2, chips)),
         ],
         compiler_params=pltpu.CompilerParams(
             collective_id=collective, has_side_effects=True, vmem_limit_bytes=32 * 2**20
@@ -497,15 +531,17 @@
     )(rows.reshape((dp_count,) + slab))
 
 
-def start_spread(src, out_ref, sems, flat, rank):
+def start_spread(src, out_ref, sems, flat, rank, cols=slice(None)):
     copies = {}
     for k in range(1, len(flat)):
-        copies[k] = send_to(src, out_ref.at[rank], sems.at[0, k], sems.at[1, k], flat[k])
+        copies[k] = send_to(
+            src.at[:, cols], out_ref.at[rank, :, cols], sems.at[0, k], sems.at[1, k], flat[k]
+        )
         copies[k].start()
     return copies
 
 
-def start_share(out_ref, spread_copies, sems, place, sibling):
+def start_share(out_ref, spread_copies, sems, place, sibling, cols=slice(None)):
     chips, chip, core = place
     copies = {}
     for k in range(chips):
@@ -513,7 +549,11 @@
             spread_copies[k].wait_recv()
         held = lax.rem(chip + chips - k, chips) * 2 + core
         copies[k] = send_to(
-            out_ref.at[held], out_ref.at[held], sems.at[0, k], sems.at[1, k], sibling
+            out_ref.at[held, :, cols],
+            out_ref.at[held, :, cols],
+            sems.at[0, k],
+            sems.at[1, k],
+            sibling,
         )
         copies[k].start()
     return copies
@@ -558,31 +598,18 @@
     return full.reshape(dp_count * each, width)
 
 
-def line_gather_kernel(
-    x_ref, out_ref, right_send, right_recv, left_send, left_recv
+def line_gather_body(
+    small, x_ref, out_ref, right_send, right_recv, left_send, left_recv
 ):
     rank = lax.axis_index("dp")
     depth = lax.axis_index("tensor")
     depths = lax.axis_size("tensor")
     last = depths - 1
     right, left = (rank, depth + 1), (rank, depth - 1)
-    barrier = pltpu.get_barrier_semaphore()
-
-    @pl.when(depth < last)
-    def _():
-        pl.semaphore_signal(barrier, inc=1, device_id=right, device_id_type=MESH_ID)
-
-    @pl.when(depth > 0)
-    def _():
-        pl.semaphore_signal(barrier, inc=1, device_id=left, device_id_type=MESH_ID)
-
-    @pl.when((depth > 0) & (depth < last))
-    def _():
-        pl.semaphore_wait(barrier, 2)
-
-    @pl.when((depth == 0) | (depth == last))
-    def _():
-        pl.semaphore_wait(barrier, 1)
+    if small is None:
+        greet_line(depth, last, rank)
+    else:
+        greet(small_peers())
 
     def to_right(step):
         src = x_ref if step == 0 else out_ref.at[depth - step]
@@ -606,6 +633,8 @@
 
         if step == 0:
             out_ref[depth] = x_ref[...]
+            if small is not None:
+                exchange_small(*small)
 
         @pl.when(depth - 1 >= step)
         def _():
@@ -632,6 +661,40 @@
         @pl.when((depth > 0) & (depth + step <= last))
         def _():
             to_left(step).wait_send()
+
+
+def line_gather_kernel(x_ref, out_ref, *sems):
+    line_gather_body(None, x_ref, out_ref, *sems)
+
+
+def line_gather_small_kernel(
+    x_ref, y_ref, out_ref, small_ref, pair, plane, line, pair_sems, plane_sems, line_sems, *sems
+):
+    small = (y_ref, small_ref, pair, plane, line, pair_sems, plane_sems, line_sems)
+    line_gather_body(small, x_ref, out_ref, *sems)
+
+
+def line_gather_small(block, small, collective):
+    chips, depths = lax.axis_size("dp") // 2, lax.axis_size("tensor")
+    rows, width = block.shape
+    out, total = pl.pallas_call(
+        line_gather_small_kernel,
+        out_shape=(
+            jax.ShapeDtypeStruct((depths, rows, width), block.dtype),
+            jax.ShapeDtypeStruct(small.shape, jnp.float32),
+        ),
+        in_specs=[whole_vmem()] * 2,
+        out_specs=(whole_vmem(), whole_vmem()),
+        scratch_shapes=small_scratch(small.shape, chips, depths)
+        + [pltpu.SemaphoreType.DMA((depths,))] * 4,
+        compiler_params=pltpu.CompilerParams(
+            collective_id=collective, has_side_effects=True, vmem_limit_bytes=16 * 2**20
+        ),
+        cost_estimate=pl.CostEstimate(
+            flops=25 * 10**9, bytes_accessed=depths * rows * width * 4, transcendentals=0
+        ),
+    )(block, small)
+    return out.reshape(depths * rows, width), total
 
 
 def line_gather(block, collective):
@@ -653,11 +716,15 @@
     return out.reshape(depths * rows, width)
 
 
-def renew_kernel(widths, flips, gains, iterate_ref, *refs):
+def renew_kernel(widths, flips, gains, group_ref, map_ref, *refs):
     olds, news = refs[: len(widths)], refs[len(widths) :]
     keep_rate = 1.0 - MUON_RATE * MUON_DECAY
     offset = 0
+    total = group_ref.shape[1]
     for width, flip, gain, old, new in zip(widths, flips, gains, olds, news):
+        iterate_ref = group_ref
+        if offset == total:
+            iterate_ref, offset = map_ref, 0
         if flip:
             for first in range(0, width, 128):
                 size = min(128, width - first)
@@ -676,17 +743,17 @@
         offset += width
 
 
-def renew(iterate, olds, widths, flips, gains):
+def renew(iterate, map_iterate, olds, widths, flips, gains):
     return pl.pallas_call(
         functools.partial(renew_kernel, widths, flips, gains),
         out_shape=tuple(jax.ShapeDtypeStruct(old.shape, jnp.float32) for old in olds),
-        in_specs=[whole_vmem()] * (1 + len(olds)),
+        in_specs=[whole_vmem()] * (2 + len(olds)),
         out_specs=tuple(whole_vmem() for _ in olds),
         compiler_params=pltpu.CompilerParams(vmem_limit_bytes=48 * 2**20),
         cost_estimate=pl.CostEstimate(
             flops=10**9, bytes_accessed=iterate.size * 10, transcendentals=0
         ),
-    )(iterate, *olds)
+    )(iterate, map_iterate, *olds)
 
 
 HALF = 128
@@ -895,6 +962,285 @@
             transcendentals=4 * count * first.shape[1],
         ),
     )(block, first, second)
+
+
+def share_gram_kernel(
+    parts_ref, extra_ref, out_ref, line_in, pair_in, line_sems, pair_sems, plane_sems
+):
+    chips, chip, core, depth = place_of()
+    depths = lax.axis_size("tensor")
+    rank = chip * 2 + core
+    sibling = (chip * 2 + 1 - core, depth)
+    flat = [(lax.rem(chip + k, chips) * 2 + core, depth) for k in range(chips)]
+    line = [lax.rem(depth + k, depths) for k in range(depths)]
+    deep = [(rank, line[k]) for k in range(depths)]
+    greet([sibling] + flat[1:] + deep[1:])
+    copies = {}
+    for k in range(1, depths):
+        copies[k] = send_to(
+            parts_ref.at[line[k]], line_in.at[k], line_sems.at[0, k], line_sems.at[1, k], deep[k]
+        )
+        copies[k].start()
+    extra = send_to(extra_ref, out_ref.at[rank], pair_sems.at[0], pair_sems.at[1], sibling)
+    main = send_to(pair_in, out_ref.at[rank], pair_sems.at[2], pair_sems.at[3], sibling)
+    plane = {}
+    for k in range(1, chips):
+        plane[k] = [
+            send_to(
+                out_ref.at[chip * 2 + i],
+                out_ref.at[chip * 2 + i],
+                plane_sems.at[0, i, k],
+                plane_sems.at[1, i, k],
+                flat[k],
+            )
+            for i in range(2)
+        ]
+
+    @pl.when(core == 0)
+    def _():
+        extra.start()
+
+    @pl.when(core == 1)
+    def _():
+        out_ref[rank] = extra_ref[...]
+        extra.wait_recv()
+        for k in range(1, chips):
+            for i in range(2):
+                plane[k][i].start()
+
+    value = parts_ref[depth]
+    for k in range(1, depths):
+        copies[k].wait_recv()
+        value = value + line_in[k]
+
+    @pl.when(core == 1)
+    def _():
+        pair_in[...] = value
+        main.start()
+
+    @pl.when(core == 0)
+    def _():
+        out_ref[rank] = value
+        main.wait_recv()
+        for k in range(1, chips):
+            for i in range(2):
+                plane[k][i].start()
+
+    for k in range(1, chips):
+        for i in range(2):
+            plane[k][i].wait_recv()
+    for k in range(1, chips):
+        for i in range(2):
+            plane[k][i].wait_send()
+    for k in range(1, depths):
+        copies[k].wait_send()
+
+    @pl.when(core == 0)
+    def _():
+        extra.wait_send()
+
+    @pl.when(core == 1)
+    def _():
+        main.wait_send()
+
+
+def share_gram(parts, extra, collective):
+    dp_count, depths = lax.axis_size("dp"), lax.axis_size("tensor")
+    chips = dp_count // 2
+    slab = extra.shape
+    out = pl.pallas_call(
+        share_gram_kernel,
+        out_shape=jax.ShapeDtypeStruct((dp_count,) + slab, jnp.float32),
+        in_specs=[whole_vmem()] * 2,
+        out_specs=whole_vmem(),
+        scratch_shapes=[
+            pltpu.VMEM((depths,) + slab, jnp.float32),
+            pltpu.VMEM(slab, jnp.float32),
+            pltpu.SemaphoreType.DMA((2, depths)),
+            pltpu.SemaphoreType.DMA((4,)),
+            pltpu.SemaphoreType.DMA((2, 2, chips)),
+        ],
+        compiler_params=pltpu.CompilerParams(
+            collective_id=collective, has_side_effects=True, vmem_limit_bytes=16 * 2**20
+        ),
+        cost_estimate=pl.CostEstimate(
+            flops=45 * 10**9, bytes_accessed=dp_count * slab[0] * slab[1] * 8, transcendentals=0
+        ),
+    )(parts.reshape((depths,) + slab), extra)
+    return out.reshape(dp_count * slab[0], slab[1])
+
+
+def line_exchange_kernel(
+    heads_ref,
+    weight_ref,
+    x_ref,
+    sum_ref,
+    all_ref,
+    y_ref,
+    from_left,
+    from_right,
+    stage,
+    right_sems,
+    left_sems,
+    row_sems,
+    sum_sems,
+    from_left_sems,
+    from_right_sems,
+):
+    rank = lax.axis_index("dp")
+    depth = lax.axis_index("tensor")
+    last = lax.axis_size("tensor") - 1
+    right, left = (rank, depth + 1), (rank, depth - 1)
+    greet_line(depth, last, rank)
+
+    def rows_right(j):
+        return send_to(all_ref.at[j], all_ref.at[j], right_sems.at[j], row_sems.at[j], right)
+
+    def rows_left(j):
+        return send_to(all_ref.at[j], all_ref.at[j], left_sems.at[j], row_sems.at[j], left)
+
+    def sum_right(j, h, src):
+        return send_to(
+            src.at[j, h], from_left.at[j, h], sum_sems.at[j, h], from_left_sems.at[j, h], right
+        )
+
+    def sum_left(j, h, src):
+        return send_to(
+            src.at[j, h], from_right.at[j, h], sum_sems.at[j, h], from_right_sems.at[j, h], left
+        )
+
+    all_ref[depth] = x_ref[...]
+
+    @pl.when(depth < last)
+    def _():
+        rows_right(depth).start()
+
+    @pl.when(depth > 0)
+    def _():
+        rows_left(depth).start()
+
+    for j in range(4):
+        for h in range(2):
+            first = (2 * j + h) * HALF
+            y_ref[j, h] = plain_dot(
+                heads_ref[first : first + HALF, :], weight_ref[...]
+            ).astype(jnp.bfloat16)
+
+    @pl.when(depth == 0)
+    def _():
+        for j in (3, 2, 1):
+            for h in range(2):
+                sum_right(j, h, y_ref).start()
+        for j in (1, 2, 3):
+            rows_left(j).wait_recv()
+
+    @pl.when(depth == last)
+    def _():
+        for j in (0, 1, 2):
+            for h in range(2):
+                sum_left(j, h, y_ref).start()
+        for j in (2, 1, 0):
+            rows_right(j).wait_recv()
+
+    def relay_right(j):
+        for h in range(2):
+            sum_right(j, h, stage).wait_recv()
+            stage[j, h] = (
+                y_ref[j, h].astype(jnp.float32) + from_left[j, h].astype(jnp.float32)
+            ).astype(jnp.bfloat16)
+            sum_right(j, h, stage).start()
+
+    def relay_left(j):
+        for h in range(2):
+            sum_left(j, h, stage).wait_recv()
+            stage[j, h] = (
+                y_ref[j, h].astype(jnp.float32) + from_right[j, h].astype(jnp.float32)
+            ).astype(jnp.bfloat16)
+            sum_left(j, h, stage).start()
+
+    def pass_right(j):
+        rows_right(j).wait_recv()
+        rows_right(j).start()
+
+    def pass_left(j):
+        rows_left(j).wait_recv()
+        rows_left(j).start()
+
+    @pl.when(depth == 1)
+    def _():
+        pass_left(2)
+        pass_right(0)
+        relay_right(3)
+        pass_left(3)
+        relay_left(0)
+        relay_right(2)
+
+    @pl.when(depth == 2)
+    def _():
+        pass_right(1)
+        pass_left(3)
+        relay_left(0)
+        pass_right(0)
+        relay_right(3)
+        relay_left(1)
+
+    for h in range(2):
+        span = slice(h * HALF, (h + 1) * HALF)
+        sum_ref[span, :] = y_ref[depth, h].astype(jnp.float32)
+
+        @pl.when(depth > 0)
+        def _():
+            sum_right(depth, h, stage).wait_recv()
+            sum_ref[span, :] += from_left[depth, h].astype(jnp.float32)
+
+        @pl.when(depth < last)
+        def _():
+            sum_left(depth, h, stage).wait_recv()
+            sum_ref[span, :] += from_right[depth, h].astype(jnp.float32)
+
+    for j in range(4):
+
+        @pl.when((depth >= j) & (depth < last))
+        def _():
+            rows_right(j).wait_send()
+
+        @pl.when((depth <= j) & (depth > 0))
+        def _():
+            rows_left(j).wait_send()
+
+        for h in range(2):
+
+            @pl.when(depth < j)
+            def _():
+                sum_right(j, h, stage).wait_send()
+
+            @pl.when(depth > j)
+            def _():
+                sum_left(j, h, stage).wait_send()
+
+
+def line_exchange(heads, weight, block, collective):
+    width = weight.shape[1]
+    slots = (4, 2, HALF, width)
+    total, rows = pl.pallas_call(
+        line_exchange_kernel,
+        out_shape=(
+            jax.ShapeDtypeStruct((2 * HALF, width), jnp.float32),
+            jax.ShapeDtypeStruct((4,) + block.shape, block.dtype),
+        ),
+        in_specs=[whole_vmem()] * 3,
+        out_specs=(whole_vmem(), whole_vmem()),
+        scratch_shapes=[pltpu.VMEM(slots, jnp.bfloat16)] * 4
+        + [pltpu.SemaphoreType.DMA((4,))] * 3
+        + [pltpu.SemaphoreType.DMA((4, 2))] * 3,
+        compiler_params=pltpu.CompilerParams(
+            collective_id=collective, has_side_effects=True, vmem_limit_bytes=32 * 2**20
+        ),
+        cost_estimate=pl.CostEstimate(
+            flops=60 * 10**9, bytes_accessed=heads.size * 16, transcendentals=0
+        ),
+    )(heads, weight, block)
+    return total, rows.reshape(-1, block.shape[1])
 
 
 NBLK = 256
@@ -1048,20 +1394,10 @@
     seq_count = replay.shape[0]
     total_rows = row_count * groups
     count_block = jnp.full((8, 128), jnp.sum(resp_mask), jnp.int32).astype(jnp.float32)
-    count_val = sum_small(count_block, 0)[0, 0]
     tokens_all = lax.axis_size("dp") * seq_count * LEN
-    factor = tokens_all / (2.0 * count_val)
 
     def teacher_gather(local_rows):
         return lax.all_gather(local_rows, "tensor", axis=0, tiled=True)
-
-    def teacher_reduce(left, right):
-        return lax.psum_scatter(
-            jnp.dot(left, right, preferred_element_type=jnp.float32).astype(jnp.bfloat16),
-            "tensor",
-            scatter_dimension=0,
-            tiled=True,
-        ).astype(jnp.float32)
 
     def student_gather(local_rows):
         return lax.all_gather(local_rows, "tensor", axis=0, tiled=True)
@@ -1083,12 +1419,6 @@
     live_slots = (jnp.arange(slot_count, dtype=jnp.int32) < live_count).astype(jnp.float32)
     teacher_normed = norm_parts(teacher_x, t_gains[0], t_shifts[0])[0].astype(jnp.bfloat16)
     teacher_all = teacher_gather(teacher_normed)
-    teacher_mixed = jnp.dot(
-        teacher_all, t_qkv.reshape(DT, 3 * slot_width), preferred_element_type=jnp.float32
-    ).astype(jnp.bfloat16)
-    teacher_head_out = attend_forward(teacher_mixed, slot_count)[0]
-    slot_mask = jnp.repeat(live_slots, HEAD)[None, :] > 0.0
-    teacher_head_out = jnp.where(slot_mask, teacher_head_out, jnp.zeros_like(teacher_head_out))
     student_x = student_in.astype(jnp.float32)
     shard_width = s_qkv.shape[2]
     shard_hidden = s_fc.shape[1]
@@ -1100,15 +1430,22 @@
     w_map = s_map.astype(jnp.bfloat16)
     normed_one, unit_one, scale_one = norm_parts(student_x, s_norms[0], s_norms[1])
     low_one = normed_one.astype(jnp.bfloat16)
-    rows_one = line_gather(low_one, 5)
+    rows_one, count_sum = line_gather_small(low_one, count_block, 5)
+    count_val = count_sum[0, 0]
+    factor = tokens_all / (2.0 * count_val)
     mixed_qkv = jnp.dot(rows_one, w_qkv, preferred_element_type=jnp.float32).astype(jnp.bfloat16)
     head_out, log_sums = attend_forward(mixed_qkv, head_count)
+    teacher_all, head_out = lax.optimization_barrier((teacher_all, head_out))
     resid = student_x + student_reduce(head_out, w_out, 0)
+    teacher_mixed = jnp.dot(
+        teacher_all, t_qkv.reshape(DT, 3 * slot_width), preferred_element_type=jnp.float32
+    ).astype(jnp.bfloat16)
+    teacher_head_out = attend_forward(teacher_mixed, slot_count)[0]
+    slot_mask = jnp.repeat(live_slots, HEAD)[None, :] > 0.0
+    teacher_head_out = jnp.where(slot_mask, teacher_head_out, jnp.zeros_like(teacher_head_out))
     normed_two, unit_two, scale_two = norm_parts(resid, s_norms[2], s_norms[3])
     low_two = normed_two.astype(jnp.bfloat16)
-    rows_two = line_gather(low_two, 6)
-    attn_part = teacher_reduce(teacher_head_out, t_out)
-    attn_part, rows_two = lax.optimization_barrier((attn_part, rows_two))
+    attn_part, rows_two = line_exchange(teacher_head_out, t_out, low_two, 6)
     teacher_resid = teacher_x + attn_part
     teacher_normed_two = norm_parts(teacher_resid, t_gains[1], t_shifts[1])[0].astype(jnp.bfloat16)
     mlp_part = line_mlp(teacher_normed_two, t_fc, t_proj, 8)
@@ -1189,13 +1526,11 @@
         )
 
     parts = jnp.concatenate([gram_rows(talls[i], sums[i]) for i in range(4)], axis=0)
-    own_rows = lax.psum_scatter(parts, "tensor", scatter_dimension=0, tiled=True)
-    both_rows = jnp.concatenate([own_rows[None], gram_rows(talls[4], sums[4])[None]], axis=0)
-    both_rows = lax.all_gather(both_rows, "dp", axis=1, tiled=True)
-    both_rows, grad_mixed = lax.optimization_barrier((both_rows, grad_mixed))
+    gram_mat = share_gram(parts, gram_rows(talls[4], sums[4]), 9)
+    gram_mat, grad_mixed = lax.optimization_barrier((gram_mat, grad_mixed))
     grad_normed_one = student_reduce(grad_mixed, w_qkv, 1)
     mine = dp_rank % 2
-    factor_mat = orthogonal_factor(jnp.where(mine == 0, both_rows[0], both_rows[1]))
+    factor_mat = orthogonal_factor(gram_mat)
     pair_rows = lax.dynamic_slice_in_dim(factor_mat, (dp_rank // 2) * 2 * slice_rows, 2 * slice_rows, 0)
     other_rows = lax.ppermute(
         pair_rows, "dp", [(i, i ^ 1) for i in range(dp_count)]
@@ -1205,7 +1540,7 @@
     even_rows = lax.dynamic_slice_in_dim(even_rows, mine * slice_rows, slice_rows, 0)
     odd_rows = lax.dynamic_slice_in_dim(odd_rows, mine * slice_rows, slice_rows, 0)
     even_rows, grad_normed_one = lax.optimization_barrier((even_rows, grad_normed_one))
-    factor_rows = lax.all_gather(even_rows, "tensor", axis=0)
+    factor_rows = line_gather(even_rows, 10).reshape(groups, slice_rows, DS)
     input_grad = grad_resid + norm_back(grad_normed_one, unit_one, scale_one, s_norms[0])
     norm_grads = jnp.stack(
         [
@@ -1222,21 +1557,23 @@
     norm_grads = small[:4]
     loss = small[4, 0] / (count_val * DT)
 
-    pieces = [
-        lax.dot_general(
-            factor_rows[i] if i < 4 else odd_rows,
-            talls[i],
-            (((1,), (1 - sums[i],)), ((), ())),
+    def piece_of(index, rows):
+        return lax.dot_general(
+            rows,
+            talls[index],
+            (((1,), (1 - sums[index],)), ((), ())),
             precision=lax.Precision.HIGH,
             preferred_element_type=jnp.float32,
         ).astype(jnp.bfloat16)
-        for i in (2, 3, 1, 0, 4)
-    ]
+
+    map_all = lax.all_gather(piece_of(4, odd_rows), "dp", axis=0, tiled=True)
+    pieces = [piece_of(i, factor_rows[i]) for i in (2, 3, 1, 0)]
     iterate_all = lax.all_gather(jnp.concatenate(pieces, axis=1), "dp", axis=0, tiled=True)
     weight_fc, weight_proj, weight_out, weight_qkv, weight_map = renew(
         iterate_all,
+        map_all,
         (s_fc, s_proj, s_out, to_tall(s_qkv), s_map.T),
-        [piece.shape[1] for piece in pieces],
+        [piece.shape[1] for piece in pieces] + [DT],
         [False, True, True, True, True],
         [math.sqrt(FS / DS), 1.0, 1.0, math.sqrt(3.0), math.sqrt(DT / DS)],
     )

time: 852 us -> 788 us (0.925)
  waiting for transfers between devices: 108 us -> 17.6 us
  Pallas kernels: 543 us -> 600 us
  other arithmetic: 51.9 us -> 37 us
  local copies, waits for them, and re-layouts: 43.9 us -> 31.4 us
  starting transfers between devices: 2.02 us -> 11.3 us
    pallas_call x0 -> x3, Pallas kernels: none -> 191 us  [the longest x1 86.7 us: line_gather_small(): pl.pallas_call(line_gather_small_kernel, out_shape=(jax.ShapeDtypeStruct(...]
    pallas_call x2 -> x1, Pallas kernels: 154 us -> 32.5 us  [line_gather(): pl.pallas_call(line_gather_kernel, out_shape=jax.ShapeDtypeStruct((depths...]
    all_gather x2 -> x1, waiting for transfers between devices: 63.8 us -> 0.01 us  [body(): map_all = lax.all_gather(piece_of(4, odd_rows), 'dp', axis=0, tiled=True)]
    reduce_scatter x2 -> x0, waiting for transfers between devices: 18.4 us -> none  [the longest x1 18.4 us: body(): lax.psum_scatter(parts, 'tensor', scatter_dimension=0, tiled=True)]
    unnamed x180 -> x164, local copies, waits for them, and re-layouts: 31.6 us -> 20.4 us
    pallas_call x2 -> x1, Pallas kernels: 22.2 us -> 11.4 us  [sum_small(): pl.pallas_call(sum_small_kernel, out_shape=jax.ShapeDtypeStruct(block.sha...]
    reduce_scatter x4, starting transfers between devices: 0.38 us -> 11 us  [student_reduce(): lax.psum_scatter(lax.dot_general(left, right, (((1,), (right_dim,)), ((),...]
    all_gather x1, waiting for transfers between devices: 23.7 us -> 13.3 us  [body(): lax.all_gather(jnp.concatenate(pieces, axis=1), 'dp', axis=0, tiled=True)]
  transfers between devices with their start and end apart: 13 -> 10, of which waited for: 6 -> 3; matrix products, arithmetic and copies ran while one was open for 8% -> 7% of each run, Pallas kernels for 54% -> 52%
where the time goes in v3:
time: 788 us; the launch traced here: 785 us
  Pallas kernels  600 us (76%)
  matrix products  67.6 us (9%)
  other arithmetic  37 us (5%)
  local copies, waits for them, and re-layouts  31.4 us (4%)
  between operations  20.1 us (3%)
  waiting for transfers between devices  17.6 us (2%)
  starting transfers between devices  11.3 us (1%)
    pallas_call x1, Pallas kernels, line_mlp(): pl.pallas_call(line_mlp_kernel, out_shape=jax.ShapeDtypeStruct((count, wi...  126 us
    pallas_call x1, Pallas kernels, line_gather_small(): pl.pallas_call(line_gather_small_kernel, out_shape=(jax.ShapeDtypeStruct(...  86.7 us
    pallas_call x2, Pallas kernels, scatter_rows(): pl.pallas_call(scatter_rows_kernel, out_shape=jax.ShapeDtypeStruct(slab,...  67.2 us
    pallas_call x1, Pallas kernels, sum_and_spread(): pl.pallas_call(sum_and_spread_kernel, out_shape=(jax.ShapeDtypeStruct((dp...  65 us
    pallas_call x1, Pallas kernels, line_exchange(): pl.pallas_call(line_exchange_kernel, out_shape=(jax.ShapeDtypeStruct((2 *...  62.8 us
    pallas_call x1, Pallas kernels, share_gram(): pl.pallas_call(share_gram_kernel, out_shape=jax.ShapeDtypeStruct((dp_coun...  41.7 us
    pallas_call x1, Pallas kernels, orthogonal_factor(): pl.pallas_call(polynomial_kernel, out_shape=jax.ShapeDtypeStruct((size, s...  33.4 us
    pallas_call x1, Pallas kernels, line_gather(): pl.pallas_call(line_gather_kernel, out_shape=jax.ShapeDtypeStruct((depths...  32.5 us
  transfers between devices with their start and end apart: 10, of which 3 were waited for; matrix products, arithmetic and copies ran while one was open for 7% of the time, Pallas kernels for 52%

profile of v3, /device:TPU:0, one launch (start us, length us, event | category | flops | bytes accessed | tf_op | source)
XLA Modules:
  0.0 784.7 jit_solution(3170378860000354513)
XLA Ops:
  13.1 86.7 %shard_map.390 = (bf16[4,256,768]{2,1,0:T(8,128)(2,1)S(1)}, f32[8,128]{1,0:T(8,128)S(1)}) custom-call(bf16[256,768]{1,0:T(8,128)(2,1)S(1)} %fusion.26.x_ref, f32[8,128]{1,0:T(8,128)S(1)} %broadcast_in_dim.18.y_ref), custom_call_target="tpu_custom_call" | custom-call | flops 24999999488 | bytes 3145728 | tf_op jit(solution)/shard_map/pallas_call | solution.py:680
  102.4 6.4 shard_map.391
  111.7 10.4 %reduce-scatter.7.cloned.1.call-start = ((), (), s32[]{:S(2)}) async-start(), calls=%async_computation.6 | async-start | bytes 1966080 | tf_op jit(solution)/shard_map/reduce_scatter | solution.py:1406
  124.2 3.0 broadcast_multiply_fusion
  127.2 8.8 %convolution_convert_fusion = bf16[1024,1344]{0,1:T(8,128)(2,1)} fusion(bf16[1024,1600]{1,0:T(8,128)(2,1)S(1)} %copy-done.72, bf16[1600,1344]{0,1:T(8,128)(2,1)} %bitcast.116), kind=kOutput, calls=%fused_computation.7 | convolution fusion | flops 4405395456 | bytes 10330112 | tf_op jit(solution)/shard_map/dot_general | solution.py:1440
  136.0 3.3 copy.53.qkv_ref
  139.3 15.7 %shard_map.392 = (bf16[1024,448]{1,0:T(8,128)(2,1)S(1)}, f32[1024,128]{1,0:T(8,128)}) custom-call(bf16[1024,1344]{1,0:T(8,128)(2,1)S(1)} %copy.53.qkv_ref), custom_call_target="tpu_custom_call" | custom-call | flops 7516192768 | bytes 3670016 | tf_op jit(solution)/shard_map/pallas_call | solution.py:114
  161.1 62.8 %shard_map.393 = (f32[256,1600]{1,0:T(8,128)S(1)}, bf16[4,256,768]{2,1,0:T(8,128)(2,1)S(1)}) custom-call(bf16[1024,448]{1,0:T(8,128)(2,1)S(1)} %broadcast_select_fusion.heads_ref, bf16[448,1600]{1,0:T(8,128)(2,1)S(1)} %copy-done.11, bf16[256,768]{1,0:T(8,128)(2,1)S(1)} %add_convert_fusion.3.x_ref), custom_call_target="tpu_custom_call" | custom-call | flops 60000002048 | bytes 7340032 | tf_op jit(solution)/shard_map/pallas_call | solution.py:1225
  227.0 3.1 convolution_convert_fusion.4
  231.3 125.9 %shard_map.394 = f32[256,1600]{1,0:T(8,128)S(1)} custom-call(bf16[256,1600]{1,0:T(8,128)(2,1)S(1)} %add_convert_fusion.1.x_ref, bf16[1600,1600]{1,0:T(8,128)(2,1)} %first_ref.1, bf16[1600,1600]{1,0:T(8,128)(2,1)} %second_ref.1), custom_call_target="tpu_custom_call" | custom-call | flops 41943040000 | bytes 6553600 | tf_op jit(solution)/shard_map/pallas_call | solution.py:943
  359.8 4.4 fusion.13
  364.2 3.2 fusion.76
  369.6 2.8 concatenate.18
  372.4 34.9 %shard_map.395.y_ref = f32[224,768]{1,0:T(8,128)S(1)} custom-call(f32[8,224,768]{2,1,0:T(8,128)S(1)} %bitcast.91), custom_call_target="tpu_custom_call" | custom-call | flops 26880000000 | bytes 5505024 | tf_op jit(solution)/shard_map/pallas_call | solution.py:511
  408.1 6.6 fusion.3
  415.8 2.6 convolution_convert_fusion.3
  418.5 3.5 fusion.82
  424.2 32.4 %shard_map.396.x_ref = f32[192,768]{1,0:T(8,128)S(1)} custom-call(f32[8,192,768]{2,1,0:T(8,128)S(1)} %bitcast.92), custom_call_target="tpu_custom_call" | custom-call | flops 23040000000 | bytes 4718592 | tf_op jit(solution)/shard_map/pallas_call | solution.py:511
  460.5 31.4 %shard_map.397 = f32[8,192,768]{2,1,0:T(8,128)S(1)} custom-call(f32[192,768]{1,0:T(8,128)S(1)} %shard_map.396.x_ref), custom_call_target="tpu_custom_call" | custom-call | flops 35000000512 | bytes 4718592 | tf_op jit(solution)/shard_map/pallas_call | solution.py:582
  499.8 8.9 %shard_map.398 = bf16[1024,576]{1,0:T(8,128)(2,1)S(1)} custom-call(bf16[1024,576]{1,0:T(8,128)(2,1)S(1)} %copy-done.18, f32[1024,128]{1,0:T(8,128)S(1)} %get-tuple-element.60.log_ref, bf16[1024,192]{1,0:T(8,128)(2,1)S(1)} %copy.55.grad_ref), custom_call_target="tpu_custom_call" | custom-call | flops 8053063680 | bytes 3145728 | tf_op jit(solution)/shard_map/pallas_call | solution.py:183
  511.0 65.0 %shard_map.399 = (f32[8,96,768]{2,1,0:T(8,128)S(1)}, f32[8,224,768]{2,1,0:T(8,128)S(1)}) custom-call(f32[8,96,768]{2,1,0:T(8,128)S(1)} %bitcast.97, f32[224,768]{1,0:T(8,128)S(1)} %copy-done.20), custom_call_target="tpu_custom_call" | custom-call | flops 60000002048 | bytes 9437184 | tf_op jit(solution)/shard_map/pallas_call | solution.py:430
  579.2 5.3 slice_bitcast_fusion
  584.5 3.2 fusion.23.extra_ref
  589.7 5.2 multiply_add_fusion.3
  599.1 41.7 %shard_map.400 = f32[8,96,768]{2,1,0:T(8,128)S(1)} custom-call(f32[4,96,768]{2,1,0:T(8,128)S(1)} %bitcast.98, f32[96,768]{1,0:T(8,128)S(1)} %fusion.23.extra_ref), custom_call_target="tpu_custom_call" | custom-call | flops 44999999488 | bytes 4718592 | tf_op jit(solution)/shard_map/pallas_call | solution.py:1051
  646.7 33.4 %shard_map.401 = f32[768,768]{1,0:T(8,128)S(1)} custom-call(f32[768,768]{1,0:T(8,128)S(1)} %bitcast.99), custom_call_target="tpu_custom_call" | custom-call | flops 30802968576 | bytes 4718592 | tf_op jit(solution)/shard_map/pallas_call | solution.py:1340
  683.1 5.4 convolution_convert_fusion.1
  689.7 32.5 %shard_map.403 = f32[4,96,768]{2,1,0:T(8,128)S(1)} custom-call(f32[96,768]{1,0:T(8,128)S(1)} %dynamic-slice_select_fusion.x_ref), custom_call_target="tpu_custom_call" | custom-call | flops 24999999488 | bytes 1179648 | tf_op jit(solution)/shard_map/pallas_call | solution.py:703
  731.8 2.9 fusion.8
  736.5 11.4 %shard_map.402 = f32[8,768]{1,0:T(8,128)S(1)} custom-call(f32[8,768]{1,0:T(8,128)S(1)} %concatenate.22.refs_0_), custom_call_target="tpu_custom_call" | custom-call | flops 10000000000 | bytes 1000000 | tf_op jit(solution)/shard_map/pallas_call | solution.py:295
  751.1 13.3 %all-gather.12.cloned.1.call-done.group_ref = bf16[768,2304]{1,0:T(8,128)(2,1)} async-done(((bf16[96,2304]{1,0:T(8,128)(2,1)}), bf16[768,2304]{1,0:T(8,128)(2,1)}) %all-gather.12.cloned.1.call-update) | async-done | bytes 3538960 | tf_op jit(solution)/shard_map/all_gather | solution.py:1571
  766.1 10.7 %shard_map.404 = (f32[768,768]{1,0:T(8,128)}, f32[768,768]{1,0:T(8,128)}, f32[192,768]{1,0:T(8,128)}, f32[576,768]{1,0:T(8,128)}, f32[1600,768]{1,0:T(8,128)}) custom-call(bf16[768,2304]{1,0:T(8,128)(2,1)} %all-gather.12.cloned.1.call-done.group_ref, bf16[768,1600]{1,0:T(8,128)(2,1)} %all-gather.14.cloned.1.call-done.map_ref, f32[768,768]{1,0:T(8,128)S(1)} %copy-done.8, ...), custom_call_target="tpu_custom_call" | custom-call | flops 1000000000 | bytes 17694720 | tf_op jit(solution)/shard_map/pallas_call | solution.py:747
  (272 shorter events, 78.1 us)
Async XLA Ops:
  7.2 102.7 %all-gather.6.cloned.1.call-start = ((), (), s32[]{:S(2)}) async-start(), calls=%async_computation.4 | async-start | bytes 4259840 | tf_op jit(solution)/shard_map/all_gather | solution.py:1400
  10.8 144.2 %reduce-scatter.5.cloned.1.call-start = ((), (), s32[]{:S(2)}) async-start(), calls=%async_computation.5 | async-start | bytes 1966080 | tf_op jit(solution)/shard_map/reduce_scatter | solution.py:1406
  12.3 87.6 %copy-start.47 = (bf16[768,3,192]{0,2,1:T(8,128)(2,1)}, bf16[768,3,192]{0,2,1:T(8,128)(2,1)S(1)}, u32[]{:S(2)}) copy-start(bf16[768,3,192]{0,2,1:T(8,128)(2,1)S(1)} %convert_element_type.128) | copy-start | bytes 2654212
  12.4 146.1 %copy-start.52 = (f32[768]{0:T(1024)}, f32[768]{0:T(1024)S(1)}, u32[]{:S(2)}) copy-start(f32[768]{0:T(1024)S(1)} %get-tuple-element.130) | copy-start | bytes 9220
  12.5 87.3 %copy-start.56 = (f32[256]{0:T(256)}, f32[256]{0:T(256)S(1)}, u32[]{:S(2)}) copy-start(f32[256]{0:T(256)S(1)} %broadcast_multiply_fusion.7) | copy-start | bytes 3076
  12.8 87.0 %copy-start.60 = (f32[256]{0:T(256)}, f32[256]{0:T(256)S(1)}, u32[]{:S(2)}) copy-start(f32[256]{0:T(256)S(1)} %add_rsqrt_fusion.2) | copy-start | bytes 3076
  109.9 17.3 %copy-start.9 = (bf16[1024,192]{1,0:T(8,128)(2,1)}, bf16[1024,192]{1,0:T(8,128)(2,1)S(1)}, u32[]{:S(2)}) copy-start(bf16[1024,192]{1,0:T(8,128)(2,1)S(1)} %get-tuple-element.52) | copy-start | bytes 1179652
  111.7 246.7 %reduce-scatter.7.cloned.1.call-start = ((), (), s32[]{:S(2)}) async-start(), calls=%async_computation.6 | async-start | bytes 1966080 | tf_op jit(solution)/shard_map/reduce_scatter | solution.py:1406
  157.2 66.7 %copy-start.58 = (f32[256]{0:T(256)}, f32[256]{0:T(256)S(1)}, u32[]{:S(2)}) copy-start(f32[256]{0:T(256)S(1)} %broadcast_multiply_fusion.6) | copy-start | bytes 3076
  158.4 65.4 %copy-start.62 = (f32[256]{0:T(256)}, f32[256]{0:T(256)S(1)}, u32[]{:S(2)}) copy-start(f32[256]{0:T(256)S(1)} %add_rsqrt_fusion.1) | copy-start | bytes 3076
  161.1 62.8 %copy-start.6 = (f32[768,768]{1,0:T(8,128)S(1)}, f32[768,768]{1,0:T(8,128)}, u32[]{:S(2)}) copy-start(f32[768,768]{1,0:T(8,128)} %refs_0_.1) | copy-start | bytes 7077892
  230.2 177.9 %all-gather.8.cloned.1.call-start = ((), (), s32[]{:S(2)}) async-start(), calls=%async_computation.7 | async-start | bytes 1966080 | tf_op jit(solution)/shard_map/all_gather | solution.py:1403
  369.4 87.2 %reduce-scatter.9.cloned.1.call-start = ((), (), s32[]{:S(2)}) async-start(), calls=%async_computation.8 | async-start | bytes 1966080 | tf_op jit(solution)/shard_map/reduce_scatter | solution.py:1406
  418.4 77.6 %all-gather.10.cloned.1.call-start = ((), (), s32[]{:S(2)}) async-start(), calls=%async_computation.9 | async-start | bytes 1966080 | tf_op jit(solution)/shard_map/all_gather | solution.py:1403
  424.2 33.6 %copy-start.25 = (bf16[256,768]{1,0:T(8,128)(2,1)S(1)}, bf16[256,768]{1,0:T(8,128)(2,1)}, u32[]{:S(2)}) copy-start(bf16[256,768]{1,0:T(8,128)(2,1)} %param.24) | copy-start | bytes 1179652
  424.2 33.6 %copy-start.35 = (bf16[256,768]{1,0:T(8,128)(2,1)S(1)}, bf16[256,768]{1,0:T(8,128)(2,1)}, u32[]{:S(2)}) copy-start(bf16[256,768]{1,0:T(8,128)(2,1)} %reduce-scatter.5.cloned.1.call-done) | copy-start | bytes 1179652
  424.2 33.6 %copy-start.53 = (f32[768]{0:T(1024)S(1)}, f32[768]{0:T(1024)}, u32[]{:S(2)}) copy-start(f32[768]{0:T(1024)} %copy-done.52) | copy-start | bytes 9220
  424.2 33.6 %copy-start.59 = (f32[256]{0:T(256)S(1)}, f32[256]{0:T(256)}, u32[]{:S(2)}) copy-start(f32[256]{0:T(256)} %copy-done.58) | copy-start | bytes 3076
  424.2 33.6 %copy-start.63 = (f32[256]{0:T(256)S(1)}, f32[256]{0:T(256)}, u32[]{:S(2)}) copy-start(f32[256]{0:T(256)} %copy-done.62) | copy-start | bytes 3076
  460.2 35.8 %copy-start.3 = (f32[192,768]{1,0:T(8,128)S(1)}, f32[192,768]{1,0:T(8,128)}, u32[]{:S(2)}) copy-start(f32[192,768]{1,0:T(8,128)} %refs_2_.1) | copy-start | bytes 1769476
  460.2 228.5 %reduce-scatter.11.cloned.1.call-start = ((), (), s32[]{:S(2)}) async-start(), calls=%async_computation.10 | async-start | bytes 1966080 | tf_op jit(solution)/shard_map/reduce_scatter | solution.py:1406
  511.0 65.1 %copy-start.32 = (f32[768,3,192]{0,2,1:T(8,128)S(1)}, f32[768,3,192]{0,2,1:T(8,128)}, u32[]{:S(2)}) copy-start(f32[768,3,192]{0,2,1:T(8,128)} %broadcast_multiply_fusion) | copy-start | bytes 5308420
  576.1 13.0 %copy-start.46 = (f32[2,96,768]{2,1,0:T(8,128)}, f32[2,96,768]{2,1,0:T(8,128)S(1)}, u32[]{:S(2)}) copy-start(f32[2,96,768]{2,1,0:T(8,128)S(1)} %slice.79) | copy-start | bytes 1769476
  599.1 43.1 %copy-start.48 = (bf16[768,3,192]{0,2,1:T(8,128)(2,1)S(1)}, bf16[768,3,192]{0,2,1:T(8,128)(2,1)}, u32[]{:S(2)}) copy-start(bf16[768,3,192]{0,2,1:T(8,128)(2,1)} %copy-done.47) | copy-start | bytes 2654212
  644.8 106.3 %all-gather.14.cloned.1.call-start = ((), (), s32[]{:S(2)}) async-start(), calls=%async_computation.12 | async-start | bytes 2875392 | tf_op jit(solution)/shard_map/all_gather | solution.py:1569
  680.9 2.2 collective-permute-start
  688.5 75.9 %all-gather.12.cloned.1.call-start = ((), (), s32[]{:S(2)}) async-start(), calls=%async_computation.11 | async-start | bytes 3981312 | tf_op jit(solution)/shard_map/all_gather | solution.py:1571
  689.7 32.5 %copy-start.40 = (f32[192,768]{1,0:T(8,128)S(1)}, f32[192,768]{1,0:T(8,128)}, u32[]{:S(2)}) copy-start(f32[192,768]{1,0:T(8,128)} %copy-done.39) | copy-start | bytes 1769476
  689.7 33.6 %copy-start.37 = (f32[6,96,768]{2,1,0:T(8,128)S(1)}, f32[6,96,768]{2,1,0:T(8,128)}, u32[]{:S(2)}) copy-start(f32[6,96,768]{2,1,0:T(8,128)} %get-tuple-element.149) | copy-start | bytes 5308420
  736.5 13.5 %copy-start.43 = (f32[256,768]{1,0:T(8,128)S(1)}, f32[256,768]{1,0:T(8,128)}, u32[]{:S(2)}) copy-start(f32[256,768]{1,0:T(8,128)} %get-tuple-element.142) | copy-start | bytes 2359300
  747.9 16.5 %copy-start.1 = (f32[768,3,192]{0,2,1:T(8,128)S(1)}, f32[768,3,192]{0,2,1:T(8,128)}, u32[]{:S(2)}) copy-start(f32[768,3,192]{0,2,1:T(8,128)} %param.34) | copy-start | bytes 5308420
  747.9 16.5 %copy-start.4 = (f32[192,768]{1,0:T(8,128)S(1)}, f32[192,768]{1,0:T(8,128)}, u32[]{:S(2)}) copy-start(f32[192,768]{1,0:T(8,128)} %refs_2_.1) | copy-start | bytes 1769476
  (59 other events, 234.2 us)
Sparse Core Ops, SparseCore 0:
  11.0 87.4 all-gather.5
  111.8 34.4 reduce-scatter.4
  230.3 59.9 reduce-scatter.6
  369.5 37.1 all-gather.7
  418.5 34.9 reduce-scatter.8
  460.3 35.6 all-gather.9
  644.9 43.6 reduce-scatter.10
  691.1 35.7 all-gather.13
  729.7 34.6 all-gather.11

commit v4 on v3

--- a/solution.py
+++ b/solution.py
@@ -598,18 +598,11 @@
     return full.reshape(dp_count * each, width)
 
 
-def line_gather_body(
-    small, x_ref, out_ref, right_send, right_recv, left_send, left_recv
-):
+def line_steps(x_ref, out_ref, right_send, right_recv, left_send, left_recv):
     rank = lax.axis_index("dp")
     depth = lax.axis_index("tensor")
-    depths = lax.axis_size("tensor")
-    last = depths - 1
+    last = lax.axis_size("tensor") - 1
     right, left = (rank, depth + 1), (rank, depth - 1)
-    if small is None:
-        greet_line(depth, last, rank)
-    else:
-        greet(small_peers())
 
     def to_right(step):
         src = x_ref if step == 0 else out_ref.at[depth - step]
@@ -621,8 +614,7 @@
         src = x_ref if step == 0 else out_ref.at[depth + step]
         return send_to(src, out_ref.at[depth + step], left_send.at[step], left_recv.at[step], left)
 
-    for step in range(last):
-
+    def send(step):
         @pl.when((depth < last) & (depth >= step))
         def _():
             to_right(step).start()
@@ -633,9 +625,8 @@
 
         if step == 0:
             out_ref[depth] = x_ref[...]
-            if small is not None:
-                exchange_small(*small)
-
+
+    def receive(step):
         @pl.when(depth - 1 >= step)
         def _():
             send_to(
@@ -652,49 +643,106 @@
                 x_ref, out_ref.at[depth + 1 + step], left_send.at[step], left_recv.at[step], right
             ).wait_recv()
 
+    def finish():
+        for step in range(last):
+
+            @pl.when((depth < last) & (depth >= step))
+            def _():
+                to_right(step).wait_send()
+
+            @pl.when((depth > 0) & (depth + step <= last))
+            def _():
+                to_left(step).wait_send()
+
+    return send, receive, finish
+
+
+def line_gather_kernel(x_ref, out_ref, *sems):
+    last = lax.axis_size("tensor") - 1
+    greet_line(lax.axis_index("tensor"), last, lax.axis_index("dp"))
+    send, receive, finish = line_steps(x_ref, out_ref, *sems)
     for step in range(last):
-
-        @pl.when((depth < last) & (depth >= step))
-        def _():
-            to_right(step).wait_send()
-
-        @pl.when((depth > 0) & (depth + step <= last))
-        def _():
-            to_left(step).wait_send()
-
-
-def line_gather_kernel(x_ref, out_ref, *sems):
-    line_gather_body(None, x_ref, out_ref, *sems)
-
-
-def line_gather_small_kernel(
-    x_ref, y_ref, out_ref, small_ref, pair, plane, line, pair_sems, plane_sems, line_sems, *sems
+        send(step)
+        receive(step)
+    finish()
+
+
+def first_gather_kernel(
+    head_count,
+    x_ref,
+    y_ref,
+    t_ref,
+    weight_ref,
+    rows_ref,
+    small_ref,
+    tall_ref,
+    qkv_ref,
+    heads_ref,
+    log_ref,
+    pair,
+    plane,
+    line,
+    pair_sems,
+    plane_sems,
+    line_sems,
+    *sems,
 ):
-    small = (y_ref, small_ref, pair, plane, line, pair_sems, plane_sems, line_sems)
-    line_gather_body(small, x_ref, out_ref, *sems)
-
-
-def line_gather_small(block, small, collective):
+    last = lax.axis_size("tensor") - 1
+    greet(small_peers())
+    send, receive, finish = line_steps(x_ref, rows_ref, *sems[:4])
+    send_tall, receive_tall, finish_tall = line_steps(t_ref, tall_ref, *sems[4:])
+    count = x_ref.shape[0]
+    for step in range(last):
+        send(step)
+        if step == 0:
+            exchange_small(y_ref, small_ref, pair, plane, line, pair_sems, plane_sems, line_sems)
+        if step == 1:
+            send_tall(0)
+        receive(step)
+    receive_tall(0)
+    send_tall(1)
+    for j in range(last + 1):
+        qkv_ref[j * count : (j + 1) * count, :] = plain_dot(
+            rows_ref[j], weight_ref[...]
+        ).astype(jnp.bfloat16)
+    attend_forward_kernel(head_count, qkv_ref, heads_ref, log_ref)
+    for step in range(1, last):
+        receive_tall(step)
+        if step + 1 < last:
+            send_tall(step + 1)
+    finish()
+    finish_tall()
+
+
+def first_gather(block, small, tall, weight, head_count, collective):
     chips, depths = lax.axis_size("dp") // 2, lax.axis_size("tensor")
     rows, width = block.shape
-    out, total = pl.pallas_call(
-        line_gather_small_kernel,
+    outs = pl.pallas_call(
+        functools.partial(first_gather_kernel, head_count),
         out_shape=(
             jax.ShapeDtypeStruct((depths, rows, width), block.dtype),
             jax.ShapeDtypeStruct(small.shape, jnp.float32),
-        ),
-        in_specs=[whole_vmem()] * 2,
-        out_specs=(whole_vmem(), whole_vmem()),
+            jax.ShapeDtypeStruct((depths,) + tall.shape, tall.dtype),
+            jax.ShapeDtypeStruct((LEN, weight.shape[1]), jnp.bfloat16),
+            jax.ShapeDtypeStruct((LEN, head_count * HEAD), jnp.bfloat16),
+            jax.ShapeDtypeStruct((LEN, 128), jnp.float32),
+        ),
+        in_specs=[whole_vmem()] * 4,
+        out_specs=tuple(whole_vmem() for _ in range(6)),
         scratch_shapes=small_scratch(small.shape, chips, depths)
-        + [pltpu.SemaphoreType.DMA((depths,))] * 4,
+        + [pltpu.SemaphoreType.DMA((depths,))] * 8,
         compiler_params=pltpu.CompilerParams(
-            collective_id=collective, has_side_effects=True, vmem_limit_bytes=16 * 2**20
+            collective_id=collective, has_side_effects=True, vmem_limit_bytes=40 * 2**20
         ),
         cost_estimate=pl.CostEstimate(
-            flops=25 * 10**9, bytes_accessed=depths * rows * width * 4, transcendentals=0
-        ),
-    )(block, small)
-    return out.reshape(depths * rows, width), total
+            flops=80 * 10**9, bytes_accessed=depths * tall.size * 4, transcendentals=0
+        ),
+    )(block, small, tall, weight)
+    return (
+        outs[0].reshape(depths * rows, width),
+        outs[1],
+        outs[2].reshape(depths * rows, tall.shape[1]),
+    ) + tuple(outs[3:])
 
 
 def line_gather(block, collective):
@@ -757,6 +805,7 @@
 
 
 HALF = 128
+QUARTER = 64
 
 
 def greet_line(depth, last, rank):
@@ -822,16 +871,16 @@
             stage.at[j, h], from_right.at[j, h], sum_sems.at[j, h], from_right_sems.at[j, h], left
         )
 
-    for h in range(2):
-        rows[depth, h] = x_ref[h * HALF : (h + 1) * HALF, :]
+    for q in range(4):
+        rows[depth, q] = x_ref[q * QUARTER : (q + 1) * QUARTER, :]
 
         @pl.when(depth < last)
         def _():
-            rows_right(depth, h).start()
+            rows_right(depth, q).start()
 
         @pl.when(depth > 0)
         def _():
-            rows_left(depth, h).start()
+            rows_left(depth, q).start()
 
     inner = depth * (last - depth) // 2
     side = depth // 2
@@ -840,53 +889,58 @@
         j = base + side * (last - 2 * base)
 
         def half_step(h, carry):
-            if step:
-
-                @pl.when(j < depth)
-                def _():
-                    rows_right(j, h).wait_recv()
-
-                @pl.when(j > depth)
-                def _():
-                    rows_left(j, h).wait_recv()
-
-                @pl.when((j < depth) & (depth < last))
-                def _():
-                    rows_right(j, h).start()
-
-                @pl.when((j > depth) & (depth > 0))
-                def _():
-                    rows_left(j, h).start()
-
-            hidden = smooth_gelu(plain_dot(rows[j, h], first_ref[...])).astype(jnp.bfloat16)
+            for q in (2 * h, 2 * h + 1):
+                if step:
+
+                    @pl.when(j < depth)
+                    def _():
+                        rows_right(j, q).wait_recv()
+
+                    @pl.when(j > depth)
+                    def _():
+                        rows_left(j, q).wait_recv()
+
+                    @pl.when((j < depth) & (depth < last))
+                    def _():
+                        rows_right(j, q).start()
+
+                    @pl.when((j > depth) & (depth > 0))
+                    def _():
+                        rows_left(j, q).start()
+
+            block = jnp.concatenate([rows[j, 2 * h], rows[j, 2 * h + 1]], axis=0)
+            hidden = smooth_gelu(plain_dot(block, first_ref[...])).astype(jnp.bfloat16)
             part = plain_dot(hidden, second_ref[...])
-            parts[j, h] = part
-            if step:
-
-                @pl.when((depth == 0) | (depth == last))
-                def _():
-                    stage[j, h] = part.astype(jnp.bfloat16)
-
-                @pl.when(depth == 0)
-                def _():
-                    sum_right(j, h).start()
-
-                @pl.when(depth == last)
-                def _():
-                    sum_left(j, h).start()
+            for i in range(2):
+                q = 2 * h + i
+                piece = part[i * QUARTER : (i + 1) * QUARTER, :]
+                parts[j, q] = piece
+                if step:
+
+                    @pl.when((depth == 0) | (depth == last))
+                    def _():
+                        stage[j, q] = piece.astype(jnp.bfloat16)
+
+                    @pl.when(depth == 0)
+                    def _():
+                        sum_right(j, q).start()
+
+                    @pl.when(depth == last)
+                    def _():
+                        sum_left(j, q).start()
 
             return carry
 
         lax.fori_loop(0, 2, half_step, 0)
 
     def relay_right(j):
-        for h in range(2):
+        for h in range(4):
             sum_right(j, h).wait_recv()
             stage[j, h] = (parts[j, h] + from_left[j, h].astype(jnp.float32)).astype(jnp.bfloat16)
             sum_right(j, h).start()
 
     def relay_left(j):
-        for h in range(2):
+        for h in range(4):
             sum_left(j, h).wait_recv()
             stage[j, h] = (parts[j, h] + from_right[j, h].astype(jnp.float32)).astype(jnp.bfloat16)
             sum_left(j, h).start()
@@ -903,8 +957,8 @@
         relay_left(0)
         relay_right(3)
 
-    for h in range(2):
-        span = slice(h * HALF, (h + 1) * HALF)
+    for h in range(4):
+        span = slice(h * QUARTER, (h + 1) * QUARTER)
         out_ref[span, :] = parts[depth, h]
 
         @pl.when(depth > 0)
@@ -918,7 +972,7 @@
             out_ref[span, :] += from_right[depth, h].astype(jnp.float32)
 
     for j in range(4):
-        for h in range(2):
+        for h in range(4):
 
             @pl.when((depth >= j) & (depth < last))
             def _():
@@ -939,7 +993,7 @@
 
 def line_mlp(block, first, second, collective):
     count, width = block.shape
-    slots = (4, 2, HALF, width)
+    slots = (4, 4, QUARTER, width)
     return pl.pallas_call(
         line_mlp_kernel,
         out_shape=jax.ShapeDtypeStruct((count, width), jnp.float32),
@@ -952,7 +1006,7 @@
             pltpu.VMEM(slots, jnp.bfloat16),
             pltpu.VMEM(slots, jnp.bfloat16),
         ]
-        + [pltpu.SemaphoreType.DMA((4, 2))] * 6,
+        + [pltpu.SemaphoreType.DMA((4, 4))] * 6,
         compiler_params=pltpu.CompilerParams(
             collective_id=collective, has_side_effects=True, vmem_limit_bytes=48 * 2**20
         ),
@@ -1396,9 +1450,6 @@
     count_block = jnp.full((8, 128), jnp.sum(resp_mask), jnp.int32).astype(jnp.float32)
     tokens_all = lax.axis_size("dp") * seq_count * LEN
 
-    def teacher_gather(local_rows):
-        return lax.all_gather(local_rows, "tensor", axis=0, tiled=True)
-
     def student_gather(local_rows):
         return lax.all_gather(local_rows, "tensor", axis=0, tiled=True)
 
@@ -1418,7 +1469,6 @@
     live_count = HT // groups + (tensor_rank < HT % groups).astype(jnp.int32)
     live_slots = (jnp.arange(slot_count, dtype=jnp.int32) < live_count).astype(jnp.float32)
     teacher_normed = norm_parts(teacher_x, t_gains[0], t_shifts[0])[0].astype(jnp.bfloat16)
-    teacher_all = teacher_gather(teacher_normed)
     student_x = student_in.astype(jnp.float32)
     shard_width = s_qkv.shape[2]
     shard_hidden = s_fc.shape[1]
@@ -1430,12 +1480,11 @@
     w_map = s_map.astype(jnp.bfloat16)
     normed_one, unit_one, scale_one = norm_parts(student_x, s_norms[0], s_norms[1])
     low_one = normed_one.astype(jnp.bfloat16)
-    rows_one, count_sum = line_gather_small(low_one, count_block, 5)
+    rows_one, count_sum, teacher_all, mixed_qkv, head_out, log_sums = first_gather(
+        low_one, count_block, teacher_normed, w_qkv, head_count, 5
+    )
     count_val = count_sum[0, 0]
     factor = tokens_all / (2.0 * count_val)
-    mixed_qkv = jnp.dot(rows_one, w_qkv, preferred_element_type=jnp.float32).astype(jnp.bfloat16)
-    head_out, log_sums = attend_forward(mixed_qkv, head_count)
-    teacher_all, head_out = lax.optimization_barrier((teacher_all, head_out))
     resid = student_x + student_reduce(head_out, w_out, 0)
     teacher_mixed = jnp.dot(
         teacher_all, t_qkv.reshape(DT, 3 * slot_width), preferred_element_type=jnp.float32

time: 788 us -> 785 us (level)
  starting transfers between devices: 11.3 us -> 0.89 us
    reduce_scatter x4, starting transfers between devices: 11 us -> 0.55 us  [student_reduce(): lax.psum_scatter(lax.dot_general(left, right, (((1,), (right_dim,)), ((),...]
    pallas_call x2 -> x1, Pallas kernels: 22.1 us -> 15.8 us  [attend_forward(): pl.pallas_call(functools.partial(attend_forward_kernel, head_count), out_...]
    unnamed x164 -> x172, local copies, waits for them, and re-layouts: 20.4 us -> 26.1 us
  transfers between devices with their start and end apart: 10 -> 9, of which waited for: 3 -> 4; matrix products, arithmetic and copies ran while one was open for 7% -> 6% of each run, Pallas kernels for 52% -> 41%
where the time goes in v4:
time: 785 us; the launch traced here: 775 us
  Pallas kernels  596 us (76%)
  matrix products  63.4 us (8%)
  local copies, waits for them, and re-layouts  38.5 us (5%)
  other arithmetic  35.8 us (5%)
  between operations  20.5 us (3%)
  waiting for transfers between devices  19.8 us (3%)
    pallas_call x1, Pallas kernels, line_mlp(): pl.pallas_call(line_mlp_kernel, out_shape=jax.ShapeDtypeStruct((count, wi...  125 us
    pallas_call x1, Pallas kernels, first_gather(): pl.pallas_call(functools.partial(first_gather_kernel, head_count), out_sh...  88.7 us
    pallas_call x2, Pallas kernels, scatter_rows(): pl.pallas_call(scatter_rows_kernel, out_shape=jax.ShapeDtypeStruct(slab,...  67.3 us
    pallas_call x1, Pallas kernels, sum_and_spread(): pl.pallas_call(sum_and_spread_kernel, out_shape=(jax.ShapeDtypeStruct((dp...  65 us
    pallas_call x1, Pallas kernels, line_exchange(): pl.pallas_call(line_exchange_kernel, out_shape=(jax.ShapeDtypeStruct((2 *...  63.6 us
    pallas_call x1, Pallas kernels, share_gram(): pl.pallas_call(share_gram_kernel, out_shape=jax.ShapeDtypeStruct((dp_coun...  41.7 us
    pallas_call x1, Pallas kernels, orthogonal_factor(): pl.pallas_call(polynomial_kernel, out_shape=jax.ShapeDtypeStruct((size, s...  33.3 us
    pallas_call x1, Pallas kernels, line_gather(): pl.pallas_call(line_gather_kernel, out_shape=jax.ShapeDtypeStruct((depths...  32.5 us
  transfers between devices with their start and end apart: 9, of which 4 were waited for; matrix products, arithmetic and copies ran while one was open for 6% of the time, Pallas kernels for 41%

profile of v4, /device:TPU:0, one launch (start us, length us, event | category | flops | bytes accessed | tf_op | source)
XLA Modules:
  0.0 775.2 jit_solution(14977240570076887512)
XLA Ops:
  15.3 88.7 %shard_map.390 = (bf16[4,256,768]{2,1,0:T(8,128)(2,1)S(1)}, f32[8,128]{1,0:T(8,128)S(1)}, bf16[4,256,1600]{2,1,0:T(8,128)(2,1)S(1)}, bf16[1024,576]{1,0:T(8,128)...) custom-call(bf16[256,768]{1,0:T(8,128)(2,1)S(1)} %fusion.26.x_ref, ...), custom_call_target="tpu_custom_call" | custom-call | flops 80000000000 | bytes 6553600 | tf_op jit(solution)/shard_map/pallas_call | solution.py:720
  112.1 8.8 %convolution_convert_fusion = bf16[1024,1344]{0,1:T(8,128)(2,1)} fusion(bf16[1024,1600]{1,0:T(8,128)(2,1)S(1)} %bitcast.98, bf16[1600,1344]{0,1:T(8,128)(2,1)} %bitcast.115), kind=kOutput, calls=%fused_computation.7 | convolution fusion | flops 4405395456 | bytes 10330112 | tf_op jit(solution)/shard_map/dot_general | solution.py:1489
  120.9 3.5 copy.59.qkv_ref
  126.5 15.8 %shard_map.391 = (bf16[1024,448]{1,0:T(8,128)(2,1)S(1)}, f32[1024,128]{1,0:T(8,128)}) custom-call(bf16[1024,1344]{1,0:T(8,128)(2,1)S(1)} %copy.59.qkv_ref), custom_call_target="tpu_custom_call" | custom-call | flops 7516192768 | bytes 3670016 | tf_op jit(solution)/shard_map/pallas_call | solution.py:114
  150.9 63.6 %shard_map.392 = (f32[256,1600]{1,0:T(8,128)S(1)}, bf16[4,256,768]{2,1,0:T(8,128)(2,1)S(1)}) custom-call(bf16[1024,448]{1,0:T(8,128)(2,1)S(1)} %broadcast_select_fusion.heads_ref, bf16[448,1600]{1,0:T(8,128)(2,1)S(1)} %copy-done.11, bf16[256,768]{1,0:T(8,128)(2,1)S(1)} %add_convert_fusion.3.x_ref), custom_call_target="tpu_custom_call" | custom-call | flops 60000002048 | bytes 7340032 | tf_op jit(solution)/shard_map/pallas_call | solution.py:1279
  217.7 3.1 convolution_convert_fusion.4
  222.0 125.5 %shard_map.393 = f32[256,1600]{1,0:T(8,128)S(1)} custom-call(bf16[256,1600]{1,0:T(8,128)(2,1)S(1)} %add_convert_fusion.1.x_ref, bf16[1600,1600]{1,0:T(8,128)(2,1)} %first_ref.1, bf16[1600,1600]{1,0:T(8,128)(2,1)} %second_ref.1), custom_call_target="tpu_custom_call" | custom-call | flops 41943040000 | bytes 6553600 | tf_op jit(solution)/shard_map/pallas_call | solution.py:997
  349.8 4.4 fusion.13
  354.2 3.2 fusion.76
  359.6 2.8 concatenate.18
  362.3 35.7 %shard_map.394.y_ref = f32[224,768]{1,0:T(8,128)S(1)} custom-call(f32[8,224,768]{2,1,0:T(8,128)S(1)} %bitcast.90), custom_call_target="tpu_custom_call" | custom-call | flops 26880000000 | bytes 5505024 | tf_op jit(solution)/shard_map/pallas_call | solution.py:511
  398.9 6.6 fusion.3
  406.6 2.6 convolution_convert_fusion.3
  409.3 3.5 fusion.82
  415.0 31.6 %shard_map.395.x_ref = f32[192,768]{1,0:T(8,128)S(1)} custom-call(f32[8,192,768]{2,1,0:T(8,128)S(1)} %bitcast.91), custom_call_target="tpu_custom_call" | custom-call | flops 23040000000 | bytes 4718592 | tf_op jit(solution)/shard_map/pallas_call | solution.py:511
  450.5 31.5 %shard_map.396 = f32[8,192,768]{2,1,0:T(8,128)S(1)} custom-call(f32[192,768]{1,0:T(8,128)S(1)} %shard_map.395.x_ref), custom_call_target="tpu_custom_call" | custom-call | flops 35000000512 | bytes 4718592 | tf_op jit(solution)/shard_map/pallas_call | solution.py:582
  484.1 2.8 all-gather.7.cloned.1.call-done
  490.6 8.9 %shard_map.397 = bf16[1024,576]{1,0:T(8,128)(2,1)S(1)} custom-call(bf16[1024,576]{1,0:T(8,128)(2,1)S(1)} %copy-done.20, f32[1024,128]{1,0:T(8,128)S(1)} %copy-done.22, bf16[1024,192]{1,0:T(8,128)(2,1)S(1)} %copy.61.grad_ref), custom_call_target="tpu_custom_call" | custom-call | flops 8053063680 | bytes 3145728 | tf_op jit(solution)/shard_map/pallas_call | solution.py:183
  501.8 65.0 %shard_map.398 = (f32[8,96,768]{2,1,0:T(8,128)S(1)}, f32[8,224,768]{2,1,0:T(8,128)S(1)}) custom-call(f32[8,96,768]{2,1,0:T(8,128)S(1)} %bitcast.96, f32[224,768]{1,0:T(8,128)S(1)} %copy-done.24), custom_call_target="tpu_custom_call" | custom-call | flops 60000002048 | bytes 9437184 | tf_op jit(solution)/shard_map/pallas_call | solution.py:430
  570.0 5.3 slice_bitcast_fusion
  575.3 3.2 fusion.23.extra_ref
  581.9 2.8 multiply_add_fusion.3
  584.7 2.4 fusion.53
  588.8 41.7 %shard_map.399 = f32[8,96,768]{2,1,0:T(8,128)S(1)} custom-call(f32[4,96,768]{2,1,0:T(8,128)S(1)} %bitcast.97, f32[96,768]{1,0:T(8,128)S(1)} %fusion.23.extra_ref), custom_call_target="tpu_custom_call" | custom-call | flops 44999999488 | bytes 4718592 | tf_op jit(solution)/shard_map/pallas_call | solution.py:1105
  631.9 2.5 convolution_convert_fusion.2
  636.4 33.3 %shard_map.400 = f32[768,768]{1,0:T(8,128)S(1)} custom-call(f32[768,768]{1,0:T(8,128)S(1)} %bitcast.99), custom_call_target="tpu_custom_call" | custom-call | flops 30802968576 | bytes 4718592 | tf_op jit(solution)/shard_map/pallas_call | solution.py:1394
  672.9 5.5 convolution_convert_fusion.1
  681.5 32.5 %shard_map.402 = f32[4,96,768]{2,1,0:T(8,128)S(1)} custom-call(f32[96,768]{1,0:T(8,128)S(1)} %dynamic-slice_select_fusion.x_ref), custom_call_target="tpu_custom_call" | custom-call | flops 24999999488 | bytes 1179648 | tf_op jit(solution)/shard_map/pallas_call | solution.py:751
  721.0 3.0 fusion.8
  725.7 11.7 %shard_map.401 = f32[8,768]{1,0:T(8,128)S(1)} custom-call(f32[8,768]{1,0:T(8,128)S(1)} %concatenate.22.refs_0_), custom_call_target="tpu_custom_call" | custom-call | flops 10000000000 | bytes 1000000 | tf_op jit(solution)/shard_map/pallas_call | solution.py:295
  740.6 13.8 %all-gather.9.cloned.1.call-done.group_ref = bf16[768,2304]{1,0:T(8,128)(2,1)} async-done(((bf16[96,2304]{1,0:T(8,128)(2,1)}), bf16[768,2304]{1,0:T(8,128)(2,1)}) %all-gather.9.cloned.1.call-update) | async-done | bytes 3538960 | tf_op jit(solution)/shard_map/all_gather | solution.py:1620
  756.1 10.7 %shard_map.403 = (f32[768,768]{1,0:T(8,128)}, f32[768,768]{1,0:T(8,128)}, f32[192,768]{1,0:T(8,128)}, f32[576,768]{1,0:T(8,128)}, f32[1600,768]{1,0:T(8,128)}) custom-call(bf16[768,2304]{1,0:T(8,128)(2,1)} %all-gather.9.cloned.1.call-done.group_ref, bf16[768,1600]{1,0:T(8,128)(2,1)} %all-gather.11.cloned.1.call-done.map_ref, f32[768,768]{1,0:T(8,128)S(1)} %copy-done.8, ...), custom_call_target="tpu_custom_call" | custom-call | flops 1000000000 | bytes 17694720 | tf_op jit(solution)/shard_map/pallas_call | solution.py:795
  (276 shorter events, 78.9 us)
Async XLA Ops:
  7.2 138.6 %reduce-scatter.5.cloned.1.call-start = ((), (), s32[]{:S(2)}) async-start(), calls=%async_computation.4 | async-start | bytes 1966080 | tf_op jit(solution)/shard_map/reduce_scatter | solution.py:1457
  9.6 138.7 %copy-start.55 = (f32[768]{0:T(1024)}, f32[768]{0:T(1024)S(1)}, u32[]{:S(2)}) copy-start(f32[768]{0:T(1024)S(1)} %get-tuple-element.152) | copy-start | bytes 9220
  15.3 94.3 %copy-start.2 = (f32[192,768]{1,0:T(8,128)S(1)}, f32[192,768]{1,0:T(8,128)}, u32[]{:S(2)}) copy-start(f32[192,768]{1,0:T(8,128)} %refs_2_.1) | copy-start | bytes 1769476
  111.3 237.3 %reduce-scatter.7.cloned.1.call-start = ((), (), s32[]{:S(2)}) async-start(), calls=%async_computation.5 | async-start | bytes 1966080 | tf_op jit(solution)/shard_map/reduce_scatter | solution.py:1457
  147.0 67.5 %copy-start.63 = (f32[256]{0:T(256)}, f32[256]{0:T(256)S(1)}, u32[]{:S(2)}) copy-start(f32[256]{0:T(256)S(1)} %broadcast_multiply_fusion.8) | copy-start | bytes 3076
  148.3 66.3 %copy-start.67 = (f32[256]{0:T(256)}, f32[256]{0:T(256)S(1)}, u32[]{:S(2)}) copy-start(f32[256]{0:T(256)S(1)} %add_rsqrt_fusion.1) | copy-start | bytes 3076
  150.9 63.7 %copy-start.6 = (f32[768,768]{1,0:T(8,128)S(1)}, f32[768,768]{1,0:T(8,128)}, u32[]{:S(2)}) copy-start(f32[768,768]{1,0:T(8,128)} %refs_0_.1) | copy-start | bytes 7077892
  220.9 178.1 %all-gather.5.cloned.1.call-start = ((), (), s32[]{:S(2)}) async-start(), calls=%async_computation.6 | async-start | bytes 1966080 | tf_op jit(solution)/shard_map/all_gather | solution.py:1454
  359.4 87.3 %reduce-scatter.9.cloned.1.call-start = ((), (), s32[]{:S(2)}) async-start(), calls=%async_computation.7 | async-start | bytes 1966080 | tf_op jit(solution)/shard_map/reduce_scatter | solution.py:1457
  398.9 7.7 copy-start.7
  409.2 77.7 %all-gather.7.cloned.1.call-start = ((), (), s32[]{:S(2)}) async-start(), calls=%async_computation.8 | async-start | bytes 1966080 | tf_op jit(solution)/shard_map/all_gather | solution.py:1454
  415.0 32.8 %copy-start.56 = (f32[768]{0:T(1024)S(1)}, f32[768]{0:T(1024)}, u32[]{:S(2)}) copy-start(f32[768]{0:T(1024)} %copy-done.55) | copy-start | bytes 9220
  415.0 32.8 %copy-start.64 = (f32[256]{0:T(256)S(1)}, f32[256]{0:T(256)}, u32[]{:S(2)}) copy-start(f32[256]{0:T(256)} %copy-done.63) | copy-start | bytes 3076
  415.0 32.8 %copy-start.68 = (f32[256]{0:T(256)S(1)}, f32[256]{0:T(256)}, u32[]{:S(2)}) copy-start(f32[256]{0:T(256)} %copy-done.67) | copy-start | bytes 3076
  450.2 36.8 %copy-start.3 = (f32[192,768]{1,0:T(8,128)S(1)}, f32[192,768]{1,0:T(8,128)}, u32[]{:S(2)}) copy-start(f32[192,768]{1,0:T(8,128)} %refs_2_.1) | copy-start | bytes 1769476
  450.2 229.3 %reduce-scatter.11.cloned.1.call-start = ((), (), s32[]{:S(2)}) async-start(), calls=%async_computation.9 | async-start | bytes 1966080 | tf_op jit(solution)/shard_map/reduce_scatter | solution.py:1457
  490.6 8.9 %copy-start.17 = (bf16[4,256,768]{2,1,0:T(8,128)(2,1)S(1)}, bf16[4,256,768]{2,1,0:T(8,128)(2,1)}, u32[]{:S(2)}) copy-start(bf16[4,256,768]{2,1,0:T(8,128)(2,1)} %copy-done.16) | copy-start | bytes 4718596
  501.8 65.1 %copy-start.35 = (f32[768,3,192]{0,2,1:T(8,128)S(1)}, f32[768,3,192]{0,2,1:T(8,128)}, u32[]{:S(2)}) copy-start(f32[768,3,192]{0,2,1:T(8,128)} %broadcast_multiply_fusion) | copy-start | bytes 5308420
  566.9 13.0 %copy-start.52 = (f32[2,96,768]{2,1,0:T(8,128)}, f32[2,96,768]{2,1,0:T(8,128)S(1)}, u32[]{:S(2)}) copy-start(f32[2,96,768]{2,1,0:T(8,128)S(1)} %slice.79) | copy-start | bytes 1769476
  581.2 132.7 %copy-start.44 = (f32[192,768]{1,0:T(8,128)}, f32[192,768]{1,0:T(8,128)S(1)}, u32[]{:S(2)}) copy-start(f32[192,768]{1,0:T(8,128)S(1)} %multiply_add_fusion.5) | copy-start | bytes 1769476
  588.8 43.1 %copy-start.46 = (bf16[768,3,192]{0,2,1:T(8,128)(2,1)S(1)}, bf16[768,3,192]{0,2,1:T(8,128)(2,1)}, u32[]{:S(2)}) copy-start(bf16[768,3,192]{0,2,1:T(8,128)(2,1)} %convert_element_type.125) | copy-start | bytes 2654212
  634.5 106.1 %all-gather.11.cloned.1.call-start = ((), (), s32[]{:S(2)}) async-start(), calls=%async_computation.11 | async-start | bytes 2875392 | tf_op jit(solution)/shard_map/all_gather | solution.py:1618
  670.6 2.3 collective-permute-start
  678.5 75.9 %all-gather.9.cloned.1.call-start = ((), (), s32[]{:S(2)}) async-start(), calls=%async_computation.10 | async-start | bytes 3981312 | tf_op jit(solution)/shard_map/all_gather | solution.py:1620
  681.5 33.0 %copy-start.40 = (f32[6,96,768]{2,1,0:T(8,128)S(1)}, f32[6,96,768]{2,1,0:T(8,128)}, u32[]{:S(2)}) copy-start(f32[6,96,768]{2,1,0:T(8,128)} %get-tuple-element.171) | copy-start | bytes 5308420
  725.6 13.1 %copy-start.75 = (f32[256]{0:T(256)S(1)}, f32[256]{0:T(256)}, u32[]{:S(2)}) copy-start(f32[256]{0:T(256)} %get-tuple-element.143) | copy-start | bytes 3076
  725.6 13.1 %copy-start.58 = (f32[4,768]{1,0:T(4,128)S(1)}, f32[4,768]{1,0:T(4,128)}, u32[]{:S(2)}) copy-start(f32[4,768]{1,0:T(4,128)} %param.33) | copy-start | bytes 36868
  725.6 13.1 %copy-start.73 = (f32[4,768]{1,0:T(4,128)S(1)}, f32[4,768]{1,0:T(4,128)}, u32[]{:S(2)}) copy-start(f32[4,768]{1,0:T(4,128)} %param.45) | copy-start | bytes 36868
  725.7 13.1 %copy-start.74 = (f32[4,768]{1,0:T(4,128)S(1)}, f32[4,768]{1,0:T(4,128)}, u32[]{:S(2)}) copy-start(f32[4,768]{1,0:T(4,128)} %param.44) | copy-start | bytes 36868
  725.7 13.8 %copy-start.48 = (f32[256,768]{1,0:T(8,128)S(1)}, f32[256,768]{1,0:T(8,128)}, u32[]{:S(2)}) copy-start(f32[256,768]{1,0:T(8,128)} %get-tuple-element.164) | copy-start | bytes 2359300
  737.4 17.0 %copy-start.1 = (f32[768,3,192]{0,2,1:T(8,128)S(1)}, f32[768,3,192]{0,2,1:T(8,128)}, u32[]{:S(2)}) copy-start(f32[768,3,192]{0,2,1:T(8,128)} %param.34) | copy-start | bytes 5308420
  737.4 17.0 %copy-start.4 = (f32[192,768]{1,0:T(8,128)S(1)}, f32[192,768]{1,0:T(8,128)}, u32[]{:S(2)}) copy-start(f32[192,768]{1,0:T(8,128)} %refs_2_.1) | copy-start | bytes 1769476
  (62 other events, 174.4 us)
Sparse Core Ops, SparseCore 0:
  111.5 34.3 reduce-scatter.4
  221.0 60.7 reduce-scatter.6
  359.5 37.6 all-gather.4
  409.4 35.1 reduce-scatter.8
  450.3 36.6 all-gather.6
  634.6 43.7 reduce-scatter.10
  680.8 35.9 all-gather.10
  719.3 35.0 all-gather.8

commit v5 on v4

--- a/solution.py
+++ b/solution.py
@@ -386,38 +386,61 @@
         plane_copies[k].wait_recv()
         value = value + plane_in[k]
     total[...] = value
-    x_spread = start_spread(total, x_out, spread_sems.at[2], flat, rank)
+    square = chips == 4
+    row, col = chip // 2, lax.rem(chip, 2)
+    if square:
+        from_chip = [chip, 2 * row + 1 - col, 2 * (1 - row) + col, 2 * (1 - row) + 1 - col]
+        peers = [(c * 2 + core, depth) for c in from_chip]
+    else:
+        from_chip = [lax.rem(chip + chips - k, chips) for k in range(chips)]
+        peers = flat
+
+    def begin(src, dst, sems, cols):
+        copies = {}
+        for k in (1, 2) if square else range(1, chips):
+            copies[k] = send_to(
+                src.at[:, cols], dst.at[rank, :, cols], sems.at[0, k], sems.at[1, k], peers[k]
+            )
+            copies[k].start()
+        return copies
+
+    def pass_on(dst, copies, sems, cols, via):
+        if square:
+            copies[via].wait_recv()
+            held = dst.at[from_chip[via] * 2 + core, :, cols]
+            copies[3] = send_to(held, held, sems.at[0, 3], sems.at[1, 3], peers[3 - via])
+            copies[3].start()
+
+    def share(dst, copies, sems, cols, via):
+        shares = {}
+        for k in (0, via, 3 - via, 3) if square else range(chips):
+            if k and not (square and k == via):
+                copies[k].wait_recv()
+            held = dst.at[from_chip[k] * 2 + core, :, cols]
+            shares[k] = send_to(held, held, sems.at[0, k], sems.at[1, k], sibling)
+            shares[k].start()
+        return shares
+
     x_out[rank] = value
-    y_spread, y_share = {}, {}
+    x_spread = [begin(total, x_out, spread_sems.at[2 + c], halves[c]) for c in range(2)]
+    y_spread = []
     for c in range(2):
         for k in range(1, depths):
             seconds[c, k].wait_recv()
-        y_spread[c] = start_spread(
-            line_out, y_out, spread_sems.at[c], flat, rank, halves[c]
-        )
         y_out[rank, :, halves[c]] = line_out[:, halves[c]]
-    place = (chips, chip, core)
-    x_share = start_share(x_out, x_spread, share_sems.at[2], place, sibling)
+        y_spread.append(begin(line_out, y_out, spread_sems.at[c], halves[c]))
+        if c == 0:
+            for i in range(2):
+                pass_on(x_out, x_spread[i], spread_sems.at[2 + i], halves[i], 1 + i)
     for c in range(2):
-        y_share[c] = start_share(
-            y_out, y_spread[c], share_sems.at[c], place, sibling, halves[c]
-        )
+        pass_on(y_out, y_spread[c], spread_sems.at[c], halves[c], 1 + c)
+    shares = [
+        share(x_out, x_spread[c], share_sems.at[2 + c], halves[c], 1 + c) for c in range(2)
+    ] + [share(y_out, y_spread[c], share_sems.at[c], halves[c], 1 + c) for c in range(2)]
     for k in range(chips):
-        x_share[k].wait_recv()
-        y_share[0][k].wait_recv()
-        y_share[1][k].wait_recv()
-    for copies in (
-        pair_copies,
-        plane_copies,
-        firsts,
-        seconds,
-        y_spread[0],
-        y_spread[1],
-        x_spread,
-        y_share[0],
-        y_share[1],
-        x_share,
-    ):
+        for copies in shares:
+            copies[k].wait_recv()
+    for copies in [pair_copies, plane_copies, firsts, seconds] + x_spread + y_spread + shares:
         for copy in copies.values():
             copy.wait_send()
 
@@ -445,8 +468,8 @@
             pltpu.SemaphoreType.DMA((2, chips)),
             pltpu.SemaphoreType.DMA((2, chips)),
             pltpu.SemaphoreType.DMA((2, 4, depths)),
-            pltpu.SemaphoreType.DMA((3, 2, chips)),
-            pltpu.SemaphoreType.DMA((3, 2, chips)),
+            pltpu.SemaphoreType.DMA((4, 2, chips)),
+            pltpu.SemaphoreType.DMA((4, 2, chips)),
         ],
         compiler_params=pltpu.CompilerParams(
             collective_id=collective, has_side_effects=True, vmem_limit_bytes=32 * 2**20

time: 785 us -> 775 us (0.987)
  Pallas kernels: 596 us -> 587 us
where the time goes in v5:
time: 775 us; the launch traced here: 766 us
  Pallas kernels  587 us (76%)
  matrix products  63.4 us (8%)
  local copies, waits for them, and re-layouts  38.5 us (5%)
  other arithmetic  35.4 us (5%)
  between operations  20.5 us (3%)
  waiting for transfers between devices  19.8 us (3%)
    pallas_call x1, Pallas kernels, line_mlp(): pl.pallas_call(line_mlp_kernel, out_shape=jax.ShapeDtypeStruct((count, wi...  125 us
    pallas_call x1, Pallas kernels, first_gather(): pl.pallas_call(functools.partial(first_gather_kernel, head_count), out_sh...  88.7 us
    pallas_call x2, Pallas kernels, scatter_rows(): pl.pallas_call(scatter_rows_kernel, out_shape=jax.ShapeDtypeStruct(slab,...  67.3 us
    pallas_call x1, Pallas kernels, line_exchange(): pl.pallas_call(line_exchange_kernel, out_shape=(jax.ShapeDtypeStruct((2 *...  63.6 us
    pallas_call x1, Pallas kernels, sum_and_spread(): pl.pallas_call(sum_and_spread_kernel, out_shape=(jax.ShapeDtypeStruct((dp...  59 us
    pallas_call x1, Pallas kernels, share_gram(): pl.pallas_call(share_gram_kernel, out_shape=jax.ShapeDtypeStruct((dp_coun...  41.5 us
    pallas_call x1, Pallas kernels, orthogonal_factor(): pl.pallas_call(polynomial_kernel, out_shape=jax.ShapeDtypeStruct((size, s...  33.3 us
    pallas_call x1, Pallas kernels, spread(): pl.pallas_call(spread_kernel, out_shape=jax.ShapeDtypeStruct((dp_count, e...  31.5 us
  transfers between devices with their start and end apart: 9, of which 4 were waited for; matrix products, arithmetic and copies ran while one was open for 6% of the time, Pallas kernels for 41%

profile of v5, /device:TPU:0, one launch (start us, length us, event | category | flops | bytes accessed | tf_op | source)
XLA Modules:
  0.0 765.8 jit_solution(422978562309231925)
XLA Ops:
  15.3 88.7 %shard_map.390 = (bf16[4,256,768]{2,1,0:T(8,128)(2,1)S(1)}, f32[8,128]{1,0:T(8,128)S(1)}, bf16[4,256,1600]{2,1,0:T(8,128)(2,1)S(1)}, bf16[1024,576]{1,0:T(8,128)...) custom-call(bf16[256,768]{1,0:T(8,128)(2,1)S(1)} %fusion.26.x_ref, ...), custom_call_target="tpu_custom_call" | custom-call | flops 80000000000 | bytes 6553600 | tf_op jit(solution)/shard_map/pallas_call | solution.py:743
  112.1 8.8 %convolution_convert_fusion = bf16[1024,1344]{0,1:T(8,128)(2,1)} fusion(bf16[1024,1600]{1,0:T(8,128)(2,1)S(1)} %bitcast.98, bf16[1600,1344]{0,1:T(8,128)(2,1)} %bitcast.115), kind=kOutput, calls=%fused_computation.7 | convolution fusion | flops 4405395456 | bytes 10330112 | tf_op jit(solution)/shard_map/dot_general | solution.py:1512
  120.9 3.5 copy.59.qkv_ref
  126.5 15.8 %shard_map.391 = (bf16[1024,448]{1,0:T(8,128)(2,1)S(1)}, f32[1024,128]{1,0:T(8,128)}) custom-call(bf16[1024,1344]{1,0:T(8,128)(2,1)S(1)} %copy.59.qkv_ref), custom_call_target="tpu_custom_call" | custom-call | flops 7516192768 | bytes 3670016 | tf_op jit(solution)/shard_map/pallas_call | solution.py:114
  150.9 63.6 %shard_map.392 = (f32[256,1600]{1,0:T(8,128)S(1)}, bf16[4,256,768]{2,1,0:T(8,128)(2,1)S(1)}) custom-call(bf16[1024,448]{1,0:T(8,128)(2,1)S(1)} %broadcast_select_fusion.heads_ref, bf16[448,1600]{1,0:T(8,128)(2,1)S(1)} %copy-done.11, bf16[256,768]{1,0:T(8,128)(2,1)S(1)} %add_convert_fusion.3.x_ref), custom_call_target="tpu_custom_call" | custom-call | flops 60000002048 | bytes 7340032 | tf_op jit(solution)/shard_map/pallas_call | solution.py:1302
  217.7 3.1 convolution_convert_fusion.4
  222.0 125.5 %shard_map.393 = f32[256,1600]{1,0:T(8,128)S(1)} custom-call(bf16[256,1600]{1,0:T(8,128)(2,1)S(1)} %add_convert_fusion.1.x_ref, bf16[1600,1600]{1,0:T(8,128)(2,1)} %first_ref.1, bf16[1600,1600]{1,0:T(8,128)(2,1)} %second_ref.1), custom_call_target="tpu_custom_call" | custom-call | flops 41943040000 | bytes 6553600 | tf_op jit(solution)/shard_map/pallas_call | solution.py:1020
  349.8 4.4 fusion.13
  354.2 3.2 fusion.76
  359.6 2.8 concatenate.18
  362.3 35.7 %shard_map.394.y_ref = f32[224,768]{1,0:T(8,128)S(1)} custom-call(f32[8,224,768]{2,1,0:T(8,128)S(1)} %bitcast.90), custom_call_target="tpu_custom_call" | custom-call | flops 26880000000 | bytes 5505024 | tf_op jit(solution)/shard_map/pallas_call | solution.py:534
  398.9 6.6 fusion.3
  406.6 2.6 convolution_convert_fusion.3
  409.3 3.5 fusion.82
  415.0 31.6 %shard_map.395.x_ref = f32[192,768]{1,0:T(8,128)S(1)} custom-call(f32[8,192,768]{2,1,0:T(8,128)S(1)} %bitcast.91), custom_call_target="tpu_custom_call" | custom-call | flops 23040000000 | bytes 4718592 | tf_op jit(solution)/shard_map/pallas_call | solution.py:534
  450.5 31.5 %shard_map.396 = f32[8,192,768]{2,1,0:T(8,128)S(1)} custom-call(f32[192,768]{1,0:T(8,128)S(1)} %shard_map.395.x_ref), custom_call_target="tpu_custom_call" | custom-call | flops 35000000512 | bytes 4718592 | tf_op jit(solution)/shard_map/pallas_call | solution.py:605
  484.1 2.8 all-gather.7.cloned.1.call-done
  490.6 8.9 %shard_map.397 = bf16[1024,576]{1,0:T(8,128)(2,1)S(1)} custom-call(bf16[1024,576]{1,0:T(8,128)(2,1)S(1)} %copy-done.20, f32[1024,128]{1,0:T(8,128)S(1)} %copy-done.22, bf16[1024,192]{1,0:T(8,128)(2,1)S(1)} %copy.61.grad_ref), custom_call_target="tpu_custom_call" | custom-call | flops 8053063680 | bytes 3145728 | tf_op jit(solution)/shard_map/pallas_call | solution.py:183
  501.8 59.0 %shard_map.398 = (f32[8,96,768]{2,1,0:T(8,128)S(1)}, f32[8,224,768]{2,1,0:T(8,128)S(1)}) custom-call(f32[8,96,768]{2,1,0:T(8,128)S(1)} %bitcast.96, f32[224,768]{1,0:T(8,128)S(1)} %copy-done.24), custom_call_target="tpu_custom_call" | custom-call | flops 60000002048 | bytes 9437184 | tf_op jit(solution)/shard_map/pallas_call | solution.py:453
  563.6 5.3 slice_bitcast_fusion
  568.9 3.2 fusion.23.extra_ref
  575.4 2.8 multiply_add_fusion.3
  578.2 2.4 fusion.53
  582.4 41.5 %shard_map.399 = f32[8,96,768]{2,1,0:T(8,128)S(1)} custom-call(f32[4,96,768]{2,1,0:T(8,128)S(1)} %bitcast.97, f32[96,768]{1,0:T(8,128)S(1)} %fusion.23.extra_ref), custom_call_target="tpu_custom_call" | custom-call | flops 44999999488 | bytes 4718592 | tf_op jit(solution)/shard_map/pallas_call | solution.py:1128
  625.3 2.5 convolution_convert_fusion.2
  629.8 33.3 %shard_map.400 = f32[768,768]{1,0:T(8,128)S(1)} custom-call(f32[768,768]{1,0:T(8,128)S(1)} %bitcast.99), custom_call_target="tpu_custom_call" | custom-call | flops 30802968576 | bytes 4718592 | tf_op jit(solution)/shard_map/pallas_call | solution.py:1417
  666.4 5.5 convolution_convert_fusion.1
  674.9 30.8 %shard_map.402 = f32[4,96,768]{2,1,0:T(8,128)S(1)} custom-call(f32[96,768]{1,0:T(8,128)S(1)} %dynamic-slice_select_fusion.x_ref), custom_call_target="tpu_custom_call" | custom-call | flops 24999999488 | bytes 1179648 | tf_op jit(solution)/shard_map/pallas_call | solution.py:774
  712.7 3.0 fusion.8
  717.4 10.6 %shard_map.401 = f32[8,768]{1,0:T(8,128)S(1)} custom-call(f32[8,768]{1,0:T(8,128)S(1)} %concatenate.22.refs_0_), custom_call_target="tpu_custom_call" | custom-call | flops 10000000000 | bytes 1000000 | tf_op jit(solution)/shard_map/pallas_call | solution.py:295
  731.2 13.7 %all-gather.9.cloned.1.call-done.group_ref = bf16[768,2304]{1,0:T(8,128)(2,1)} async-done(((bf16[96,2304]{1,0:T(8,128)(2,1)}), bf16[768,2304]{1,0:T(8,128)(2,1)}) %all-gather.9.cloned.1.call-update) | async-done | bytes 3538960 | tf_op jit(solution)/shard_map/all_gather | solution.py:1643
  746.7 10.7 %shard_map.403 = (f32[768,768]{1,0:T(8,128)}, f32[768,768]{1,0:T(8,128)}, f32[192,768]{1,0:T(8,128)}, f32[576,768]{1,0:T(8,128)}, f32[1600,768]{1,0:T(8,128)}) custom-call(bf16[768,2304]{1,0:T(8,128)(2,1)} %all-gather.9.cloned.1.call-done.group_ref, bf16[768,1600]{1,0:T(8,128)(2,1)} %all-gather.11.cloned.1.call-done.map_ref, f32[768,768]{1,0:T(8,128)S(1)} %copy-done.8, ...), custom_call_target="tpu_custom_call" | custom-call | flops 1000000000 | bytes 17694720 | tf_op jit(solution)/shard_map/pallas_call | solution.py:818
  (276 shorter events, 78.5 us)
Async XLA Ops:
  7.2 138.6 %reduce-scatter.5.cloned.1.call-start = ((), (), s32[]{:S(2)}) async-start(), calls=%async_computation.4 | async-start | bytes 1966080 | tf_op jit(solution)/shard_map/reduce_scatter | solution.py:1480
  9.6 138.7 %copy-start.55 = (f32[768]{0:T(1024)}, f32[768]{0:T(1024)S(1)}, u32[]{:S(2)}) copy-start(f32[768]{0:T(1024)S(1)} %get-tuple-element.152) | copy-start | bytes 9220
  15.3 94.3 %copy-start.2 = (f32[192,768]{1,0:T(8,128)S(1)}, f32[192,768]{1,0:T(8,128)}, u32[]{:S(2)}) copy-start(f32[192,768]{1,0:T(8,128)} %refs_2_.1) | copy-start | bytes 1769476
  111.3 237.3 %reduce-scatter.7.cloned.1.call-start = ((), (), s32[]{:S(2)}) async-start(), calls=%async_computation.5 | async-start | bytes 1966080 | tf_op jit(solution)/shard_map/reduce_scatter | solution.py:1480
  147.0 67.5 %copy-start.63 = (f32[256]{0:T(256)}, f32[256]{0:T(256)S(1)}, u32[]{:S(2)}) copy-start(f32[256]{0:T(256)S(1)} %broadcast_multiply_fusion.8) | copy-start | bytes 3076
  148.3 66.3 %copy-start.67 = (f32[256]{0:T(256)}, f32[256]{0:T(256)S(1)}, u32[]{:S(2)}) copy-start(f32[256]{0:T(256)S(1)} %add_rsqrt_fusion.1) | copy-start | bytes 3076
  150.9 63.7 %copy-start.6 = (f32[768,768]{1,0:T(8,128)S(1)}, f32[768,768]{1,0:T(8,128)}, u32[]{:S(2)}) copy-start(f32[768,768]{1,0:T(8,128)} %refs_0_.1) | copy-start | bytes 7077892
  220.9 178.1 %all-gather.5.cloned.1.call-start = ((), (), s32[]{:S(2)}) async-start(), calls=%async_computation.6 | async-start | bytes 1966080 | tf_op jit(solution)/shard_map/all_gather | solution.py:1477
  359.4 87.3 %reduce-scatter.9.cloned.1.call-start = ((), (), s32[]{:S(2)}) async-start(), calls=%async_computation.7 | async-start | bytes 1966080 | tf_op jit(solution)/shard_map/reduce_scatter | solution.py:1480
  398.9 7.7 %copy-start.7 = (f32[768,768]{1,0:T(8,128)S(1)}, f32[768,768]{1,0:T(8,128)}, u32[]{:S(2)}) copy-start(f32[768,768]{1,0:T(8,128)} %refs_0_.1) | copy-start | bytes 7077892
  409.2 77.7 %all-gather.7.cloned.1.call-start = ((), (), s32[]{:S(2)}) async-start(), calls=%async_computation.8 | async-start | bytes 1966080 | tf_op jit(solution)/shard_map/all_gather | solution.py:1477
  415.0 32.8 %copy-start.56 = (f32[768]{0:T(1024)S(1)}, f32[768]{0:T(1024)}, u32[]{:S(2)}) copy-start(f32[768]{0:T(1024)} %copy-done.55) | copy-start | bytes 9220
  415.0 32.8 %copy-start.64 = (f32[256]{0:T(256)S(1)}, f32[256]{0:T(256)}, u32[]{:S(2)}) copy-start(f32[256]{0:T(256)} %copy-done.63) | copy-start | bytes 3076
  415.0 32.8 %copy-start.68 = (f32[256]{0:T(256)S(1)}, f32[256]{0:T(256)}, u32[]{:S(2)}) copy-start(f32[256]{0:T(256)} %copy-done.67) | copy-start | bytes 3076
  450.2 36.8 %copy-start.3 = (f32[192,768]{1,0:T(8,128)S(1)}, f32[192,768]{1,0:T(8,128)}, u32[]{:S(2)}) copy-start(f32[192,768]{1,0:T(8,128)} %refs_2_.1) | copy-start | bytes 1769476
  450.2 222.7 %reduce-scatter.11.cloned.1.call-start = ((), (), s32[]{:S(2)}) async-start(), calls=%async_computation.9 | async-start | bytes 1966080 | tf_op jit(solution)/shard_map/reduce_scatter | solution.py:1480
  490.6 8.9 %copy-start.17 = (bf16[4,256,768]{2,1,0:T(8,128)(2,1)S(1)}, bf16[4,256,768]{2,1,0:T(8,128)(2,1)}, u32[]{:S(2)}) copy-start(bf16[4,256,768]{2,1,0:T(8,128)(2,1)} %copy-done.16) | copy-start | bytes 4718596
  501.8 59.1 %copy-start.35 = (f32[768,3,192]{0,2,1:T(8,128)S(1)}, f32[768,3,192]{0,2,1:T(8,128)}, u32[]{:S(2)}) copy-start(f32[768,3,192]{0,2,1:T(8,128)} %broadcast_multiply_fusion) | copy-start | bytes 5308420
  560.9 12.6 %copy-start.52 = (f32[2,96,768]{2,1,0:T(8,128)}, f32[2,96,768]{2,1,0:T(8,128)S(1)}, u32[]{:S(2)}) copy-start(f32[2,96,768]{2,1,0:T(8,128)S(1)} %slice.79) | copy-start | bytes 1769476
  574.8 130.9 %copy-start.44 = (f32[192,768]{1,0:T(8,128)}, f32[192,768]{1,0:T(8,128)S(1)}, u32[]{:S(2)}) copy-start(f32[192,768]{1,0:T(8,128)S(1)} %multiply_add_fusion.5) | copy-start | bytes 1769476
  582.4 43.0 %copy-start.46 = (bf16[768,3,192]{0,2,1:T(8,128)(2,1)S(1)}, bf16[768,3,192]{0,2,1:T(8,128)(2,1)}, u32[]{:S(2)}) copy-start(bf16[768,3,192]{0,2,1:T(8,128)(2,1)} %convert_element_type.125) | copy-start | bytes 2654212
  627.9 103.3 %all-gather.11.cloned.1.call-start = ((), (), s32[]{:S(2)}) async-start(), calls=%async_computation.11 | async-start | bytes 2875392 | tf_op jit(solution)/shard_map/all_gather | solution.py:1641
  664.0 2.3 collective-permute-start
  671.9 73.1 %all-gather.9.cloned.1.call-start = ((), (), s32[]{:S(2)}) async-start(), calls=%async_computation.10 | async-start | bytes 3981312 | tf_op jit(solution)/shard_map/all_gather | solution.py:1643
  674.9 31.3 %copy-start.40 = (f32[6,96,768]{2,1,0:T(8,128)S(1)}, f32[6,96,768]{2,1,0:T(8,128)}, u32[]{:S(2)}) copy-start(f32[6,96,768]{2,1,0:T(8,128)} %get-tuple-element.171) | copy-start | bytes 5308420
  717.4 12.0 %copy-start.75 = (f32[256]{0:T(256)S(1)}, f32[256]{0:T(256)}, u32[]{:S(2)}) copy-start(f32[256]{0:T(256)} %get-tuple-element.143) | copy-start | bytes 3076
  717.4 12.0 %copy-start.58 = (f32[4,768]{1,0:T(4,128)S(1)}, f32[4,768]{1,0:T(4,128)}, u32[]{:S(2)}) copy-start(f32[4,768]{1,0:T(4,128)} %param.33) | copy-start | bytes 36868
  717.4 12.0 %copy-start.73 = (f32[4,768]{1,0:T(4,128)S(1)}, f32[4,768]{1,0:T(4,128)}, u32[]{:S(2)}) copy-start(f32[4,768]{1,0:T(4,128)} %param.45) | copy-start | bytes 36868
  717.4 12.0 %copy-start.74 = (f32[4,768]{1,0:T(4,128)S(1)}, f32[4,768]{1,0:T(4,128)}, u32[]{:S(2)}) copy-start(f32[4,768]{1,0:T(4,128)} %param.44) | copy-start | bytes 36868
  717.4 12.6 %copy-start.48 = (f32[256,768]{1,0:T(8,128)S(1)}, f32[256,768]{1,0:T(8,128)}, u32[]{:S(2)}) copy-start(f32[256,768]{1,0:T(8,128)} %get-tuple-element.164) | copy-start | bytes 2359300
  728.0 17.0 %copy-start.1 = (f32[768,3,192]{0,2,1:T(8,128)S(1)}, f32[768,3,192]{0,2,1:T(8,128)}, u32[]{:S(2)}) copy-start(f32[768,3,192]{0,2,1:T(8,128)} %param.34) | copy-start | bytes 5308420
  728.0 17.0 %copy-start.4 = (f32[192,768]{1,0:T(8,128)S(1)}, f32[192,768]{1,0:T(8,128)}, u32[]{:S(2)}) copy-start(f32[192,768]{1,0:T(8,128)} %refs_2_.1) | copy-start | bytes 1769476
  (62 other events, 174.4 us)
Sparse Core Ops, SparseCore 0:
  111.5 34.3 reduce-scatter.4
  221.0 60.7 reduce-scatter.6
  359.5 37.6 all-gather.4
  409.4 35.1 reduce-scatter.8
  450.3 36.6 all-gather.6
  628.0 40.9 reduce-scatter.10
  672.0 35.4 all-gather.10
  710.6 34.3 all-gather.8

commit v6 on v5

--- a/solution.py
+++ b/solution.py
@@ -1565,7 +1565,7 @@
     grad_attn_rows, grad_map = sum_and_spread(
         jnp.concatenate([grad_out, grad_qkv], axis=0), map_slab, 3
     )
-    grad_map = grad_map[:DT]
+    raw_map, grad_map = grad_map, grad_map[:DT]
     grad_out, grad_qkv = grad_attn_rows[:shard_width], grad_attn_rows[shard_width:]
     grad_fc = grad_fc.reshape(DS, shard_hidden)
     def to_tall(mat):
@@ -1593,7 +1593,7 @@
             lax.dynamic_slice_in_dim(tall, first_row, slice_rows, 1 - axis),
             tall,
             (((axis,), (axis,)), ((), ())),
-            precision=HIGH,
+            precision=lax.Precision.HIGH,
             preferred_element_type=jnp.float32,
         )
 
@@ -1640,7 +1640,14 @@
 
     map_all = lax.all_gather(piece_of(4, odd_rows), "dp", axis=0, tiled=True)
     pieces = [piece_of(i, factor_rows[i]) for i in (2, 3, 1, 0)]
-    iterate_all = lax.all_gather(jnp.concatenate(pieces, axis=1), "dp", axis=0, tiled=True)
+    joined, grad_attn_rows, grad_mlp_rows, raw_map = lax.optimization_barrier(
+        (jnp.concatenate(pieces, axis=1), grad_attn_rows, grad_mlp_rows, raw_map)
+    )
+    iterate_all = lax.all_gather(joined, "dp", axis=0, tiled=True)
+    grad_out, grad_qkv = grad_attn_rows[:shard_width], grad_attn_rows[shard_width:]
+    grad_proj = grad_mlp_rows[:shard_hidden]
+    grad_fc = grad_mlp_rows[shard_hidden:].reshape(DS, shard_hidden)
+    grad_map = raw_map[:DT]
     weight_fc, weight_proj, weight_out, weight_qkv, weight_map = renew(
         iterate_all,
         map_all,

time: 775 us -> 776 us (level)
  local copies, waits for them, and re-layouts: 38.5 us -> 53 us
  waiting for transfers between devices: 19.8 us -> 7.85 us
    all_gather x1, waiting for transfers between devices: 13.7 us -> 2.14 us  [body(): iterate_all = lax.all_gather(joined, 'dp', axis=0, tiled=True)]
    unnamed x172 -> x176, local copies, waits for them, and re-layouts: 26.1 us -> 28.9 us
  transfers between devices with their start and end apart: 9 -> 9, of which waited for: 4 -> 4; matrix products, arithmetic and copies ran while one was open for 6% -> 8% of each run, Pallas kernels for 41% -> 41%
where the time goes in v6:
time: 776 us; the launch traced here: 766 us
  Pallas kernels  586 us (76%)
  matrix products  64.5 us (8%)
  local copies, waits for them, and re-layouts  53 us (7%)
  other arithmetic  32.8 us (4%)
  between operations  20.4 us (3%)
  waiting for transfers between devices  7.85 us (1%)
    pallas_call x1, Pallas kernels, line_mlp(): pl.pallas_call(line_mlp_kernel, out_shape=jax.ShapeDtypeStruct((count, wi...  125 us
    pallas_call x1, Pallas kernels, first_gather(): pl.pallas_call(functools.partial(first_gather_kernel, head_count), out_sh...  88.7 us
    pallas_call x2, Pallas kernels, scatter_rows(): pl.pallas_call(scatter_rows_kernel, out_shape=jax.ShapeDtypeStruct(slab,...  67.3 us
    pallas_call x1, Pallas kernels, line_exchange(): pl.pallas_call(line_exchange_kernel, out_shape=(jax.ShapeDtypeStruct((2 *...  63.6 us
    pallas_call x1, Pallas kernels, sum_and_spread(): pl.pallas_call(sum_and_spread_kernel, out_shape=(jax.ShapeDtypeStruct((dp...  58.7 us
    pallas_call x1, Pallas kernels, share_gram(): pl.pallas_call(share_gram_kernel, out_shape=jax.ShapeDtypeStruct((dp_coun...  41.5 us
    pallas_call x1, Pallas kernels, orthogonal_factor(): pl.pallas_call(polynomial_kernel, out_shape=jax.ShapeDtypeStruct((size, s...  33.7 us
    pallas_call x1, Pallas kernels, spread(): pl.pallas_call(spread_kernel, out_shape=jax.ShapeDtypeStruct((dp_count, e...  31.5 us
  transfers between devices with their start and end apart: 9, of which 4 were waited for; matrix products, arithmetic and copies ran while one was open for 8% of the time, Pallas kernels for 41%

profile of v6, /device:TPU:0, one launch (start us, length us, event | category | flops | bytes accessed | tf_op | source)
XLA Modules:
  0.0 766.1 jit_solution(5447564013565954649)
XLA Ops:
  18.7 88.7 %shard_map.390 = (bf16[4,256,768]{2,1,0:T(8,128)(2,1)S(1)}, f32[8,128]{1,0:T(8,128)S(1)}, bf16[4,256,1600]{2,1,0:T(8,128)(2,1)S(1)}, bf16[1024,576]{1,0:T(8,128)...) custom-call(bf16[256,768]{1,0:T(8,128)(2,1)S(1)} %fusion.26.x_ref, ...), custom_call_target="tpu_custom_call" | custom-call | flops 80000000000 | bytes 6553600 | tf_op jit(solution)/shard_map/pallas_call | solution.py:743
  115.5 8.7 %convolution_convert_fusion = bf16[1024,1344]{0,1:T(8,128)(2,1)} fusion(bf16[1024,1600]{1,0:T(8,128)(2,1)S(1)} %bitcast.106, bf16[1600,1344]{0,1:T(8,128)(2,1)} %bitcast.124), kind=kOutput, calls=%fused_computation.7 | convolution fusion | flops 4405395456 | bytes 10330112 | tf_op jit(solution)/shard_map/dot_general | solution.py:1512
  124.2 3.5 copy.59.qkv_ref
  129.8 15.9 %shard_map.391 = (bf16[1024,448]{1,0:T(8,128)(2,1)S(1)}, f32[1024,128]{1,0:T(8,128)}) custom-call(bf16[1024,1344]{1,0:T(8,128)(2,1)S(1)} %copy.59.qkv_ref), custom_call_target="tpu_custom_call" | custom-call | flops 7516192768 | bytes 3670016 | tf_op jit(solution)/shard_map/pallas_call | solution.py:114
  154.3 63.6 %shard_map.392 = (f32[256,1600]{1,0:T(8,128)S(1)}, bf16[4,256,768]{2,1,0:T(8,128)(2,1)S(1)}) custom-call(bf16[1024,448]{1,0:T(8,128)(2,1)S(1)} %broadcast_select_fusion.heads_ref, bf16[448,1600]{1,0:T(8,128)(2,1)S(1)} %copy-done.14, bf16[256,768]{1,0:T(8,128)(2,1)S(1)} %add_convert_fusion.3.x_ref), custom_call_target="tpu_custom_call" | custom-call | flops 60000002048 | bytes 7340032 | tf_op jit(solution)/shard_map/pallas_call | solution.py:1302
  223.3 3.1 convolution_convert_fusion.4
  226.9 125.0 %shard_map.393 = f32[256,1600]{1,0:T(8,128)S(1)} custom-call(bf16[256,1600]{1,0:T(8,128)(2,1)S(1)} %add_convert_fusion.1.x_ref, bf16[1600,1600]{1,0:T(8,128)(2,1)} %first_ref.1, bf16[1600,1600]{1,0:T(8,128)(2,1)} %second_ref.1), custom_call_target="tpu_custom_call" | custom-call | flops 41943040000 | bytes 6553600 | tf_op jit(solution)/shard_map/pallas_call | solution.py:1020
  354.4 4.4 fusion.13
  360.8 3.2 fusion.76
  364.2 2.8 concatenate.18
  367.0 35.7 %shard_map.394.y_ref = f32[224,768]{1,0:T(8,128)S(1)} custom-call(f32[8,224,768]{2,1,0:T(8,128)S(1)} %bitcast.102), custom_call_target="tpu_custom_call" | custom-call | flops 26880000000 | bytes 5505024 | tf_op jit(solution)/shard_map/pallas_call | solution.py:534
  402.8 6.6 fusion.3
  410.5 2.6 convolution_convert_fusion.3
  413.2 3.5 fusion.83
  418.9 31.5 %shard_map.395.x_ref = f32[192,768]{1,0:T(8,128)S(1)} custom-call(f32[8,192,768]{2,1,0:T(8,128)S(1)} %bitcast.103), custom_call_target="tpu_custom_call" | custom-call | flops 23040000000 | bytes 4718592 | tf_op jit(solution)/shard_map/pallas_call | solution.py:534
  454.5 31.5 %shard_map.396 = f32[8,192,768]{2,1,0:T(8,128)S(1)} custom-call(f32[192,768]{1,0:T(8,128)S(1)} %shard_map.395.x_ref), custom_call_target="tpu_custom_call" | custom-call | flops 35000000512 | bytes 4718592 | tf_op jit(solution)/shard_map/pallas_call | solution.py:605
  488.2 2.5 all-gather.7.cloned.1.call-done
  492.9 2.7 fusion.84
  495.7 3.0 slice_add_fusion.2
  503.2 9.1 %shard_map.397 = bf16[1024,576]{1,0:T(8,128)(2,1)S(1)} custom-call(bf16[1024,576]{1,0:T(8,128)(2,1)S(1)} %copy-done.23, f32[1024,128]{1,0:T(8,128)S(1)} %copy-done.25, bf16[1024,192]{1,0:T(8,128)(2,1)S(1)} %copy.61.grad_ref), custom_call_target="tpu_custom_call" | custom-call | flops 8053063680 | bytes 3145728 | tf_op jit(solution)/shard_map/pallas_call | solution.py:183
  513.6 58.7 %shard_map.398 = (f32[8,96,768]{2,1,0:T(8,128)S(1)}, f32[8,224,768]{2,1,0:T(8,128)S(1)}) custom-call(f32[8,96,768]{2,1,0:T(8,128)S(1)} %bitcast.104, f32[224,768]{1,0:T(8,128)S(1)} %shard_map.394.y_ref), custom_call_target="tpu_custom_call" | custom-call | flops 60000002048 | bytes 9437184 | tf_op jit(solution)/shard_map/pallas_call | solution.py:453
  581.3 41.5 %shard_map.399 = f32[8,96,768]{2,1,0:T(8,128)S(1)} custom-call(f32[4,96,768]{2,1,0:T(8,128)S(1)} %bitcast.105, f32[96,768]{1,0:T(8,128)S(1)} %fusion.23.extra_ref), custom_call_target="tpu_custom_call" | custom-call | flops 44999999488 | bytes 4718592 | tf_op jit(solution)/shard_map/pallas_call | solution.py:1128
  624.2 2.5 convolution_convert_fusion.2
  628.7 33.7 %shard_map.400 = f32[768,768]{1,0:T(8,128)S(1)} custom-call(f32[768,768]{1,0:T(8,128)S(1)} %bitcast.107), custom_call_target="tpu_custom_call" | custom-call | flops 30802968576 | bytes 4718592 | tf_op jit(solution)/shard_map/pallas_call | solution.py:1417
  664.6 2.3 collective-permute-done
  667.0 5.6 convolution_convert_fusion.1
  675.7 30.8 %shard_map.402 = f32[4,96,768]{2,1,0:T(8,128)S(1)} custom-call(f32[96,768]{1,0:T(8,128)S(1)} %dynamic-slice_select_fusion.x_ref), custom_call_target="tpu_custom_call" | custom-call | flops 24999999488 | bytes 1179648 | tf_op jit(solution)/shard_map/pallas_call | solution.py:774
  716.7 3.6 fusion.8
  724.4 9.9 %shard_map.401 = f32[8,768]{1,0:T(8,128)S(1)} custom-call(f32[8,768]{1,0:T(8,128)S(1)} %concatenate.22.refs_0_), custom_call_target="tpu_custom_call" | custom-call | flops 10000000000 | bytes 1000000 | tf_op jit(solution)/shard_map/pallas_call | solution.py:295
  737.4 2.5 fusion.81
  740.5 2.6 slice_bitcast_fusion
  746.9 10.7 %shard_map.403 = (f32[768,768]{1,0:T(8,128)}, f32[768,768]{1,0:T(8,128)}, f32[192,768]{1,0:T(8,128)}, f32[576,768]{1,0:T(8,128)}, f32[1600,768]{1,0:T(8,128)}) custom-call(bf16[768,2304]{1,0:T(8,128)(2,1)} %all-gather.9.cloned.1.call-done.group_ref, bf16[768,1600]{1,0:T(8,128)(2,1)} %all-gather.11.cloned.1.call-done.map_ref, f32[768,768]{1,0:T(8,128)S(1)} %copy-done.10, ...), custom_call_target="tpu_custom_call" | custom-call | flops 1000000000 | bytes 17694720 | tf_op jit(solution)/shard_map/pallas_call | solution.py:818
  (286 shorter events, 93.5 us)
Async XLA Ops:
  7.2 142.0 %reduce-scatter.5.cloned.1.call-start = ((), (), s32[]{:S(2)}) async-start(), calls=%async_computation.4 | async-start | bytes 1966080 | tf_op jit(solution)/shard_map/reduce_scatter | solution.py:1480
  8.2 143.5 %copy-start.57 = (f32[768]{0:T(1024)}, f32[768]{0:T(1024)S(1)}, u32[]{:S(2)}) copy-start(f32[768]{0:T(1024)S(1)} %get-tuple-element.160) | copy-start | bytes 9220
  18.6 94.3 %copy-start.5 = (f32[192,768]{1,0:T(8,128)S(1)}, f32[192,768]{1,0:T(8,128)}, u32[]{:S(2)}) copy-start(f32[192,768]{1,0:T(8,128)} %refs_2_.1) | copy-start | bytes 1769476
  114.7 238.4 %reduce-scatter.7.cloned.1.call-start = ((), (), s32[]{:S(2)}) async-start(), calls=%async_computation.5 | async-start | bytes 1966080 | tf_op jit(solution)/shard_map/reduce_scatter | solution.py:1480
  150.4 67.5 %copy-start.64 = (f32[256]{0:T(256)}, f32[256]{0:T(256)S(1)}, u32[]{:S(2)}) copy-start(f32[256]{0:T(256)S(1)} %broadcast_multiply_fusion.8) | copy-start | bytes 3076
  151.6 66.3 %copy-start.68 = (f32[256]{0:T(256)}, f32[256]{0:T(256)S(1)}, u32[]{:S(2)}) copy-start(f32[256]{0:T(256)S(1)} %add_rsqrt_fusion.1) | copy-start | bytes 3076
  154.3 63.7 %copy-start.27 = (bf16[256,1600]{1,0:T(8,128)(2,1)S(1)}, bf16[256,1600]{1,0:T(8,128)(2,1)}, u32[]{:S(2)}) copy-start(bf16[256,1600]{1,0:T(8,128)(2,1)} %copy-done.26) | copy-start | bytes 2457604
  226.4 176.4 %all-gather.5.cloned.1.call-start = ((), (), s32[]{:S(2)}) async-start(), calls=%async_computation.6 | async-start | bytes 1966080 | tf_op jit(solution)/shard_map/all_gather | solution.py:1477
  364.0 86.5 %reduce-scatter.9.cloned.1.call-start = ((), (), s32[]{:S(2)}) async-start(), calls=%async_computation.7 | async-start | bytes 1966080 | tf_op jit(solution)/shard_map/reduce_scatter | solution.py:1480
  413.1 77.6 %all-gather.7.cloned.1.call-start = ((), (), s32[]{:S(2)}) async-start(), calls=%async_computation.8 | async-start | bytes 1966080 | tf_op jit(solution)/shard_map/all_gather | solution.py:1477
  418.9 32.8 %copy-start.40 = (bf16[256,768]{1,0:T(8,128)(2,1)S(1)}, bf16[256,768]{1,0:T(8,128)(2,1)}, u32[]{:S(2)}) copy-start(bf16[256,768]{1,0:T(8,128)(2,1)} %reduce-scatter.5.cloned.1.call-done) | copy-start | bytes 1179652
  418.9 32.8 %copy-start.58 = (f32[768]{0:T(1024)S(1)}, f32[768]{0:T(1024)}, u32[]{:S(2)}) copy-start(f32[768]{0:T(1024)} %copy-done.57) | copy-start | bytes 9220
  418.9 32.8 %copy-start.65 = (f32[256]{0:T(256)S(1)}, f32[256]{0:T(256)}, u32[]{:S(2)}) copy-start(f32[256]{0:T(256)} %copy-done.64) | copy-start | bytes 3076
  418.9 32.8 %copy-start.69 = (f32[256]{0:T(256)S(1)}, f32[256]{0:T(256)}, u32[]{:S(2)}) copy-start(f32[256]{0:T(256)} %copy-done.68) | copy-start | bytes 3076
  454.0 36.7 %copy-start.6 = (f32[192,768]{1,0:T(8,128)S(1)}, f32[192,768]{1,0:T(8,128)}, u32[]{:S(2)}) copy-start(f32[192,768]{1,0:T(8,128)} %refs_2_.1) | copy-start | bytes 1769476
  454.0 219.7 %reduce-scatter.11.cloned.1.call-start = ((), (), s32[]{:S(2)}) async-start(), calls=%async_computation.9 | async-start | bytes 1966080 | tf_op jit(solution)/shard_map/reduce_scatter | solution.py:1480
  512.3 66.5 %slice-start.6 = ((s8[4915200]{0:T(1024)(128)(4,1)}), s8[4194304]{0:T(1024)(128)(4,1)S(1)}, s32[]{:S(2)}) async-start(s8[4915200]{0:T(1024)(128)(4,1)} %bitcast.118), calls=%async_computation.18 | async-start | bytes 8388608
  513.6 58.8 %copy-start.54 = (f32[192,768]{1,0:T(8,128)S(1)}, f32[192,768]{1,0:T(8,128)}, u32[]{:S(2)}) copy-start(f32[192,768]{1,0:T(8,128)} %param.40) | copy-start | bytes 1769476
  513.6 65.2 %slice-start.7 = ((s8[4915200]{0:T(1024)(128)(4,1)}), s8[720896]{0:T(1024)(128)(4,1)S(1)}, s32[]{:S(2)}) async-start(s8[4915200]{0:T(1024)(128)(4,1)} %bitcast.118), calls=%async_computation.19 | async-start | bytes 1441792
  572.5 134.0 %copy-start.45 = (f32[192,768]{1,0:T(8,128)}, f32[192,768]{1,0:T(8,128)S(1)}, u32[]{:S(2)}) copy-start(f32[192,768]{1,0:T(8,128)S(1)} %bitcast_add_fusion.2) | copy-start | bytes 1769476
  579.4 43.3 %copy-start.32 = (f32[1600,768]{1,0:T(8,128)}, f32[1600,768]{1,0:T(8,128)S(1)}, u32[]{:S(2)}) copy-start(f32[1600,768]{1,0:T(8,128)S(1)} %slice_add_fusion) | copy-start | bytes 14745604
  581.3 42.9 %copy-start.47 = (bf16[768,3,192]{0,2,1:T(8,128)(2,1)S(1)}, bf16[768,3,192]{0,2,1:T(8,128)(2,1)}, u32[]{:S(2)}) copy-start(bf16[768,3,192]{0,2,1:T(8,128)(2,1)} %convert_element_type.125) | copy-start | bytes 2654212
  626.7 116.3 %all-gather.11.cloned.1.call-start = ((), (), s32[]{:S(2)}) async-start(), calls=%async_computation.11 | async-start | bytes 2875392 | tf_op jit(solution)/shard_map/all_gather | solution.py:1641
  664.6 2.3 collective-permute-start
  672.6 72.6 %all-gather.9.cloned.1.call-start = ((), (), s32[]{:S(2)}) async-start(), calls=%async_computation.10 | async-start | bytes 3981312 | tf_op jit(solution)/shard_map/all_gather | solution.py:1646
  675.7 31.3 %copy-start.42 = (f32[6,96,768]{2,1,0:T(8,128)S(1)}, f32[6,96,768]{2,1,0:T(8,128)}, u32[]{:S(2)}) copy-start(f32[6,96,768]{2,1,0:T(8,128)} %get-tuple-element.175) | copy-start | bytes 5308420
  723.6 13.8 %slice-start = ((s8[4718592]{0:T(1024)(128)(4,1)}), s8[524288]{0:T(1024)(128)(4,1)S(1)}, s32[]{:S(2)}) async-start(s8[4718592]{0:T(1024)(128)(4,1)} %bitcast.92), calls=%async_computation.12 | async-start | bytes 1048576
  724.3 11.2 %copy-start.59 = (f32[4,768]{1,0:T(4,128)S(1)}, f32[4,768]{1,0:T(4,128)}, u32[]{:S(2)}) copy-start(f32[4,768]{1,0:T(4,128)} %param.33) | copy-start | bytes 36868
  724.4 11.2 %copy-start.72 = (f32[4,768]{1,0:T(4,128)S(1)}, f32[4,768]{1,0:T(4,128)}, u32[]{:S(2)}) copy-start(f32[4,768]{1,0:T(4,128)} %param.45) | copy-start | bytes 36868
  724.4 11.2 %copy-start.73 = (f32[4,768]{1,0:T(4,128)S(1)}, f32[4,768]{1,0:T(4,128)}, u32[]{:S(2)}) copy-start(f32[4,768]{1,0:T(4,128)} %param.44) | copy-start | bytes 36868
  724.4 11.8 %copy-start.49 = (f32[256,768]{1,0:T(8,128)S(1)}, f32[256,768]{1,0:T(8,128)}, u32[]{:S(2)}) copy-start(f32[256,768]{1,0:T(8,128)} %get-tuple-element.168) | copy-start | bytes 2359300
  724.4 13.0 %slice-start.1 = ((s8[4718592]{0:T(1024)(128)(4,1)}), s8[4194304]{0:T(1024)(128)(4,1)S(1)}, s32[]{:S(2)}) async-start(s8[4718592]{0:T(1024)(128)(4,1)} %bitcast.92), calls=%async_computation.13 | async-start | bytes 8388608
  (64 other events, 206.2 us)
Sparse Core Ops, SparseCore 0:
  114.8 34.3 reduce-scatter.4
  226.5 60.8 reduce-scatter.6
  364.1 37.3 all-gather.4
  413.2 34.9 reduce-scatter.8
  454.1 36.4 all-gather.6
  626.9 40.9 reduce-scatter.10
  672.7 35.4 all-gather.10
  712.6 32.5 all-gather.8
